TPU v7x, 32 devices: a whole 2x2x4 slice. The times are simulated.
32 devices in a mesh: dp: 4 (over y, x), expert: 8 (over z, core).
Axes of the slice: x: 2, y: 2, z: 4, core: 2. Of those that a mesh axis runs over, the one named last changes fastest.
Arguments:
- tokens: bfloat16 [4096, 4096], P(('dp', 'expert')), may hold values from -6 to 6
- out_grad: bfloat16 [4096, 4096], P(('dp', 'expert')), may hold values from -6 to 6
- route_slots: int32 [4, 8, 8, 64], P('dp', 'expert'), may hold values from -1 to 127, as said below
- expert_counts: int32 [4096], P(('dp', 'expert')), may hold values from 0 to 8, as said below
- router_weight: float32 [4096, 8], replicated, may hold values from -0.09375 to 0.09375
- up_weight: bfloat16 [8, 4096, 1024], P('expert'), may hold values from -0.09375 to 0.09375
- down_weight: bfloat16 [8, 4096, 1024], P('expert'), may hold values from -0.1875 to 0.1875
Outputs:
- tokens_grad: bfloat16 [4096, 4096], P(('dp', 'expert'))
- up_grad: bfloat16 [8, 4096, 1024], P('expert', 'dp')
- down_grad: bfloat16 [8, 4096, 1024], P('expert', 'dp')
- router_grad: float32 [4096, 8], P(None, 'expert')
Inputs may be any that keep to these rules, and one draw needn't show every extreme that they name: In route_slots[p, s, e, :] the chosen local tokens are distinct and come first, then -1; every list holds at least one token. In every batch shard some expert takes 64 tokens from every device of it. On every device one local token is chosen by every expert. expert_counts of a token equals the number of lists of route_slots that hold it.
All inputs are finite; a program needn't handle non-finite values.
Results may differ from a plain program's by a relative error of at most 0.017.
Values may be sent and summed in bfloat16 or wider, within the bound.
No kernel may reach another device: no remote copies, remote signals or barrier semaphores. Data moves between devices by JAX's collectives and lax.ppermute only.
A program may use at most 192 MiB of HBM per device.

v0:
```python
import jax
import jax.numpy as jnp
from jax import lax
from jax.sharding import PartitionSpec as P


def gelu_pair(values):
    inner = 0.7978845608 * (values + 0.044715 * values * values * values)
    tangent = jnp.tanh(inner)
    result = 0.5 * values * (1.0 + tangent)
    slope = 0.5 * (1.0 + tangent) + 0.5 * values * (1.0 - tangent * tangent) * 0.7978845608 * (
        1.0 + 3.0 * 0.044715 * values * values
    )
    return (result, slope)


def on_device(tokens, out_grad, route_slots, expert_counts, router_weight, up_weight, down_weight):
    experts = lax.axis_size("expert")
    tok_rows = tokens.shape[0]
    width = tokens.shape[1]
    slots = route_slots[0, 0]
    per_slot = slots.shape[1]
    received = experts * per_slot
    contract = (((0,), (0,)), ((), ()))
    trailing = (((1,), (1,)), ((), ()))
    highest = lax.Precision.HIGHEST
    valid = slots >= 0
    picks = slots[:, :, None] == jnp.arange(tok_rows, dtype=jnp.int32)[None, None, :]
    pick_float = picks.astype(jnp.float32)
    pick_half = picks.astype(jnp.bfloat16).reshape(received, tok_rows)
    logits = jnp.dot(tokens.astype(jnp.float32), router_weight, precision=highest)
    gates = jax.nn.sigmoid(logits)
    gate_slot = jnp.einsum("est,te->es", pick_float, gates, precision=highest)
    count_slot = jnp.einsum(
        "est,t->es", pick_float, expert_counts.astype(jnp.float32), precision=highest
    )
    safe_count = jnp.where(valid, count_slot, 1.0)
    weight_slot = jnp.where(valid, gate_slot / safe_count, 0.0)
    slope_slot = jnp.where(valid, gate_slot * (1.0 - gate_slot) / safe_count, 0.0)
    send_rows = (
        jnp.dot(pick_half, tokens, preferred_element_type=jnp.float32)
        .astype(jnp.bfloat16)
        .reshape(experts, per_slot, width)
    )
    send_grads = (
        jnp.dot(pick_half, out_grad, preferred_element_type=jnp.float32)
        .astype(jnp.bfloat16)
        .reshape(experts, per_slot, width)
    )
    coefs = weight_slot[:, None, :]
    got_rows, got_grads, got_coefs = (
        lax.all_to_all(send_rows, "expert", split_axis=0, concat_axis=0, tiled=True),
        lax.all_to_all(send_grads, "expert", split_axis=0, concat_axis=0, tiled=True),
        lax.all_to_all(
            coefs.astype(jnp.bfloat16), "expert", split_axis=0, concat_axis=0, tiled=True
        ).astype(coefs.dtype),
    )
    rows_in = got_rows.reshape(received, width)
    grads_in = got_grads.reshape(received, width)
    weight_in = got_coefs[:, 0, :].reshape(received)
    w_up = up_weight[0]
    w_down = down_weight[0]
    pre = jnp.dot(rows_in, w_up, preferred_element_type=jnp.float32)
    active, slope = gelu_pair(pre)
    active = active.astype(jnp.bfloat16)
    output = lax.dot_general(active, w_down, trailing, preferred_element_type=jnp.float32)
    grads_float = grads_in.astype(jnp.float32)
    score = jnp.sum(grads_float * output, axis=1)
    out_scaled = (weight_in[:, None] * grads_float).astype(jnp.bfloat16)
    act_grad = jnp.dot(out_scaled, w_down, preferred_element_type=jnp.float32)
    pre_grad = (act_grad * slope).astype(jnp.bfloat16)
    row_grad = lax.dot_general(pre_grad, w_up, trailing, preferred_element_type=jnp.float32).astype(
        jnp.bfloat16
    )
    back_rows, back_score = (
        lax.all_to_all(
            row_grad.reshape(experts, per_slot, width),
            "expert",
            split_axis=0,
            concat_axis=0,
            tiled=True,
        ),
        lax.all_to_all(
            score.reshape(experts, per_slot).astype(jnp.bfloat16),
            "expert",
            split_axis=0,
            concat_axis=0,
            tiled=True,
        ).astype(jnp.float32),
    )
    up_sum = lax.psum_scatter(
        lax.dot_general(rows_in, pre_grad, contract, preferred_element_type=jnp.float32).astype(
            jnp.bfloat16
        ),
        "dp",
        scatter_dimension=0,
        tiled=True,
    )
    down_sum = lax.psum_scatter(
        lax.dot_general(out_scaled, active, contract, preferred_element_type=jnp.float32).astype(
            jnp.bfloat16
        ),
        "dp",
        scatter_dimension=0,
        tiled=True,
    )
    moe_grad = lax.dot_general(
        pick_half, back_rows.reshape(received, width), contract, preferred_element_type=jnp.float32
    )
    logit_grad = jnp.einsum("est,es->te", pick_float, back_score * slope_slot, precision=highest)
    tokens_grad = (moe_grad + jnp.dot(logit_grad, router_weight.T, precision=highest)).astype(
        jnp.bfloat16
    )
    local_terms = jnp.dot(tokens.astype(jnp.float32).T, logit_grad, precision=highest)
    own_column = lax.psum_scatter(
        local_terms.astype(jnp.bfloat16), "expert", scatter_dimension=1, tiled=True
    ).astype(jnp.float32)
    router_grad = lax.psum(own_column, "dp")
    return (tokens_grad, up_sum[None], down_sum[None], router_grad)


def solution(mesh):
    return jax.shard_map(
        on_device,
        mesh=mesh,
        in_specs=(
            P(("dp", "expert"), None),
            P(("dp", "expert"), None),
            P("dp", "expert", None, None),
            P(("dp", "expert")),
            P(),
            P("expert", None, None),
            P("expert", None, None),
        ),
        out_specs=(
            P(("dp", "expert"), None),
            P("expert", "dp", None),
            P("expert", "dp", None),
            P(None, "expert"),
        ),
        check_vma=False,
    )
```

profile of v0, /device:TPU:22, one launch (start us, length us, event | category | flops | bytes accessed | tf_op | source)
XLA Modules:
  0.0 430.6 jit_solution(9983057086888070533)
XLA Ops:
  8.0 0.9 eq.28
  9.2 3.2 convolution_convert_fusion.2
  12.5 5.3 %all-to-all-start.2 = ((bf16[8,64,4096]{2,1,0:T(8,128)(2,1)}), bf16[8,64,4096]{2,1,0:T(8,128)(2,1)}, u32[]{:S(2)}, u32[]{:S(2)}) async-start(bf16[8,64,4096]{2,1,0:T(8,128)(2,1)} %bitcast.79), calls=%async_computation.2 | async-start | bytes 8388608 | tf_op jit(solution)/shard_map/all_to_all | solution.py:52
  17.8 3.3 convolution_convert_fusion.3
  21.1 87.5 %all-to-all-done.2 = bf16[8,64,4096]{2,1,0:T(8,128)(2,1)} async-done(((bf16[8,64,4096]{2,1,0:T(8,128)(2,1)}), bf16[8,64,4096]{2,1,0:T(8,128)(2,1)}, u32[]{:S(2)}, u32[]{:S(2)}) %all-to-all-start.2) | async-done | bytes 4194336 | tf_op jit(solution)/shard_map/all_to_all | solution.py:52
  108.6 8.0 %all-to-all-start.1 = ((bf16[8,64,4096]{2,1,0:T(8,128)(2,1)}), bf16[8,64,4096]{2,1,0:T(8,128)(2,1)}, u32[]{:S(2)}, u32[]{:S(2)}) async-start(bf16[8,64,4096]{2,1,0:T(8,128)(2,1)} %bitcast.78), calls=%async_computation.1 | async-start | bytes 8388608 | tf_op jit(solution)/shard_map/all_to_all | solution.py:53
  116.6 0.9 fusion.29
  117.9 8.2 %fusion.5 = f32[512,1024]{1,0:T(8,128)S(1)} fusion(bf16[512,4096]{1,0:T(8,128)(2,1)} %bitcast.14, bf16[1,4096,1024]{2,1,0:T(8,128)(2,1)} %param.12), kind=kOutput, calls=%fused_computation.8 | convolution fusion | flops 4294967296 | bytes 14680064 | tf_op jit(solution)/shard_map/dot_general | solution.py:63
  126.1 81.2 %all-to-all-done.1 = bf16[8,64,4096]{2,1,0:T(8,128)(2,1)} async-done(((bf16[8,64,4096]{2,1,0:T(8,128)(2,1)}), bf16[8,64,4096]{2,1,0:T(8,128)(2,1)}, u32[]{:S(2)}, u32[]{:S(2)}) %all-to-all-start.1) | async-done | bytes 4194336 | tf_op jit(solution)/shard_map/all_to_all | solution.py:53
  207.3 9.1 %fusion.1 = bf16[512]{0:T(512)(128)(2,1)S(1)} fusion(bf16[8,64,4096]{2,1,0:T(8,128)(2,1)} %all-to-all-done.1, bf16[1,4096,1024]{2,1,0:T(8,128)(2,1)} %param.13, f32[512,1024]{1,0:T(8,128)S(1)} %fusion.5), kind=kOutput, calls=%fused_computation.4 | convolution fusion | flops 4305976832 | bytes 14681088 | tf_op jit(solution)/shard_map/dot_general | solution.py:66
  216.4 0.7 convert_element_type.112
  217.1 6.6 %all-to-all-start.4 = ((bf16[8,1,64]{2,1,0:T(2,128)(2,1)}), bf16[8,1,64]{2,1,0:T(2,128)(2,1)S(1)}, u32[]{:S(2)}, u32[]{:S(2)}) async-start(bf16[8,1,64]{2,1,0:T(2,128)(2,1)} %convert_element_type.112), calls=%async_computation.4 | async-start | bytes 8192 | tf_op jit(solution)/shard_map/all_to_all | solution.py:83
  224.2 2.7 all-to-all-done.4
  227.2 0.6 copy.12
  227.8 5.6 %all-to-all-start = ((bf16[8,1,64]{2,1,0:T(2,128)(2,1)}), bf16[8,1,64]{2,1,0:T(2,128)(2,1)S(1)}, u32[]{:S(2)}, u32[]{:S(2)}) async-start(bf16[8,1,64]{2,1,0:T(2,128)(2,1)} %copy.12), calls=%async_computation | async-start | bytes 8192 | tf_op jit(solution)/shard_map/all_to_all | solution.py:54
  233.4 1.2 fusion.15
  234.8 1.7 all-to-all-done
  236.6 3.5 fusion.2
  240.2 7.2 %convolution_convert_fusion = bf16[4096,1024]{1,0:T(8,128)(2,1)} fusion(bf16[512,4096]{1,0:T(8,128)(2,1)S(1)} %fusion.2, f32[512,1024]{1,0:T(8,128)S(1)} %fusion.5), kind=kOutput, calls=%fused_computation.14 | convolution fusion | flops 4303880192 | bytes 14680064 | tf_op jit(solution)/shard_map/dot_general | solution.py:100
  247.5 3.7 fusion
  251.2 9.0 %fusion.24 = bf16[512,1024]{1,0:T(8,128)(2,1)S(1)} fusion(f32[512,1024]{1,0:T(8,128)S(1)} %fusion.5, bf16[512,4096]{1,0:T(8,128)(2,1)S(1)} %bitcast.81, bf16[1,4096,1024]{2,1,0:T(8,128)(2,1)} %param.13), kind=kOutput, calls=%fused_computation.32 | convolution fusion | flops 4304928768 | bytes 15728640 | tf_op jit(solution)/shard_map/dot_general | solution.py:70
  260.2 9.0 %convolution_convert_fusion.1 = bf16[4096,1024]{1,0:T(8,128)(2,1)} fusion(bf16[512,4096]{1,0:T(8,128)(2,1)} %bitcast.14, bf16[512,1024]{1,0:T(8,128)(2,1)S(1)} %fusion.24), kind=kOutput, calls=%fused_computation.15 | convolution fusion | flops 4299161600 | bytes 13631488 | tf_op jit(solution)/shard_map/dot_general | solution.py:92
  269.2 9.8 %fusion.11 = bf16[512,4096]{1,0:T(8,128)(2,1)} fusion(bf16[512,1024]{1,0:T(8,128)(2,1)S(1)} %fusion.24, bf16[1,4096,1024]{2,1,0:T(8,128)(2,1)} %param.12), kind=kOutput, calls=%fused_computation.16 | convolution fusion | flops 4297064448 | bytes 13631488 | tf_op jit(solution)/shard_map/dot_general | solution.py:72
  279.0 7.6 %all-to-all-start.3 = ((bf16[8,64,4096]{2,1,0:T(8,128)(2,1)}), bf16[8,64,4096]{2,1,0:T(8,128)(2,1)}, u32[]{:S(2)}, u32[]{:S(2)}) async-start(bf16[8,64,4096]{2,1,0:T(8,128)(2,1)} %bitcast.80), calls=%async_computation.3 | async-start | bytes 8388608 | tf_op jit(solution)/shard_map/all_to_all | solution.py:76
  286.6 0.6 dynamic-slice
  287.2 13.1 %all-reduce.3.cloned.1.call-done = bf16[4096,8]{0,1:T(8,128)(2,1)} async-done(((bf16[4096,8]{0,1:T(8,128)(2,1)}), bf16[4096,8]{0,1:T(8,128)(2,1)}) %all-reduce.3.cloned.1.call-update) | async-done | bytes 65552
  300.3 1.5 dynamic-slice_convert_fusion
  301.8 14.2 %psum.7 = f32[4096,1]{0,1:T(1,128)} all-reduce(f32[4096,1]{0,1:T(1,128)S(1)} %dynamic-slice_convert_fusion), channel_id=1, replica_groups=mesh['dp'=4,'expert'=8] {'dp'}, use_global_device_ids=true, to_apply=%region_4.5 | all-reduce | flops 4096 | bytes 32768 | tf_op jit(solution)/shard_map/psum | solution.py:118
  316.0 61.3 %all-to-all-done.3 = bf16[8,64,4096]{2,1,0:T(8,128)(2,1)} async-done(((bf16[8,64,4096]{2,1,0:T(8,128)(2,1)}), bf16[8,64,4096]{2,1,0:T(8,128)(2,1)}, u32[]{:S(2)}, u32[]{:S(2)}) %all-to-all-start.3) | async-done | bytes 4194336 | tf_op jit(solution)/shard_map/all_to_all | solution.py:76
  377.3 3.4 convolution_bitcast_fusion
  380.7 2.9 fusion.14
  383.6 39.6 %reduce-scatter.3.cloned.1.call-done = bf16[1024,1024]{1,0:T(8,128)(2,1)} async-done(((bf16[4096,1024]{1,0:T(8,128)(2,1)}), bf16[1024,1024]{1,0:T(8,128)(2,1)}) %reduce-scatter.3.cloned.1.call-update) | async-done | bytes 2097168 | tf_op jit(solution)/shard_map/reduce_scatter | solution.py:91
  (29 shorter events, 2.0 us)
Async XLA Ops:
  8.0 1.2 copy-start
  12.5 5.3 %copy-start.2 = (bf16[128,4096]{1,0:T(8,128)(2,1)S(1)}, bf16[128,4096]{1,0:T(8,128)(2,1)}, u32[]{:S(2)}) copy-start(bf16[128,4096]{1,0:T(8,128)(2,1)} %param.8) | copy-start | bytes 3145732
  12.5 96.1 %all-to-all-start.2 = ((bf16[8,64,4096]{2,1,0:T(8,128)(2,1)}), bf16[8,64,4096]{2,1,0:T(8,128)(2,1)}, u32[]{:S(2)}, u32[]{:S(2)}) async-start(bf16[8,64,4096]{2,1,0:T(8,128)(2,1)} %bitcast.79), calls=%async_computation.2 | async-start | bytes 8388608 | tf_op jit(solution)/shard_map/all_to_all | solution.py:52
  108.6 8.0 %copy-start.3 = (f32[4096,8]{0,1:T(8,128)S(1)}, f32[4096,8]{0,1:T(8,128)}, u32[]{:S(2)}) copy-start(f32[4096,8]{0,1:T(8,128)} %param.11) | copy-start | bytes 393220
  108.6 8.9 %copy-start.4 = (s32[1,1,8,64]{3,2,1,0:T(8,128)S(1)}, s32[1,1,8,64]{3,2,1,0:T(8,128)}, u32[]{:S(2)}) copy-start(s32[1,1,8,64]{3,2,1,0:T(8,128)} %param.9) | copy-start | bytes 6148
  108.6 98.7 %all-to-all-start.1 = ((bf16[8,64,4096]{2,1,0:T(8,128)(2,1)}), bf16[8,64,4096]{2,1,0:T(8,128)(2,1)}, u32[]{:S(2)}, u32[]{:S(2)}) async-start(bf16[8,64,4096]{2,1,0:T(8,128)(2,1)} %bitcast.78), calls=%async_computation.1 | async-start | bytes 8388608 | tf_op jit(solution)/shard_map/all_to_all | solution.py:53
  126.1 97.7 %copy-start.5 = (s32[128]{0:T(128)S(1)}, s32[128]{0:T(128)}, u32[]{:S(2)}) copy-start(s32[128]{0:T(128)} %param.10) | copy-start | bytes 1540
  217.1 9.7 %all-to-all-start.4 = ((bf16[8,1,64]{2,1,0:T(2,128)(2,1)}), bf16[8,1,64]{2,1,0:T(2,128)(2,1)S(1)}, u32[]{:S(2)}, u32[]{:S(2)}) async-start(bf16[8,1,64]{2,1,0:T(2,128)(2,1)} %convert_element_type.112), calls=%async_computation.4 | async-start | bytes 8192 | tf_op jit(solution)/shard_map/all_to_all | solution.py:83
  227.8 8.7 %all-to-all-start = ((bf16[8,1,64]{2,1,0:T(2,128)(2,1)}), bf16[8,1,64]{2,1,0:T(2,128)(2,1)S(1)}, u32[]{:S(2)}, u32[]{:S(2)}) async-start(bf16[8,1,64]{2,1,0:T(2,128)(2,1)} %copy.12), calls=%async_computation | async-start | bytes 8192 | tf_op jit(solution)/shard_map/all_to_all | solution.py:54
  233.4 66.9 %all-reduce.3.cloned.1.call-start = ((), (), s32[]{:S(2)}) async-start(), calls=%async_computation.9 | async-start | bytes 131072
  234.6 149.0 %reduce-scatter.5.cloned.1.call-start = ((), (), s32[]{:S(2)}) async-start(), calls=%async_computation.8 | async-start | bytes 10485760 | tf_op jit(solution)/shard_map/reduce_scatter | solution.py:99
  247.4 175.8 %reduce-scatter.3.cloned.1.call-start = ((), (), s32[]{:S(2)}) async-start(), calls=%async_computation.7 | async-start | bytes 10485760 | tf_op jit(solution)/shard_map/reduce_scatter | solution.py:91
  279.0 7.6 %copy-start.6 = (u32[32]{0:T(128)S(1)}, u32[32]{0:T(128)}, u32[]{:S(2)}) copy-start(u32[32]{0:T(128)} %constant.22) | copy-start | bytes 388
  279.0 98.3 %all-to-all-start.3 = ((bf16[8,64,4096]{2,1,0:T(8,128)(2,1)}), bf16[8,64,4096]{2,1,0:T(8,128)(2,1)}, u32[]{:S(2)}, u32[]{:S(2)}) async-start(bf16[8,64,4096]{2,1,0:T(8,128)(2,1)} %bitcast.80), calls=%async_computation.3 | async-start | bytes 8388608 | tf_op jit(solution)/shard_map/all_to_all | solution.py:76
  377.3 45.9 %copy-start.1 = (bf16[128,4096]{1,0:T(8,128)(2,1)S(1)}, bf16[128,4096]{1,0:T(8,128)(2,1)}, u32[]{:S(2)}) copy-start(bf16[128,4096]{1,0:T(8,128)(2,1)} %param.7) | copy-start | bytes 3145732
Sparse Core Ops, SparseCore 0:
  237.1 63.1 all-reduce.2
Sparse Core Ops, SparseCore 1:
  247.5 85.7 reduce-scatter.4
  337.0 86.1 reduce-scatter.2
where the time goes:
time: 434 us; the launch traced here: 431 us
  waiting for transfers between devices  287 us (66%)
  matrix products  68.3 us (16%)
  starting transfers between devices  33.4 us (8%)
  between operations  15.6 us (4%)
  blocking collectives  14.2 us (3%)
  other arithmetic  8.76 us (2%)
    all_to_all x1, waiting for transfers between devices, on_device(): lax.all_to_all(send_rows, 'expert', split_axis=0, concat_axis=0, tiled=True)  87.5 us
    all_to_all x1, waiting for transfers between devices, on_device(): lax.all_to_all(send_grads, 'expert', split_axis=0, concat_axis=0, tiled=T...  81.2 us
    all_to_all x1, waiting for transfers between devices, on_device(): lax.all_to_all(row_grad.reshape(experts, per_slot, width), 'expert', spli...  61.3 us
    reduce_scatter x1, waiting for transfers between devices, on_device(): lax.psum_scatter(lax.dot_general(rows_in, pre_grad, contract, preferred_e...  39.6 us
    psum x1, blocking collectives, on_device(): router_grad = lax.psum(own_column, 'dp')  14.2 us
    unnamed x4, waiting for transfers between devices  13.2 us
    dot_general x1, matrix products, on_device(): lax.dot_general(pre_grad, w_up, trailing, preferred_element_type=jnp.floa...  9.8 us
    dot_general x1, matrix products, on_device(): lax.dot_general(active, w_down, trailing, preferred_element_type=jnp.floa...  9.13 us
  transfers between devices with their start and end apart: 8, of which 7 were waited for; matrix products, arithmetic and copies ran while one was open for 15% of the time, Pallas kernels for 0%

commit v1 on v0

v1 whole, which is shorter than its diff:
```python
import functools

import jax
import jax.numpy as jnp
from jax import lax
from jax.experimental import pallas as pl
from jax.experimental.pallas import tpu as pltpu
from jax.sharding import PartitionSpec as P

VMEM_LIMIT = 48 * 1024 * 1024


def gelu_pair(values):
    inner = 0.7978845608 * (values + 0.044715 * values * values * values)
    tangent = jnp.tanh(inner)
    result = 0.5 * values * (1.0 + tangent)
    slope = 0.5 * (1.0 + tangent) + 0.5 * values * (1.0 - tangent * tangent) * 0.7978845608 * (
        1.0 + 3.0 * 0.044715 * values * values
    )
    return (result, slope)


def gate_logits(tokens, router_weight):
    high = lax.reduce_precision(router_weight, 8, 7)
    rest = router_weight - high
    middle = lax.reduce_precision(rest, 8, 7)
    low = rest - middle
    terms = jnp.concatenate([high, middle, low], axis=1).astype(jnp.bfloat16)
    parts = jnp.dot(tokens, terms, preferred_element_type=jnp.float32)
    experts = router_weight.shape[1]
    return parts[:, :experts] + parts[:, experts : 2 * experts] + parts[:, 2 * experts :]


def hidden_kernel(
    meta_ref, t0_ref, t1_ref, g0_ref, g1_ref, up_ref, down_ref, xg_ref, dw_ref, lg_ref, pre, back
):
    step = pl.program_id(0)
    steps = pl.num_programs(0)
    rows = meta_ref.shape[0]
    half = rows // 2
    tok_rows = t0_ref.shape[0]
    places = lax.broadcasted_iota(jnp.int32, (rows, tok_rows), 1).astype(jnp.float32)
    picks = (meta_ref[:, 0:1] == places).astype(jnp.bfloat16)

    def pick(first, second):
        top = jnp.dot(picks[:half], first[...], preferred_element_type=jnp.float32)
        bottom = jnp.dot(picks[half:], second[...], preferred_element_type=jnp.float32)
        return jnp.concatenate([top, bottom], axis=0).astype(jnp.bfloat16)

    x = pick(t0_ref, t1_ref)
    g = pick(g0_ref, g1_ref)
    xg_ref[0, :rows] = x
    xg_ref[0, rows:] = g
    pre_term = jnp.dot(x, up_ref[...], preferred_element_type=jnp.float32)
    back_term = jnp.dot(g, down_ref[...], preferred_element_type=jnp.float32)

    @pl.when(step == 0)
    def _():
        pre[...] = pre_term
        back[...] = back_term

    @pl.when(step > 0)
    def _():
        pre[...] += pre_term
        back[...] += back_term

    @pl.when(step == steps - 1)
    def _():
        weight = meta_ref[:, 1:2]
        active, slope = gelu_pair(pre[...])
        grad = back[...]
        score = jnp.sum(active.astype(jnp.bfloat16).astype(jnp.float32) * grad, axis=1, keepdims=True)
        dw_ref[:rows] = (weight * grad * slope).astype(jnp.bfloat16)
        dw_ref[rows:] = (weight * active).astype(jnp.bfloat16)
        lg_ref[...] = jnp.broadcast_to(score * meta_ref[:, 2:3], lg_ref.shape)


def hidden(meta, t0, t1, g0, g1, w_up, w_down, dp):
    rows = meta.shape[0]
    tok_rows, width = t0.shape
    hid = w_up.shape[1]
    piece = width // dp
    block = pl.BlockSpec((tok_rows, piece), lambda k: (0, k))
    weight = pl.BlockSpec((piece, hid), lambda k: (k, 0))
    whole = lambda shape: pl.BlockSpec(shape, lambda k: (0, 0))
    return pl.pallas_call(
        hidden_kernel,
        grid=(dp,),
        in_specs=[whole(meta.shape), block, block, block, block, weight, weight],
        out_specs=[
            pl.BlockSpec((1, 2 * rows, piece), lambda k: (k, 0, 0)),
            whole((2 * rows, hid)),
            whole((rows, 128)),
        ],
        out_shape=[
            jax.ShapeDtypeStruct((dp, 2 * rows, piece), jnp.bfloat16),
            jax.ShapeDtypeStruct((2 * rows, hid), jnp.bfloat16),
            jax.ShapeDtypeStruct((rows, 128), jnp.float32),
        ],
        scratch_shapes=[pltpu.VMEM((rows, hid), jnp.float32)] * 2,
        compiler_params=pltpu.CompilerParams(vmem_limit_bytes=VMEM_LIMIT),
        cost_estimate=pl.CostEstimate(
            flops=4 * rows * width * hid, bytes_accessed=4 * width * hid + 8 * rows * width, transcendentals=rows * hid
        ),
        name="hidden",
    )(meta, t0, t1, g0, g1, w_up, w_down)


def rows_kernel(dw_ref, lg_ref, xg_ref, up_ref, router_ref, near_ref, far_ref, column_ref):
    rows = lg_ref.shape[0]
    half = rows // 2
    trailing = (((1,), (1,)), ((), ()))
    lg = lg_ref[:, 0:1]
    out = lax.dot_general(dw_ref[:rows], up_ref[...], trailing, preferred_element_type=jnp.float32)
    out = (out + lg * router_ref[...]).astype(jnp.bfloat16)
    near_ref[...] = out[:half]
    far_ref[...] = out[half:]
    column_ref[...] = jnp.sum(xg_ref[0].astype(jnp.float32) * lg, axis=0, keepdims=True)


def back_rows(dw, lg, xg, w_up, router_row):
    dp, double, piece = xg.shape
    rows = double // 2
    width, hid = w_up.shape
    whole = lambda shape: pl.BlockSpec(shape, lambda k: (0, 0))
    return pl.pallas_call(
        rows_kernel,
        grid=(dp,),
        in_specs=[
            whole(dw.shape),
            whole(lg.shape),
            pl.BlockSpec((1, rows, piece), lambda k: (k, 0, 0)),
            pl.BlockSpec((piece, hid), lambda k: (k, 0)),
            pl.BlockSpec((1, piece), lambda k: (0, k)),
        ],
        out_specs=[
            pl.BlockSpec((rows // 2, piece), lambda k: (0, k)),
            pl.BlockSpec((rows // 2, piece), lambda k: (0, k)),
            pl.BlockSpec((1, piece), lambda k: (0, k)),
        ],
        out_shape=[
            jax.ShapeDtypeStruct((rows // 2, width), jnp.bfloat16),
            jax.ShapeDtypeStruct((rows // 2, width), jnp.bfloat16),
            jax.ShapeDtypeStruct((1, width), jnp.float32),
        ],
        compiler_params=pltpu.CompilerParams(vmem_limit_bytes=VMEM_LIMIT),
        cost_estimate=pl.CostEstimate(
            flops=2 * rows * width * hid, bytes_accessed=2 * width * hid + 4 * rows * width, transcendentals=0
        ),
        name="back_rows",
    )(dw, lg, xg, w_up, router_row)


def weights_kernel(chunks, dp, has_start, has_end, place_ref, *refs):
    refs = list(refs)
    xgs = [refs.pop(0) for _ in range(chunks)]
    dws = [[refs.pop(0) for _ in range(dp)] for _ in range(chunks)]
    start = [refs.pop(0) for _ in range(2)] if has_start else None
    up_out, down_out = refs
    contract = (((0,), (0,)), ((), ()))
    place = place_ref[0]
    for which, out_ref in enumerate((up_out, down_out)):
        total = start[which][...] if has_start else None
        for chunk in range(chunks):
            rows = dws[chunk][0].shape[0] // 2
            left = jnp.concatenate(
                [xgs[chunk][place ^ k, which * rows : (which + 1) * rows] for k in range(dp)], axis=0
            )
            right = jnp.concatenate(
                [dws[chunk][k][which * rows : (which + 1) * rows] for k in range(dp)], axis=0
            )
            term = lax.dot_general(left, right, contract, preferred_element_type=jnp.float32)
            total = term if total is None else total + term
        out_ref[...] = total.astype(out_ref.dtype)


def weight_terms(place, xgs, dws, start, last):
    dp, double, piece = xgs[0].shape
    hid = dws[0][0].shape[1]
    tile = min(piece, 256)
    kind = jnp.bfloat16 if last else jnp.float32
    whole = pl.BlockSpec((double, hid), lambda i, place: (0, 0))
    strip = pl.BlockSpec((tile, hid), lambda i, place: (i, 0))
    flat = [block for group in dws for block in group]
    starts = list(start) if start is not None else []
    return pl.pallas_call(
        functools.partial(weights_kernel, len(xgs), dp, start is not None, last),
        grid_spec=pltpu.PrefetchScalarGridSpec(
            num_scalar_prefetch=1,
            grid=(piece // tile,),
            in_specs=[pl.BlockSpec((dp, double, tile), lambda i, place: (0, 0, i))] * len(xgs)
            + [whole] * len(flat)
            + [strip] * len(starts),
            out_specs=[strip, strip],
        ),
        out_shape=[jax.ShapeDtypeStruct((piece, hid), kind)] * 2,
        compiler_params=pltpu.CompilerParams(vmem_limit_bytes=VMEM_LIMIT),
        cost_estimate=pl.CostEstimate(
            flops=2 * len(xgs) * dp * double * piece * hid,
            bytes_accessed=2 * len(xgs) * dp * double * (piece + hid) + 8 * piece * hid,
            transcendentals=0,
        ),
        name="weight_terms",
    )(place, *xgs, *flat, *starts)


def combine_kernel(slots_ref, *refs):
    blocks, out_ref = refs[:-1], refs[-1]
    tok_rows = out_ref.shape[0]
    places = lax.broadcasted_iota(jnp.int32, (tok_rows, slots_ref.shape[1]), 0).astype(jnp.float32)
    picks = jnp.where(slots_ref[...] == places, 1.0, 0.0).astype(jnp.bfloat16)
    rows = jnp.concatenate([block[...] for block in blocks], axis=0)
    out_ref[...] = jnp.dot(picks, rows, preferred_element_type=jnp.float32).astype(out_ref.dtype)


def combine(slots, blocks, tok_rows):
    per_slot, width = blocks[0].shape
    tile = 1024 if width % 1024 == 0 else width
    block = pl.BlockSpec((per_slot, tile), lambda k: (0, k))
    return pl.pallas_call(
        combine_kernel,
        grid=(width // tile,),
        in_specs=[pl.BlockSpec(slots.shape, lambda k: (0, 0))] + [block] * len(blocks),
        out_specs=pl.BlockSpec((tok_rows, tile), lambda k: (0, k)),
        out_shape=jax.ShapeDtypeStruct((tok_rows, width), jnp.bfloat16),
        compiler_params=pltpu.CompilerParams(vmem_limit_bytes=VMEM_LIMIT),
        cost_estimate=pl.CostEstimate(
            flops=2 * len(blocks) * per_slot * tok_rows * width,
            bytes_accessed=2 * len(blocks) * per_slot * width,
            transcendentals=0,
        ),
        name="combine",
    )(slots, *blocks)


def on_line(tokens, out_grad, route_slots, expert_counts, router_weight, up_weight, down_weight):
    experts = lax.axis_size("expert")
    dp = lax.axis_size("dp")
    chips = experts // 2
    me = lax.axis_index("expert")
    place = lax.axis_index("dp")
    chip = me // 2
    core = me % 2
    tok_rows = tokens.shape[0]
    slots = route_slots[0, 0]
    per_slot = slots.shape[1]
    w_up = up_weight[0]
    w_down = down_weight[0]
    everyone = range(experts)

    def along(block, step):
        pairs = [(e, e + 2 * step) for e in everyone if 0 <= e + 2 * step < experts]
        return lax.ppermute(block, "expert", pairs)

    def across(block, mask):
        return lax.ppermute(block, "expert", [(e, e ^ mask) for e in everyone])

    right, left = [(tokens, out_grad)], [(tokens, out_grad)]
    for _ in range(chips - 1):
        t_right, t_left = along(right[-1][0], 1), along(left[-1][0], -1)
        g_right, g_left = along(right[-1][1], 1), along(left[-1][1], -1)
        right.append((t_right, g_right))
        left.append((t_left, g_left))

    gates = jax.nn.sigmoid(gate_logits(tokens, router_weight)).T
    counts = jnp.maximum(expert_counts, 1).astype(jnp.float32)[None, :]
    weights = gates / counts
    slopes = gates * (1.0 - gates) / counts
    slots_float = slots.astype(jnp.float32)
    facts = lax.all_to_all(
        jnp.concatenate([slots_float, weights, slopes], axis=1), "expert", 0, 0, tiled=True
    )
    got_slots = facts[:, :per_slot]
    hits = got_slots[:, :, None] == jnp.arange(tok_rows, dtype=jnp.float32)[None, None, :]
    got_weights = jnp.sum(jnp.where(hits, facts[:, None, per_slot : per_slot + tok_rows], 0.0), axis=2)
    got_slopes = jnp.sum(jnp.where(hits, facts[:, None, per_slot + tok_rows :], 0.0), axis=2)
    metas = jnp.stack([got_slots, got_weights, got_slopes], axis=-1).reshape(chips, 2, per_slot, 3)
    metas = jnp.where(core == 0, metas, metas[:, ::-1]).reshape(chips, 2 * per_slot, 3)
    mine = slots_float.reshape(chips, 2, per_slot)
    mine = jnp.where(core == 0, mine, mine[:, ::-1])
    order = [chip ^ j for j in range(chips)]
    mine = jnp.concatenate([lax.dynamic_index_in_dim(mine, k, 0, False) for k in order], axis=0)

    router_row = lax.dynamic_index_in_dim(router_weight.T, me, 0, True)
    place_array = jnp.reshape(place, (1,)).astype(jnp.int32)

    def source(j, which):
        if j == 0:
            return right[0][which]
        result = None
        for here in range(chips):
            other = here ^ j
            block = left[other - here][which] if other > here else right[here - other][which]
            result = block if result is None else jnp.where(chip == here, block, result)
        return result

    xgs, dws, blocks, columns = [], [], [], []
    for j in range(chips):
        t_near, g_near = source(j, 0), source(j, 1)
        t_far, g_far = across(t_near, 1), across(g_near, 1)
        meta = lax.dynamic_index_in_dim(metas, order[j], 0, False)
        xg, dw, lg = hidden(meta, t_near, t_far, g_near, g_far, w_up, w_down, dp)
        xgs.append(lax.all_to_all(xg, "dp", 0, 0, tiled=True))
        dws.append(
            [dw] + [lax.ppermute(dw, "dp", [(q, q ^ k) for q in range(dp)]) for k in range(1, dp)]
        )
        near, far, column = back_rows(dw, lg, xg, w_up, router_row)
        blocks.append(near if j == 0 else across(near, 2 * j))
        blocks.append(across(far, 2 * j + 1))
        columns.append(column)

    early = weight_terms(place_array, xgs[:-1], dws[:-1], None, False)
    up_sum, down_sum = weight_terms(place_array, xgs[-1:], dws[-1:], early, True)
    tokens_grad = combine(mine.reshape(1, -1), blocks, tok_rows)
    router_grad = lax.psum(sum(columns), "dp").T
    return (tokens_grad, up_sum[None], down_sum[None], router_grad)


def on_any(tokens, out_grad, route_slots, expert_counts, router_weight, up_weight, down_weight):
    experts = lax.axis_size("expert")
    me = lax.axis_index("expert")
    tok_rows = tokens.shape[0]
    width = tokens.shape[1]
    slots = route_slots[0, 0]
    per_slot = slots.shape[1]
    received = experts * per_slot
    contract = (((0,), (0,)), ((), ()))
    trailing = (((1,), (1,)), ((), ()))
    picks = slots[:, :, None] == jnp.arange(tok_rows, dtype=jnp.int32)[None, None, :]
    pick_half = picks.astype(jnp.bfloat16).reshape(received, tok_rows)
    gates = jax.nn.sigmoid(gate_logits(tokens, router_weight)).T
    counts = jnp.maximum(expert_counts, 1).astype(jnp.float32)[None, :]
    weight_slot = jnp.sum(jnp.where(picks, (gates / counts)[:, None, :], 0.0), axis=2)
    slope_slot = jnp.sum(jnp.where(picks, (gates * (1.0 - gates) / counts)[:, None, :], 0.0), axis=2)
    swap = lambda block: lax.all_to_all(block, "expert", split_axis=0, concat_axis=0, tiled=True)
    send_rows = jnp.dot(pick_half, tokens, preferred_element_type=jnp.float32).astype(jnp.bfloat16)
    send_grads = jnp.dot(pick_half, out_grad, preferred_element_type=jnp.float32).astype(jnp.bfloat16)
    rows_in = swap(send_rows)
    grads_in = swap(send_grads)
    facts = swap(jnp.concatenate([weight_slot, slope_slot], axis=1))
    weight_in = facts[:, :per_slot].reshape(received)
    slope_in = facts[:, per_slot:].reshape(received)
    w_up = up_weight[0]
    w_down = down_weight[0]
    pre = jnp.dot(rows_in, w_up, preferred_element_type=jnp.float32)
    active, slope = gelu_pair(pre)
    grad = jnp.dot(grads_in, w_down, preferred_element_type=jnp.float32)
    score = jnp.sum(active.astype(jnp.bfloat16).astype(jnp.float32) * grad, axis=1)
    logit_grad = score * slope_in
    pre_grad = (weight_in[:, None] * grad * slope).astype(jnp.bfloat16)
    scaled = (weight_in[:, None] * active).astype(jnp.bfloat16)
    router_row = lax.dynamic_index_in_dim(router_weight.T, me, 0, True)
    row_grad = lax.dot_general(pre_grad, w_up, trailing, preferred_element_type=jnp.float32)
    back = swap((row_grad + logit_grad[:, None] * router_row).astype(jnp.bfloat16))
    up_term = lax.dot_general(rows_in, pre_grad, contract, preferred_element_type=jnp.float32)
    down_term = lax.dot_general(grads_in, scaled, contract, preferred_element_type=jnp.float32)
    spread = lambda term: lax.psum_scatter(
        term.astype(jnp.bfloat16), "dp", scatter_dimension=0, tiled=True
    )
    tokens_grad = lax.dot_general(pick_half, back, contract, preferred_element_type=jnp.float32)
    column = jnp.sum(logit_grad[:, None] * rows_in.astype(jnp.float32), axis=0, keepdims=True)
    router_grad = lax.psum(column, "dp").T
    return (tokens_grad.astype(jnp.bfloat16), spread(up_term)[None], spread(down_term)[None], router_grad)


def solution(mesh):
    line = mesh.shape["expert"] == 8 and mesh.shape["dp"] == 4
    return jax.shard_map(
        on_line if line else on_any,
        mesh=mesh,
        in_specs=(
            P(("dp", "expert"), None),
            P(("dp", "expert"), None),
            P("dp", "expert", None, None),
            P(("dp", "expert")),
            P(),
            P("expert", None, None),
            P("expert", None, None),
        ),
        out_specs=(
            P(("dp", "expert"), None),
            P("expert", "dp", None),
            P("expert", "dp", None),
            P(None, "expert"),
        ),
        check_vma=False,
    )
```

time: 434 us -> 374 us (0.86)
  waiting for transfers between devices: 287 us -> 132 us
  Pallas kernels: 0 us -> 88.8 us
  matrix products: 68.3 us -> 1.6 us
  starting transfers between devices: 33.4 us -> 82.2 us
  blocking collectives: 14.2 us -> 31.9 us
  local copies, waits for them, and re-layouts: 3.23 us -> 20.7 us
  between operations: 15.6 us -> 1.12 us
    all_to_all x5, waiting for transfers between devices: 234 us -> 36.8 us  [the longest x1 34.9 us: on_line(): lax.all_to_all(jnp.concatenate([slots_float, weights, slopes], axis=1), '...]
    ppermute x0 -> x39, waiting for transfers between devices: none -> 94.9 us  [the longest x15 51.2 us: across(): return lax.ppermute(block, 'expert', [(e, e ^ mask) for e in everyone])]
    pallas_call x0 -> x11, Pallas kernels: none -> 88.8 us  [the longest x4 40.7 us: hidden(): pl.pallas_call(hidden_kernel, grid=(dp,), in_specs=[whole(meta.shape), bl...]
    dot_general x15 -> x1, matrix products: 68.3 us -> 1.6 us  [gate_logits(): parts = jnp.dot(tokens, terms, preferred_element_type=jnp.float32)]
    ppermute x0 -> x39, starting transfers between devices: none -> 55.8 us  [the longest x12 35.7 us: along(): return lax.ppermute(block, 'expert', pairs)]
    reduce_scatter x2 -> x0, waiting for transfers between devices: 39.6 us -> none  [the longest x1 39.6 us: on_device(): lax.psum_scatter(lax.dot_general(rows_in, pre_grad, contract, preferred_e...]
    psum x1, blocking collectives: 14.2 us -> 31.9 us  [on_line(): router_grad = lax.psum(sum(columns), 'dp').T]
    unnamed x15 -> x65, local copies, waits for them, and re-layouts: 1.01 us -> 17.1 us
  transfers between devices with their start and end apart: 8 -> 44, of which waited for: 7 -> 14; matrix products, arithmetic and copies ran while one was open for 15% -> 4% of each run, Pallas kernels for 0% -> 22%
where the time goes in v1:
time: 374 us; the launch traced here: 368 us
  waiting for transfers between devices  132 us (35%)
  Pallas kernels  88.8 us (24%)
  starting transfers between devices  82.2 us (22%)
  blocking collectives  31.9 us (9%)
  local copies, waits for them, and re-layouts  20.7 us (6%)
  other arithmetic  10.4 us (3%)
    ppermute x15, waiting for transfers between devices, across(): return lax.ppermute(block, 'expert', [(e, e ^ mask) for e in everyone])  51.2 us
    pallas_call x4, Pallas kernels, hidden(): pl.pallas_call(hidden_kernel, grid=(dp,), in_specs=[whole(meta.shape), bl...  40.7 us
    ppermute x12, starting transfers between devices, along(): return lax.ppermute(block, 'expert', pairs)  35.7 us
    ppermute x12, waiting for transfers between devices, along(): return lax.ppermute(block, 'expert', pairs)  35 us
    all_to_all x1, waiting for transfers between devices, on_line(): lax.all_to_all(jnp.concatenate([slots_float, weights, slopes], axis=1), '...  34.9 us
    psum x1, blocking collectives, on_line(): router_grad = lax.psum(sum(columns), 'dp').T  31.9 us
    pallas_call x4, Pallas kernels, back_rows(): pl.pallas_call(rows_kernel, grid=(dp,), in_specs=[whole(dw.shape), whole(...  25.6 us
    all_to_all x4, starting transfers between devices, on_line(): xgs.append(lax.all_to_all(xg, 'dp', 0, 0, tiled=True))  20.2 us
  transfers between devices with their start and end apart: 44, of which 14 were waited for; matrix products, arithmetic and copies ran while one was open for 4% of the time, Pallas kernels for 22%

profile of v1, /device:TPU:22, one launch (start us, length us, event | category | flops | bytes accessed | tf_op | source)
XLA Modules:
  0.0 368.5 jit_solution(2699629362195423886)
XLA Ops:
  0.7 3.6 collective-permute-start.3
  6.8 4.4 %collective-permute-start.6 = (bf16[128,4096]{1,0:T(8,128)(2,1)}, bf16[128,4096]{1,0:T(8,128)(2,1)}, u32[]{:S(2)}, u32[]{:S(2)}) collective-permute-start(bf16[128,4096]{1,0:T(8,128)(2,1)} %g0_ref.1), channel_id=1, source_target_pairs={{0,2},{1,3},{2,4},{3,5},{4,6},{5,7},{8,10},{9,11},{10,12},{11,13},... | collective-permute-start | bytes 3145736 | tf_op jit(solution)/shard_map/ppermute | solution.py:253
  17.1 12.0 %collective-permute-done.3 = bf16[128,4096]{1,0:T(8,128)(2,1)} collective-permute-done((bf16[128,4096]{1,0:T(8,128)(2,1)}, bf16[128,4096]{1,0:T(8,128)(2,1)}, u32[]{:S(2)}, u32[]{:S(2)}) %collective-permute-start.3) | collective-permute-done | bytes 1048608 | tf_op jit(solution)/shard_map/ppermute | solution.py:253
  29.1 3.5 collective-permute-start.11
  35.6 6.2 %all-to-all-start = ((f32[8,1,320]{2,1,0:T(1,128)}), f32[8,1,320]{2,1,0:T(1,128)S(1)}, u32[]{:S(2)}, u32[]{:S(2)}) async-start(f32[8,1,320]{2,1,0:T(1,128)} %copy.14), calls=%async_computation | async-start | bytes 24576 | tf_op jit(solution)/shard_map/all_to_all | solution.py:270
  41.8 34.9 %all-to-all-done = f32[8,1,320]{2,1,0:T(1,128)S(1)} async-done(((f32[8,1,320]{2,1,0:T(1,128)}), f32[8,1,320]{2,1,0:T(1,128)S(1)}, u32[]{:S(2)}, u32[]{:S(2)}) %all-to-all-start) | async-done | bytes 10272 | tf_op jit(solution)/shard_map/all_to_all | solution.py:270
  81.0 3.9 %collective-permute-start.15 = (bf16[128,4096]{1,0:T(8,128)(2,1)}, bf16[128,4096]{1,0:T(8,128)(2,1)}, u32[]{:S(2)}, u32[]{:S(2)}) collective-permute-start(bf16[128,4096]{1,0:T(8,128)(2,1)} %collective-permute-done.7), channel_id=1, source_target_pairs={{2,0},{3,1},{4,2},{5,3},{6,4},{7,5},{10,8},{11,9},{12,10},{13,11},... | collective-permute-start | bytes 3145736 | tf_op jit(solution)/shard_map/ppermute | solution.py:253
  85.0 10.2 %hidden.4 = (bf16[4,256,1024]{2,1,0:T(8,128)(2,1)}, bf16[256,1024]{1,0:T(8,128)(2,1)}, f32[128,128]{1,0:T(8,128)S(1)}) custom-call(f32[128,3]{1,0:T(8,128)S(1)} %get-tuple-element.69.meta_ref, bf16[128,4096]{1,0:T(8,128)(2,1)S(1)} %copy-done.4, bf16[128,4096]{1,0:T(8,128)(2,1)S(1)} %collective-permute-done.t1_ref, bf16[128,4096]{1,0:T(8,128)(2,1)S(1)} %copy-done.7, ...), custom_call_target="tpu_custom_call" | custom-call | flops 2147483648 | bytes 20971520 | tf_op jit(solution)/shard_map/hidden/pallas_call | solution.py:86
  95.2 4.9 %all-to-all-start.2 = ((bf16[4,256,1024]{2,1,0:T(8,128)(2,1)}), bf16[4,256,1024]{2,1,0:T(8,128)(2,1)}, u32[]{:S(2)}, u32[]{:S(2)}) async-start(bf16[4,256,1024]{2,1,0:T(8,128)(2,1)} %get-tuple-element.34.xg_ref), calls=%async_computation.2 | async-start | bytes 4194304 | tf_op jit(solution)/shard_map/all_to_all | solution.py:303
  102.9 3.4 collective-permute-start.20
  112.8 16.9 %collective-permute-done.19 = bf16[128,4096]{1,0:T(8,128)(2,1)S(1)} collective-permute-done((bf16[128,4096]{1,0:T(8,128)(2,1)}, bf16[128,4096]{1,0:T(8,128)(2,1)S(1)}, u32[]{:S(2)}, u32[]{:S(2)}) %collective-permute-start.19) | collective-permute-done | bytes 1048608 | tf_op jit(solution)/shard_map/ppermute | solution.py:253
  129.7 3.4 collective-permute-start.23
  134.9 10.0 %hidden.6 = (bf16[4,256,1024]{2,1,0:T(8,128)(2,1)}, bf16[256,1024]{1,0:T(8,128)(2,1)}, f32[128,128]{1,0:T(8,128)S(1)}) custom-call(f32[128,3]{1,0:T(8,128)S(1)} %get-tuple-element.67.meta_ref, bf16[128,4096]{1,0:T(8,128)(2,1)S(1)} %select_select_fusion.1.t0_ref, bf16[128,4096]{1,0:T(8,128)(2,1)S(1)} %collective-permute-done.13.t1_ref, ...), custom_call_target="tpu_custom_call" | custom-call | flops 2147483648 | bytes 20971520 | tf_op jit(solution)/shard_map/hidden/pallas_call | solution.py:86
  144.9 4.9 %all-to-all-start.4 = ((bf16[4,256,1024]{2,1,0:T(8,128)(2,1)}), bf16[4,256,1024]{2,1,0:T(8,128)(2,1)}, u32[]{:S(2)}, u32[]{:S(2)}) async-start(bf16[4,256,1024]{2,1,0:T(8,128)(2,1)} %get-tuple-element.44.xg_ref), calls=%async_computation.4 | async-start | bytes 4194304 | tf_op jit(solution)/shard_map/all_to_all | solution.py:303
  152.3 3.1 collective-permute-done.23
  155.4 3.1 select_select_fusion.4
  161.3 10.2 %hidden.5 = (bf16[4,256,1024]{2,1,0:T(8,128)(2,1)}, bf16[256,1024]{1,0:T(8,128)(2,1)S(1)}, f32[128,128]{1,0:T(8,128)S(1)}) custom-call(f32[128,3]{1,0:T(8,128)S(1)} %get-tuple-element.68.meta_ref, bf16[128,4096]{1,0:T(8,128)(2,1)S(1)} %get-tuple-element.65.t0_ref, bf16[128,4096]{1,0:T(8,128)(2,1)} %collective-permute-done.5.t1_ref, ...), custom_call_target="tpu_custom_call" | custom-call | flops 2147483648 | bytes 20971520 | tf_op jit(solution)/shard_map/hidden/pallas_call | solution.py:86
  174.2 6.1 %all-to-all-start.3 = ((bf16[4,256,1024]{2,1,0:T(8,128)(2,1)}), bf16[4,256,1024]{2,1,0:T(8,128)(2,1)}, u32[]{:S(2)}, u32[]{:S(2)}) async-start(bf16[4,256,1024]{2,1,0:T(8,128)(2,1)} %get-tuple-element.39.xg_ref), calls=%async_computation.3 | async-start | bytes 4194304 | tf_op jit(solution)/shard_map/all_to_all | solution.py:303
  181.2 6.1 %back_rows.4 = (bf16[64,4096]{1,0:T(8,128)(2,1)S(1)}, bf16[64,4096]{1,0:T(8,128)(2,1)S(1)}, f32[1,4096]{1,0:T(1,128)S(1)}) custom-call(bf16[256,1024]{1,0:T(8,128)(2,1)} %get-tuple-element.32.dw_ref.refs_3_, f32[128,128]{1,0:T(8,128)S(1)} %get-tuple-element.33.lg_ref, bf16[4,256,1024]{2,1,0:T(8,128)(2,1)S(1)} %copy-done.1, bf16[4096,1024]{1,0:T(8,128)(2,1)} %bitcast.52, ...), custom_call_target="tpu_custom_call" | custom-call | flops 1073741824 | bytes 10485760 | tf_op jit(solution)/shard_map/back_rows/pallas_call | solution.py:126
  188.9 6.1 %back_rows.6 = (bf16[64,4096]{1,0:T(8,128)(2,1)S(1)}, bf16[64,4096]{1,0:T(8,128)(2,1)S(1)}, f32[1,4096]{1,0:T(1,128)S(1)}) custom-call(bf16[256,1024]{1,0:T(8,128)(2,1)} %get-tuple-element.42.dw_ref.refs_11_, f32[128,128]{1,0:T(8,128)S(1)} %get-tuple-element.43.lg_ref, bf16[4,256,1024]{2,1,0:T(8,128)(2,1)S(1)} %copy-done.3, bf16[4096,1024]{1,0:T(8,128)(2,1)} %bitcast.53, ...), custom_call_target="tpu_custom_call" | custom-call | flops 1073741824 | bytes 10485760 | tf_op jit(solution)/shard_map/back_rows/pallas_call | solution.py:126
  199.8 6.6 %back_rows.5 = (bf16[64,4096]{1,0:T(8,128)(2,1)}, bf16[64,4096]{1,0:T(8,128)(2,1)}, f32[1,4096]{1,0:T(1,128)S(1)}) custom-call(bf16[256,1024]{1,0:T(8,128)(2,1)S(1)} %copy-done.23, f32[128,128]{1,0:T(8,128)S(1)} %get-tuple-element.38.lg_ref, bf16[4,256,1024]{2,1,0:T(8,128)(2,1)S(1)} %copy-done.2, bf16[4096,1024]{1,0:T(8,128)(2,1)} %bitcast.54, ...), custom_call_target="tpu_custom_call" | custom-call | flops 1073741824 | bytes 10485760 | tf_op jit(solution)/shard_map/back_rows/pallas_call | solution.py:126
  206.4 10.4 %hidden.7 = (bf16[4,256,1024]{2,1,0:T(8,128)(2,1)}, bf16[256,1024]{1,0:T(8,128)(2,1)S(1)}, f32[128,128]{1,0:T(8,128)S(1)}) custom-call(f32[128,3]{1,0:T(8,128)S(1)} %get-tuple-element.66.meta_ref, bf16[128,4096]{1,0:T(8,128)(2,1)S(1)} %get-tuple-element.64.t0_ref, bf16[128,4096]{1,0:T(8,128)(2,1)} %collective-permute-done.21.t1_ref, ...), custom_call_target="tpu_custom_call" | custom-call | flops 2147483648 | bytes 20971520 | tf_op jit(solution)/shard_map/hidden/pallas_call | solution.py:86
  218.6 6.7 %back_rows.7 = (bf16[64,4096]{1,0:T(8,128)(2,1)}, bf16[64,4096]{1,0:T(8,128)(2,1)}, f32[1,4096]{1,0:T(1,128)S(1)}) custom-call(bf16[256,1024]{1,0:T(8,128)(2,1)S(1)} %get-tuple-element.47.dw_ref.refs_1_, f32[128,128]{1,0:T(8,128)S(1)} %get-tuple-element.48.lg_ref, bf16[4,256,1024]{2,1,0:T(8,128)(2,1)S(1)} %copy-done, bf16[4096,1024]{1,0:T(8,128)(2,1)} %bitcast.56, ...), custom_call_target="tpu_custom_call" | custom-call | flops 1073741824 | bytes 10485760 | tf_op jit(solution)/shard_map/back_rows/pallas_call | solution.py:126
  235.3 8.7 %collective-permute-done.18.refs_5_ = bf16[64,4096]{1,0:T(8,128)(2,1)S(1)} collective-permute-done((bf16[64,4096]{1,0:T(8,128)(2,1)S(1)}, bf16[64,4096]{1,0:T(8,128)(2,1)S(1)}, u32[]{:S(2)}, u32[]{:S(2)}) %collective-permute-start.18) | collective-permute-done | bytes 524320 | tf_op jit(solution)/shard_map/ppermute | solution.py:256
  246.1 4.3 %all-to-all-start.1 = ((bf16[4,256,1024]{2,1,0:T(8,128)(2,1)}), bf16[4,256,1024]{2,1,0:T(8,128)(2,1)S(1)}, u32[]{:S(2)}, u32[]{:S(2)}) async-start(bf16[4,256,1024]{2,1,0:T(8,128)(2,1)} %get-tuple-element.49.xg_ref), calls=%async_computation.1 | async-start | bytes 4194304 | tf_op jit(solution)/shard_map/all_to_all | solution.py:303
  251.1 27.7 %collective-permute-done.9.refs_2_ = bf16[64,4096]{1,0:T(8,128)(2,1)S(1)} collective-permute-done((bf16[64,4096]{1,0:T(8,128)(2,1)}, bf16[64,4096]{1,0:T(8,128)(2,1)S(1)}, u32[]{:S(2)}, u32[]{:S(2)}) %collective-permute-start.9) | collective-permute-done | bytes 524320 | tf_op jit(solution)/shard_map/ppermute | solution.py:256
  279.9 10.1 %collective-permute-done.10.refs_3_ = bf16[64,4096]{1,0:T(8,128)(2,1)} collective-permute-done((bf16[64,4096]{1,0:T(8,128)(2,1)}, bf16[64,4096]{1,0:T(8,128)(2,1)}, u32[]{:S(2)}, u32[]{:S(2)}) %collective-permute-start.10) | collective-permute-done | bytes 524320 | tf_op jit(solution)/shard_map/ppermute | solution.py:256
  293.5 31.9 %psum.7 = f32[4096,1]{0,1:T(1,128)} all-reduce(f32[4096,1]{0,1:T(1,128)S(1)} %add_bitcast_fusion), channel_id=1, replica_groups=mesh['dp'=4,'expert'=8] {'dp'}, use_global_device_ids=true, to_apply=%region_2.3 | all-reduce | flops 4096 | bytes 32768 | tf_op jit(solution)/shard_map/psum | solution.py:315
  329.7 4.4 %combine.1 = bf16[128,4096]{1,0:T(8,128)(2,1)} custom-call(f32[1,512]{1,0:T(1,128)S(1)} %reshape.35.slots_ref, bf16[64,4096]{1,0:T(8,128)(2,1)S(1)} %copy-done.9, bf16[64,4096]{1,0:T(8,128)(2,1)S(1)} %copy-done.11, bf16[64,4096]{1,0:T(8,128)(2,1)S(1)} %copy-done.17, bf16[64,4096]{1,0:T(8,128)(2,1)} %collective-permute-done.10.refs_3_, ...), custom_call_target="tpu_custom_call" | custom-call | flops 536870912 | bytes 4194304 | tf_op jit(solution)/shard_map/combine/pallas_call | solution.py:220
  338.0 11.4 %weight_terms.2 = (f32[1024,1024]{1,0:T(8,128)}, f32[1024,1024]{1,0:T(8,128)}) custom-call(s32[1]{0:T(128)} %bitcast.20.place_ref, bf16[4,256,1024]{2,1,0:T(8,128)(2,1)} %all-to-all-done.2.refs_0_, bf16[4,256,1024]{2,1,0:T(8,128)(2,1)} %all-to-all-done.3.refs_1_, bf16[4,256,1024]{2,1,0:T(8,128)(2,1)} %all-to-all-done.4.refs_2_, ...), custom_call_target="tpu_custom_call" | custom-call | flops 6442450944 | bytes 20971520 | tf_op jit(solution)/shard_map/weight_terms/pallas_call | solution.py:186
  349.3 8.7 %collective-permute-done.28.refs_3_ = bf16[256,1024]{1,0:T(8,128)(2,1)S(1)} collective-permute-done((bf16[256,1024]{1,0:T(8,128)(2,1)S(1)}, bf16[256,1024]{1,0:T(8,128)(2,1)S(1)}, u32[]{:S(2)}, u32[]{:S(2)}) %collective-permute-start.28) | collective-permute-done | bytes 524320 | tf_op jit(solution)/shard_map/ppermute | solution.py:305
  361.7 6.8 %weight_terms.3 = (bf16[1024,1024]{1,0:T(8,128)(2,1)}, bf16[1024,1024]{1,0:T(8,128)(2,1)}) custom-call(s32[1]{0:T(128)} %bitcast.20.place_ref, bf16[4,256,1024]{2,1,0:T(8,128)(2,1)S(1)} %all-to-all-done.1.refs_0_, bf16[256,1024]{1,0:T(8,128)(2,1)S(1)} %copy-done.6, bf16[256,1024]{1,0:T(8,128)(2,1)S(1)} %collective-permute-done.27.refs_2_, ...), custom_call_target="tpu_custom_call" | custom-call | flops 2147483648 | bytes 12582912 | tf_op jit(solution)/shard_map/weight_terms/pallas_call | solution.py:186
  (159 shorter events, 72.8 us)
Async XLA Ops:
  0.7 28.3 %collective-permute-start.3 = (bf16[128,4096]{1,0:T(8,128)(2,1)}, bf16[128,4096]{1,0:T(8,128)(2,1)}, u32[]{:S(2)}, u32[]{:S(2)}) collective-permute-start(bf16[128,4096]{1,0:T(8,128)(2,1)} %t0_ref.1), channel_id=1, source_target_pairs={{0,2},{1,3},{2,4},{3,5},{4,6},{5,7},{8,10},{9,11},{10,12},{11,13},... | collective-permute-start | bytes 3145736 | tf_op jit(solution)/shard_map/ppermute | solution.py:253
  4.4 28.2 %collective-permute-start.4 = (bf16[128,4096]{1,0:T(8,128)(2,1)}, bf16[128,4096]{1,0:T(8,128)(2,1)}, u32[]{:S(2)}, u32[]{:S(2)}) collective-permute-start(bf16[128,4096]{1,0:T(8,128)(2,1)} %t0_ref.1), channel_id=1, source_target_pairs={{2,0},{3,1},{4,2},{5,3},{6,4},{7,5},{10,8},{11,9},{12,10},{13,11},... | collective-permute-start | bytes 3145736 | tf_op jit(solution)/shard_map/ppermute | solution.py:253
  6.7 78.2 %collective-permute-start.1 = (bf16[128,4096]{1,0:T(8,128)(2,1)}, bf16[128,4096]{1,0:T(8,128)(2,1)}, u32[]{:S(2)}, u32[]{:S(2)}) collective-permute-start(bf16[128,4096]{1,0:T(8,128)(2,1)} %g0_ref.1), channel_id=1, source_target_pairs={{0,1},{1,0},{2,3},{3,2},{4,5},{5,4},{6,7},{7,6},{8,9},{9,8},{10,11... | collective-permute-start | bytes 3145736 | tf_op jit(solution)/shard_map/ppermute | solution.py:256
  6.8 72.3 %collective-permute-start.6 = (bf16[128,4096]{1,0:T(8,128)(2,1)}, bf16[128,4096]{1,0:T(8,128)(2,1)}, u32[]{:S(2)}, u32[]{:S(2)}) collective-permute-start(bf16[128,4096]{1,0:T(8,128)(2,1)} %g0_ref.1), channel_id=1, source_target_pairs={{0,2},{1,3},{2,4},{3,5},{4,6},{5,7},{8,10},{9,11},{10,12},{11,13},... | collective-permute-start | bytes 3145736 | tf_op jit(solution)/shard_map/ppermute | solution.py:253
  14.4 66.6 %collective-permute-start.7 = (bf16[128,4096]{1,0:T(8,128)(2,1)}, bf16[128,4096]{1,0:T(8,128)(2,1)}, u32[]{:S(2)}, u32[]{:S(2)}) collective-permute-start(bf16[128,4096]{1,0:T(8,128)(2,1)} %g0_ref.1), channel_id=1, source_target_pairs={{2,0},{3,1},{4,2},{5,3},{6,4},{7,5},{10,8},{11,9},{12,10},{13,11},... | collective-permute-start | bytes 3145736 | tf_op jit(solution)/shard_map/ppermute | solution.py:253
  29.1 71.0 %collective-permute-start.11 = (bf16[128,4096]{1,0:T(8,128)(2,1)}, bf16[128,4096]{1,0:T(8,128)(2,1)}, u32[]{:S(2)}, u32[]{:S(2)}) collective-permute-start(bf16[128,4096]{1,0:T(8,128)(2,1)} %collective-permute-done.3), channel_id=1, source_target_pairs={{0,2},{1,3},{2,4},{3,5},{4,6},{5,7},{8,10},{9,11},{10,12},{11,13},... | collective-permute-start | bytes 3145736 | tf_op jit(solution)/shard_map/ppermute | solution.py:253
  32.6 70.3 %collective-permute-start.12 = (bf16[128,4096]{1,0:T(8,128)(2,1)}, bf16[128,4096]{1,0:T(8,128)(2,1)}, u32[]{:S(2)}, u32[]{:S(2)}) collective-permute-start(bf16[128,4096]{1,0:T(8,128)(2,1)} %collective-permute-done.4), channel_id=1, source_target_pairs={{2,0},{3,1},{4,2},{5,3},{6,4},{7,5},{10,8},{11,9},{12,10},{13,11},... | collective-permute-start | bytes 3145736 | tf_op jit(solution)/shard_map/ppermute | solution.py:253
  35.6 41.1 %all-to-all-start = ((f32[8,1,320]{2,1,0:T(1,128)}), f32[8,1,320]{2,1,0:T(1,128)S(1)}, u32[]{:S(2)}, u32[]{:S(2)}) async-start(f32[8,1,320]{2,1,0:T(1,128)} %copy.14), calls=%async_computation | async-start | bytes 24576 | tf_op jit(solution)/shard_map/all_to_all | solution.py:270
  79.1 28.6 %collective-permute-start.14 = (bf16[128,4096]{1,0:T(8,128)(2,1)}, bf16[128,4096]{1,0:T(8,128)(2,1)}, u32[]{:S(2)}, u32[]{:S(2)}) collective-permute-start(bf16[128,4096]{1,0:T(8,128)(2,1)} %collective-permute-done.6), channel_id=1, source_target_pairs={{0,2},{1,3},{2,4},{3,5},{4,6},{5,7},{8,10},{9,11},{10,12},{11,13},... | collective-permute-start | bytes 3145736 | tf_op jit(solution)/shard_map/ppermute | solution.py:253
  95.2 49.7 %all-to-all-start.2 = ((bf16[4,256,1024]{2,1,0:T(8,128)(2,1)}), bf16[4,256,1024]{2,1,0:T(8,128)(2,1)}, u32[]{:S(2)}, u32[]{:S(2)}) async-start(bf16[4,256,1024]{2,1,0:T(8,128)(2,1)} %get-tuple-element.34.xg_ref), calls=%async_computation.2 | async-start | bytes 4194304 | tf_op jit(solution)/shard_map/all_to_all | solution.py:303
  100.1 29.6 %collective-permute-start.19 = (bf16[128,4096]{1,0:T(8,128)(2,1)}, bf16[128,4096]{1,0:T(8,128)(2,1)S(1)}, u32[]{:S(2)}, u32[]{:S(2)}) collective-permute-start(bf16[128,4096]{1,0:T(8,128)(2,1)} %collective-permute-done.11), channel_id=1, source_target_pairs={{0,2},{1,3},{2,4},{3,5},{4,6},{5,7},{8,10},{9,11},{10,12},{11,13},... | collective-permute-start | bytes 3145736 | tf_op jit(solution)/shard_map/ppermute | solution.py:253
  102.9 30.2 %collective-permute-start.20 = (bf16[128,4096]{1,0:T(8,128)(2,1)}, bf16[128,4096]{1,0:T(8,128)(2,1)S(1)}, u32[]{:S(2)}, u32[]{:S(2)}) collective-permute-start(bf16[128,4096]{1,0:T(8,128)(2,1)} %collective-permute-done.12), channel_id=1, source_target_pairs={{2,0},{3,1},{4,2},{5,3},{6,4},{7,5},{10,8},{11,9},{12,10},{13,11},... | collective-permute-start | bytes 3145736 | tf_op jit(solution)/shard_map/ppermute | solution.py:253
  110.7 40.6 %collective-permute-start.22 = (bf16[128,4096]{1,0:T(8,128)(2,1)}, bf16[128,4096]{1,0:T(8,128)(2,1)S(1)}, u32[]{:S(2)}, u32[]{:S(2)}) collective-permute-start(bf16[128,4096]{1,0:T(8,128)(2,1)} %collective-permute-done.14), channel_id=1, source_target_pairs={{0,2},{1,3},{2,4},{3,5},{4,6},{5,7},{8,10},{9,11},{10,12},{11,13},... | collective-permute-start | bytes 3145736 | tf_op jit(solution)/shard_map/ppermute | solution.py:253
  144.9 29.3 %all-to-all-start.4 = ((bf16[4,256,1024]{2,1,0:T(8,128)(2,1)}), bf16[4,256,1024]{2,1,0:T(8,128)(2,1)}, u32[]{:S(2)}, u32[]{:S(2)}) async-start(bf16[4,256,1024]{2,1,0:T(8,128)(2,1)} %get-tuple-element.44.xg_ref), calls=%async_computation.4 | async-start | bytes 4194304 | tf_op jit(solution)/shard_map/all_to_all | solution.py:303
  158.5 39.4 %collective-permute-start.21 = (bf16[128,4096]{1,0:T(8,128)(2,1)S(1)}, bf16[128,4096]{1,0:T(8,128)(2,1)}, u32[]{:S(2)}, u32[]{:S(2)}) collective-permute-start(bf16[128,4096]{1,0:T(8,128)(2,1)S(1)} %get-tuple-element.64.t0_ref), channel_id=1, source_target_pairs={{0,1},{1,0},{2,3},{3,2},{4,5},{5,4},{6,7},{7,6},{8,9},{9,8},{10,11... | collective-permute-start | bytes 3145736 | tf_op jit(solution)/shard_map/ppermute | solution.py:256
  159.0 40.5 %collective-permute-start.24 = (bf16[128,4096]{1,0:T(8,128)(2,1)}, bf16[128,4096]{1,0:T(8,128)(2,1)}, u32[]{:S(2)}, u32[]{:S(2)}) collective-permute-start(bf16[128,4096]{1,0:T(8,128)(2,1)} %get-tuple-element.62.g0_ref), channel_id=1, source_target_pairs={{0,1},{1,0},{2,3},{3,2},{4,5},{5,4},{6,7},{7,6},{8,9},{9,8},{10,11... | collective-permute-start | bytes 3145736 | tf_op jit(solution)/shard_map/ppermute | solution.py:256
  174.2 71.9 %all-to-all-start.3 = ((bf16[4,256,1024]{2,1,0:T(8,128)(2,1)}), bf16[4,256,1024]{2,1,0:T(8,128)(2,1)}, u32[]{:S(2)}, u32[]{:S(2)}) async-start(bf16[4,256,1024]{2,1,0:T(8,128)(2,1)} %get-tuple-element.39.xg_ref), calls=%async_computation.3 | async-start | bytes 4194304 | tf_op jit(solution)/shard_map/all_to_all | solution.py:303
  188.1 37.2 %collective-permute-start.30 = (bf16[256,1024]{1,0:T(8,128)(2,1)}, bf16[256,1024]{1,0:T(8,128)(2,1)S(1)}, u32[]{:S(2)}, u32[]{:S(2)}) collective-permute-start(bf16[256,1024]{1,0:T(8,128)(2,1)} %get-tuple-element.32.dw_ref.refs_3_), channel_id=1, source_target_pairs={{0,8},{8,0},{16,24},{24,16},{1,9},{9,1},{17,25},{25,17},{2,10},{10... | collective-permute-start | bytes 1572872 | tf_op jit(solution)/shard_map/ppermute | solution.py:305
  188.7 38.0 %collective-permute-start.31 = (bf16[256,1024]{1,0:T(8,128)(2,1)}, bf16[256,1024]{1,0:T(8,128)(2,1)S(1)}, u32[]{:S(2)}, u32[]{:S(2)}) collective-permute-start(bf16[256,1024]{1,0:T(8,128)(2,1)} %get-tuple-element.32.dw_ref.refs_3_), channel_id=1, source_target_pairs={{0,16},{8,24},{16,0},{24,8},{1,17},{9,25},{17,1},{25,9},{2,18},{10... | collective-permute-start | bytes 1572872 | tf_op jit(solution)/shard_map/ppermute | solution.py:305
  195.1 34.0 %collective-permute-start.32 = (bf16[256,1024]{1,0:T(8,128)(2,1)}, bf16[256,1024]{1,0:T(8,128)(2,1)S(1)}, u32[]{:S(2)}, u32[]{:S(2)}) collective-permute-start(bf16[256,1024]{1,0:T(8,128)(2,1)} %get-tuple-element.32.dw_ref.refs_3_), channel_id=1, source_target_pairs={{0,24},{8,16},{16,8},{24,0},{1,25},{9,17},{17,9},{25,1},{2,26},{10... | collective-permute-start | bytes 1572872 | tf_op jit(solution)/shard_map/ppermute | solution.py:305
  197.9 34.9 %collective-permute-start.17 = (bf16[64,4096]{1,0:T(8,128)(2,1)S(1)}, bf16[64,4096]{1,0:T(8,128)(2,1)S(1)}, u32[]{:S(2)}, u32[]{:S(2)}) collective-permute-start(bf16[64,4096]{1,0:T(8,128)(2,1)S(1)} %get-tuple-element.45), channel_id=1, source_target_pairs={{0,4},{1,5},{2,6},{3,7},{4,0},{5,1},{6,2},{7,3},{8,12},{9,13},{10,... | collective-permute-start | bytes 1572872 | tf_op jit(solution)/shard_map/ppermute | solution.py:256
  199.5 44.5 %collective-permute-start.18 = (bf16[64,4096]{1,0:T(8,128)(2,1)S(1)}, bf16[64,4096]{1,0:T(8,128)(2,1)S(1)}, u32[]{:S(2)}, u32[]{:S(2)}) collective-permute-start(bf16[64,4096]{1,0:T(8,128)(2,1)S(1)} %get-tuple-element.46), channel_id=1, source_target_pairs={{0,5},{1,4},{2,7},{3,6},{4,1},{5,0},{6,3},{7,2},{8,13},{9,12},{10,... | collective-permute-start | bytes 1572872 | tf_op jit(solution)/shard_map/ppermute | solution.py:256
  227.5 51.3 %collective-permute-start.9 = (bf16[64,4096]{1,0:T(8,128)(2,1)}, bf16[64,4096]{1,0:T(8,128)(2,1)S(1)}, u32[]{:S(2)}, u32[]{:S(2)}) collective-permute-start(bf16[64,4096]{1,0:T(8,128)(2,1)} %get-tuple-element.40), channel_id=1, source_target_pairs={{0,2},{1,3},{2,0},{3,1},{4,6},{5,7},{6,4},{7,5},{8,10},{9,11},{10,... | collective-permute-start | bytes 1572872 | tf_op jit(solution)/shard_map/ppermute | solution.py:256
  229.9 60.1 %collective-permute-start.10 = (bf16[64,4096]{1,0:T(8,128)(2,1)}, bf16[64,4096]{1,0:T(8,128)(2,1)}, u32[]{:S(2)}, u32[]{:S(2)}) collective-permute-start(bf16[64,4096]{1,0:T(8,128)(2,1)} %get-tuple-element.41), channel_id=1, source_target_pairs={{0,3},{1,2},{2,1},{3,0},{4,7},{5,6},{6,5},{7,4},{8,11},{9,10},{10,... | collective-permute-start | bytes 1572872 | tf_op jit(solution)/shard_map/ppermute | solution.py:256
  233.7 56.9 %collective-permute-start.25 = (bf16[64,4096]{1,0:T(8,128)(2,1)}, bf16[64,4096]{1,0:T(8,128)(2,1)}, u32[]{:S(2)}, u32[]{:S(2)}) collective-permute-start(bf16[64,4096]{1,0:T(8,128)(2,1)} %get-tuple-element.50), channel_id=1, source_target_pairs={{0,6},{1,7},{2,4},{3,5},{4,2},{5,3},{6,0},{7,1},{8,14},{9,15},{10,... | collective-permute-start | bytes 1572872 | tf_op jit(solution)/shard_map/ppermute | solution.py:256
  244.8 46.1 %collective-permute-start.26 = (bf16[64,4096]{1,0:T(8,128)(2,1)}, bf16[64,4096]{1,0:T(8,128)(2,1)}, u32[]{:S(2)}, u32[]{:S(2)}) collective-permute-start(bf16[64,4096]{1,0:T(8,128)(2,1)} %get-tuple-element.51), channel_id=1, source_target_pairs={{0,7},{1,6},{2,5},{3,4},{4,3},{5,2},{6,1},{7,0},{8,15},{9,14},{10,... | collective-permute-start | bytes 1572872 | tf_op jit(solution)/shard_map/ppermute | solution.py:256
  246.1 113.6 %all-to-all-start.1 = ((bf16[4,256,1024]{2,1,0:T(8,128)(2,1)}), bf16[4,256,1024]{2,1,0:T(8,128)(2,1)S(1)}, u32[]{:S(2)}, u32[]{:S(2)}) async-start(bf16[4,256,1024]{2,1,0:T(8,128)(2,1)} %get-tuple-element.49.xg_ref), calls=%async_computation.1 | async-start | bytes 4194304 | tf_op jit(solution)/shard_map/all_to_all | solution.py:303
  250.5 83.5 %collective-permute-start.37 = (bf16[256,1024]{1,0:T(8,128)(2,1)}, bf16[256,1024]{1,0:T(8,128)(2,1)}, u32[]{:S(2)}, u32[]{:S(2)}) collective-permute-start(bf16[256,1024]{1,0:T(8,128)(2,1)} %get-tuple-element.42.dw_ref.refs_11_), channel_id=1, source_target_pairs={{0,16},{8,24},{16,0},{24,8},{1,17},{9,25},{17,1},{25,9},{2,18},{10... | collective-permute-start | bytes 1572872 | tf_op jit(solution)/shard_map/ppermute | solution.py:305
  279.6 56.8 %collective-permute-start.38 = (bf16[256,1024]{1,0:T(8,128)(2,1)}, bf16[256,1024]{1,0:T(8,128)(2,1)}, u32[]{:S(2)}, u32[]{:S(2)}) collective-permute-start(bf16[256,1024]{1,0:T(8,128)(2,1)} %get-tuple-element.42.dw_ref.refs_11_), channel_id=1, source_target_pairs={{0,24},{8,16},{16,8},{24,0},{1,25},{9,17},{17,9},{25,1},{2,26},{10... | collective-permute-start | bytes 1572872 | tf_op jit(solution)/shard_map/ppermute | solution.py:305
  290.0 47.9 %collective-permute-start.33 = (bf16[256,1024]{1,0:T(8,128)(2,1)}, bf16[256,1024]{1,0:T(8,128)(2,1)}, u32[]{:S(2)}, u32[]{:S(2)}) collective-permute-start(bf16[256,1024]{1,0:T(8,128)(2,1)} %copy-done.22), channel_id=1, source_target_pairs={{0,8},{8,0},{16,24},{24,16},{1,9},{9,1},{17,25},{25,17},{2,10},{10... | collective-permute-start | bytes 1572872 | tf_op jit(solution)/shard_map/ppermute | solution.py:305
  290.6 47.4 %collective-permute-start.34 = (bf16[256,1024]{1,0:T(8,128)(2,1)}, bf16[256,1024]{1,0:T(8,128)(2,1)}, u32[]{:S(2)}, u32[]{:S(2)}) collective-permute-start(bf16[256,1024]{1,0:T(8,128)(2,1)} %copy-done.22), channel_id=1, source_target_pairs={{0,16},{8,24},{16,0},{24,8},{1,17},{9,25},{17,1},{25,9},{2,18},{10... | collective-permute-start | bytes 1572872 | tf_op jit(solution)/shard_map/ppermute | solution.py:305
  291.0 47.0 %collective-permute-start.35 = (bf16[256,1024]{1,0:T(8,128)(2,1)}, bf16[256,1024]{1,0:T(8,128)(2,1)}, u32[]{:S(2)}, u32[]{:S(2)}) collective-permute-start(bf16[256,1024]{1,0:T(8,128)(2,1)} %copy-done.22), channel_id=1, source_target_pairs={{0,24},{8,16},{16,8},{24,0},{1,25},{9,17},{17,9},{25,1},{2,26},{10... | collective-permute-start | bytes 1572872 | tf_op jit(solution)/shard_map/ppermute | solution.py:305
  (44 other events, 594.5 us)

commit v2 on v1

v2 whole, which is shorter than its diff:
```python
import functools

import jax
import jax.numpy as jnp
from jax import lax
from jax.experimental import pallas as pl
from jax.experimental.pallas import tpu as pltpu
from jax.sharding import PartitionSpec as P

SPLIT = True
VMEM_LIMIT = 48 * 1024 * 1024
SMALL = pl.CostEstimate(flops=1024, bytes_accessed=1024, transcendentals=0)


def gelu_pair(values):
    inner = 0.7978845608 * (values + 0.044715 * values * values * values)
    tangent = jnp.tanh(inner)
    result = 0.5 * values * (1.0 + tangent)
    slope = 0.5 * (1.0 + tangent) + 0.5 * values * (1.0 - tangent * tangent) * 0.7978845608 * (
        1.0 + 3.0 * 0.044715 * values * values
    )
    return (result, slope)


def gate_logits(tokens, router_weight):
    high = lax.reduce_precision(router_weight, 8, 7)
    rest = router_weight - high
    middle = lax.reduce_precision(rest, 8, 7)
    low = rest - middle
    terms = jnp.concatenate([high, middle, low], axis=1).astype(jnp.bfloat16)
    parts = jnp.dot(tokens, terms, preferred_element_type=jnp.float32)
    experts = router_weight.shape[1]
    return parts[:, :experts] + parts[:, experts : 2 * experts] + parts[:, 2 * experts :]


EXTRA = 16


LARGE = pl.CostEstimate(flops=10000000000, bytes_accessed=1024, transcendentals=0)


def picks_of(meta_ref, tok_rows):
    places = lax.broadcasted_iota(jnp.int32, (meta_ref.shape[0], tok_rows), 1).astype(jnp.float32)
    return jnp.where(meta_ref[:, 0:1] == places, 1.0, 0.0).astype(jnp.bfloat16)


def pick(picks, near_ref, far_ref, first):
    half = picks.shape[0] // 2
    part = pl.ds(first, picks.shape[1])
    top = jnp.dot(picks[:half], near_ref[part], preferred_element_type=jnp.float32)
    bottom = jnp.dot(picks[half:], far_ref[part], preferred_element_type=jnp.float32)
    return jnp.concatenate([top, bottom], axis=0).astype(jnp.bfloat16)


def pick_kernel(meta_ref, near_ref, far_ref, out_ref):
    rows = meta_ref.shape[0]
    tok_rows = near_ref.shape[0] // 2
    picks = picks_of(meta_ref, tok_rows)
    out_ref[0, :rows] = pick(picks, near_ref, far_ref, 0)
    out_ref[0, rows:] = pick(picks, near_ref, far_ref, tok_rows)


def pick_rows(meta, near, far, dp):
    rows = meta.shape[0]
    both_rows, width = near.shape
    piece = width // dp
    block = pl.BlockSpec((both_rows, piece), lambda k: (0, k))
    return pl.pallas_call(
        pick_kernel,
        grid=(dp,),
        in_specs=[pl.BlockSpec(meta.shape, lambda k: (0, 0)), block, block],
        out_specs=pl.BlockSpec((1, 2 * rows, piece), lambda k: (k, 0, 0)),
        out_shape=jax.ShapeDtypeStruct((dp, 2 * rows, piece), jnp.bfloat16),
        compiler_params=pltpu.CompilerParams(vmem_limit_bytes=VMEM_LIMIT),
        cost_estimate=SMALL,
        name="pick_rows",
    )(meta, near, far)


def hidden_kernel(ready, meta_ref, router_ref, *refs):
    sources, refs = (refs[:1], refs[1:]) if ready else (refs[:2], refs[2:])
    up_ref, down_ref, message_ref, lg_ref, pre, back, logit, held = refs
    step = pl.program_id(0)
    steps = pl.num_programs(0)
    rows = meta_ref.shape[0]
    trailing = (((1,), (1,)), ((), ()))
    if ready:
        x, g = sources[0][0, :rows], sources[0][0, rows:]
    else:
        tok_rows = sources[0].shape[0] // 2
        picks = picks_of(meta_ref, tok_rows)
        x, g = pick(picks, *sources, 0), pick(picks, *sources, tok_rows)
        message_ref[step, :rows] = x
        message_ref[step, rows : 2 * rows] = g
    held[step] = x
    pre_term = jnp.dot(x, up_ref[...], preferred_element_type=jnp.float32)
    back_term = jnp.dot(g, down_ref[...], preferred_element_type=jnp.float32)
    logit_term = lax.dot_general(x, router_ref[...], trailing, preferred_element_type=jnp.float32)

    @pl.when(step == 0)
    def _():
        pre[...] = pre_term
        back[...] = back_term
        logit[...] = logit_term

    @pl.when(step > 0)
    def _():
        pre[...] += pre_term
        back[...] += back_term
        logit[...] += logit_term

    @pl.when(step == steps - 1)
    def _():
        gate = jax.nn.sigmoid(jnp.sum(logit[...], axis=1, keepdims=True))
        weight = gate * meta_ref[:, 1:2]
        active, slope = gelu_pair(pre[...])
        grad = back[...]
        score = jnp.sum(active.astype(jnp.bfloat16).astype(jnp.float32) * grad, axis=1, keepdims=True)
        pre_grad = (weight * grad * slope).astype(jnp.bfloat16)
        scaled = (weight * active).astype(jnp.bfloat16)
        lg = score * weight * (1.0 - gate)
        lg_ref[...] = jnp.broadcast_to(lg, lg_ref.shape)
        flat = jnp.transpose(jnp.broadcast_to(lg, (rows, rows)))[:8]
        high = flat.astype(jnp.bfloat16)
        rest = flat - high.astype(jnp.float32)
        middle = rest.astype(jnp.bfloat16)
        low = (rest - middle.astype(jnp.float32)).astype(jnp.bfloat16)
        columns = []
        for k in range(held.shape[0]):
            terms = [jnp.dot(part, held[k], preferred_element_type=jnp.float32) for part in (high, middle, low)]
            columns.append((terms[0] + terms[1] + terms[2])[0:1])
        column = jnp.concatenate(columns, axis=0)
        first = column.astype(jnp.bfloat16)
        second = (column - first.astype(jnp.float32)).astype(jnp.bfloat16)
        empty = jnp.zeros((EXTRA - 2 * column.shape[0], column.shape[1]), jnp.float32)
        extra = jnp.concatenate(
            [first.astype(jnp.float32), second.astype(jnp.float32), empty], axis=0
        ).astype(jnp.bfloat16)
        base = 0 if ready else 2 * rows
        for k in range(message_ref.shape[0]):
            message_ref[k, base : base + rows] = pre_grad
            message_ref[k, base + rows : base + 2 * rows] = scaled
            message_ref[k, base + 2 * rows :] = extra


def hidden(meta, router, sources, w_up, w_down, dp):
    rows = meta.shape[0]
    width, hid = w_up.shape
    piece = width // dp
    ready = len(sources) == 1
    shape = (1, 2 * rows + EXTRA, piece) if ready else (dp, 4 * rows + EXTRA, piece)
    weight = pl.BlockSpec((piece, hid), lambda k: (k, 0))
    whole = lambda shape: pl.BlockSpec(shape, lambda k: (0,) * len(shape))
    if ready:
        blocks = [pl.BlockSpec((1, 2 * rows, piece), lambda k: (k, 0, 0))]
    else:
        blocks = [pl.BlockSpec((sources[0].shape[0], piece), lambda k: (0, k))] * 2
    return pl.pallas_call(
        functools.partial(hidden_kernel, ready),
        grid=(dp,),
        in_specs=[whole(meta.shape), pl.BlockSpec((router.shape[0], piece), lambda k: (0, k))]
        + blocks
        + [weight, weight],
        out_specs=[whole(shape), whole((rows, 128))],
        out_shape=[
            jax.ShapeDtypeStruct(shape, jnp.bfloat16),
            jax.ShapeDtypeStruct((rows, 128), jnp.float32),
        ],
        scratch_shapes=[pltpu.VMEM((rows, hid), jnp.float32)] * 2
        + [pltpu.VMEM((rows, router.shape[0]), jnp.float32), pltpu.VMEM((dp, rows, piece), jnp.bfloat16)],
        compiler_params=pltpu.CompilerParams(vmem_limit_bytes=VMEM_LIMIT),
        cost_estimate=SMALL,
        name="hidden",
    )(meta, router, *sources, w_up, w_down)


def rows_kernel(grad_ref, lg_ref, up_ref, router_ref, near_ref, far_ref):
    rows = lg_ref.shape[0]
    half = rows // 2
    trailing = (((1,), (1,)), ((), ()))
    out = lax.dot_general(grad_ref[...].reshape(rows, -1), up_ref[...], trailing, preferred_element_type=jnp.float32)
    out = (out + lg_ref[:, 0:1] * router_ref[...]).astype(jnp.bfloat16)
    near_ref[...] = out[:half]
    far_ref[...] = out[half:]


def back_rows(message, lg, w_up, router_row, steps):
    first = 0 if message.shape[0] == 1 else 2
    rows = lg.shape[0]
    width, hid = w_up.shape
    piece = width // steps
    whole = lambda shape: pl.BlockSpec(shape, lambda k: (0, 0))
    half = pl.BlockSpec((rows // 2, piece), lambda k: (0, k))
    return pl.pallas_call(
        rows_kernel,
        grid=(steps,),
        in_specs=[
            pl.BlockSpec((1, rows, hid), lambda k: (0, first, 0)),
            whole(lg.shape),
            pl.BlockSpec((piece, hid), lambda k: (k, 0)),
            pl.BlockSpec((1, piece), lambda k: (0, k)),
        ],
        out_specs=[half, half],
        out_shape=[jax.ShapeDtypeStruct((rows // 2, width), jnp.bfloat16)] * 2,
        compiler_params=pltpu.CompilerParams(vmem_limit_bytes=VMEM_LIMIT),
        cost_estimate=SMALL,
        name="back_rows",
    )(message, lg, w_up, router_row)


def weights_kernel(sizes, has_start, place_ref, *refs):
    refs = list(refs)
    chunks = []
    for size in sizes:
        left = refs.pop(0)
        dp, double = left.shape[:2]
        rows = double // 2
        rights = [refs.pop(0) for _ in range(size)]
        if size == 1:
            pairs = [(left.at[k], rights[0].at[k], 2 * rows) for k in range(dp)]
        else:
            pairs = [(left.at[place_ref[0] ^ k], rights[k].at[0], 0) for k in range(dp)]
        chunks.append(pairs)
    start = [refs.pop(0) for _ in range(3)] if has_start else None
    outs = refs
    contract = (((0,), (0,)), ((), ()))
    for which in range(2):
        total = start[which][...] if has_start else None
        low = which * rows
        for pairs in chunks:
            left = jnp.concatenate([ref[low : low + rows] for ref, _, _ in pairs], axis=0)
            right = jnp.concatenate([ref[base + low : base + low + rows] for _, ref, base in pairs], axis=0)
            term = lax.dot_general(left, right, contract, preferred_element_type=jnp.float32)
            total = term if total is None else total + term
        outs[which][...] = total.astype(outs[which].dtype)
    column = start[2][...] if has_start else jnp.zeros(outs[2].shape, jnp.float32)
    for pairs in chunks:
        for _, ref, base in pairs:
            both = ref[base + 2 * rows :].astype(jnp.float32)
            column = column + both[:dp] + both[dp : 2 * dp]
    outs[2][...] = column


def weight_terms(place, chunks, rows, start, last):
    dp, _, piece = chunks[0][0].shape
    tile = min(piece, 256)
    kind = jnp.bfloat16 if last else jnp.float32
    strip = pl.BlockSpec((tile, piece), lambda i, place: (i, 0))
    column = pl.BlockSpec((dp, piece), lambda i, place: (0, 0))
    specs, arrays = [], []
    for blocks in chunks:
        rights = blocks if len(blocks) == 1 else blocks[1:]
        specs.append(pl.BlockSpec((dp, 2 * rows, tile), lambda i, place: (0, 0, i)))
        specs += [pl.BlockSpec(block.shape, lambda i, place: (0, 0, 0)) for block in rights]
        arrays += [blocks[0], *rights]
    if start is not None:
        specs += [strip, strip, column]
        arrays += list(start)
    sizes = [1 if len(blocks) == 1 else len(blocks) - 1 for blocks in chunks]
    return pl.pallas_call(
        functools.partial(weights_kernel, sizes, start is not None),
        grid_spec=pltpu.PrefetchScalarGridSpec(
            num_scalar_prefetch=1, grid=(piece // tile,), in_specs=specs, out_specs=[strip, strip, column]
        ),
        out_shape=[jax.ShapeDtypeStruct((piece, piece), kind)] * 2
        + [jax.ShapeDtypeStruct((dp, piece), jnp.float32)],
        compiler_params=pltpu.CompilerParams(vmem_limit_bytes=VMEM_LIMIT),
        cost_estimate=SMALL if last else LARGE,
        name="weight_terms",
    )(place, *arrays)


def combine_kernel(slots_ref, *refs):
    blocks, out_ref = refs[:-1], refs[-1]
    tok_rows = out_ref.shape[0]
    places = lax.broadcasted_iota(jnp.int32, (tok_rows, slots_ref.shape[1]), 0).astype(jnp.float32)
    picks = jnp.where(slots_ref[...] == places, 1.0, 0.0).astype(jnp.bfloat16)
    rows = jnp.concatenate([block[...] for block in blocks], axis=0)
    out_ref[...] = jnp.dot(picks, rows, preferred_element_type=jnp.float32).astype(out_ref.dtype)


def combine(slots, blocks, tok_rows):
    per_slot, width = blocks[0].shape
    tile = 1024 if width % 1024 == 0 else width
    block = pl.BlockSpec((per_slot, tile), lambda k: (0, k))
    return pl.pallas_call(
        combine_kernel,
        grid=(width // tile,),
        in_specs=[pl.BlockSpec(slots.shape, lambda k: (0, 0))] + [block] * len(blocks),
        out_specs=pl.BlockSpec((tok_rows, tile), lambda k: (0, k)),
        out_shape=jax.ShapeDtypeStruct((tok_rows, width), jnp.bfloat16),
        compiler_params=pltpu.CompilerParams(vmem_limit_bytes=VMEM_LIMIT),
        cost_estimate=SMALL,
        name="combine",
    )(slots, *blocks)


def after(block, *others):
    return lax.optimization_barrier((block,) + others)[0]


def on_line(tokens, out_grad, route_slots, expert_counts, router_weight, up_weight, down_weight):
    experts = lax.axis_size("expert")
    dp = lax.axis_size("dp")
    chips = experts // 2
    me = lax.axis_index("expert")
    chip = me // 2
    core = me % 2
    tok_rows = tokens.shape[0]
    slots = route_slots[0, 0]
    per_slot = slots.shape[1]
    w_up = up_weight[0]
    w_down = down_weight[0]
    middle = jnp.logical_and(chip >= 1, chip <= 2)

    def between(block, chip_pairs):
        pairs = [(2 * a + c, 2 * b + c) for a, b in chip_pairs for c in range(2)]
        return lax.ppermute(block, "expert", pairs)

    def across(block, mask):
        return lax.ppermute(block, "expert", [(e, e ^ mask) for e in range(experts)])

    slots_float = slots.astype(jnp.float32)
    counts = jnp.broadcast_to(expert_counts.astype(jnp.float32)[None, :], (experts, tok_rows))
    own_facts = jnp.concatenate([slots_float, counts], axis=1)
    facts = lax.all_to_all(own_facts, "expert", 0, 0, tiled=True)
    got_slots = facts[:, :per_slot]
    hits = got_slots[:, :, None] == jnp.arange(tok_rows, dtype=jnp.float32)[None, None, :]
    got_counts = jnp.sum(jnp.where(hits, facts[:, None, per_slot:], 0.0), axis=2)
    shares = jnp.where(got_slots >= 0, 1.0 / jnp.maximum(got_counts, 1.0), 0.0)
    metas = jnp.stack([got_slots, shares], axis=-1).reshape(chips, 2, per_slot, 2)
    metas = jnp.where(core == 0, metas, metas[:, ::-1]).reshape(chips, 2 * per_slot, 2)
    mine = slots_float.reshape(chips, 2, per_slot)
    mine = jnp.where(core == 0, mine, mine[:, ::-1])
    order = [chip ^ j for j in range(chips)]
    mine = jnp.concatenate([lax.dynamic_index_in_dim(mine, k, 0, False) for k in order], axis=0)

    router_row = lax.dynamic_index_in_dim(router_weight.T, me, 0, True)
    high = lax.reduce_precision(router_row, 8, 7)
    rest = router_row - high
    mid = lax.reduce_precision(rest, 8, 7)
    router = jnp.concatenate([high, mid, rest - mid, jnp.zeros((13, high.shape[1]), jnp.float32)], axis=0)
    router = router.astype(jnp.bfloat16)

    ends = [(0, 1), (1, 0), (2, 3), (3, 2)]
    inner = [(1, 2), (2, 1)]
    outward = [(1, 0), (2, 3)]

    def settle(pair):
        return pair if not isinstance(pair, tuple) else jnp.where(middle, pair[0], pair[1])

    own = after(jnp.concatenate([tokens, out_grad], axis=0), facts)
    one, inside = between(own, ends), between(own, inner)

    place = jnp.reshape(lax.axis_index("dp"), (1,)).astype(jnp.int32)

    def exchange(block):
        return lax.all_to_all(block, "dp", 0, 0, tiled=True)

    def chunk(j, pair, before, split=False):
        near_block = settle(pair)
        far_block = across(near_block, 1)
        meta = lax.dynamic_index_in_dim(metas, order[j], 0, False)
        meta = after(meta, *before)
        if split:
            rows = pick_rows(meta, near_block, far_block, dp)
            message, lg = hidden(meta, router, (rows,), w_up, w_down, dp)
            got = [exchange(rows), message]
            for k in range(1, dp):
                got.append(lax.ppermute(message, "dp", [(q, q ^ k) for q in range(dp)]))
        else:
            message, lg = hidden(meta, router, (near_block, far_block), w_up, w_down, dp)
            got = [exchange(message)]
        near, far = back_rows(message, lg, w_up, router_row, dp)
        return got, jnp.concatenate([near, across(far, 1)], axis=0)

    got0, back0 = chunk(0, own, ())
    inside_two, out_two = between(one, inner), between(inside, outward)
    got1, back1 = chunk(1, one, (back0,))
    out_three = between(inside_two, outward)
    got2, back2 = chunk(2, (inside_two, out_two), (back1,))
    got3, back3 = chunk(3, (inside, out_three), (back2,), split=SPLIT)
    back1, back2 = across(back1, 2), across(back2, 4)
    back3 = across(after(back3, back1, back2), 6)
    rows = 2 * per_slot
    early = weight_terms(place, [got0, got1, got2], rows, None, False)
    blocks = [back0, back1, back2, back3]
    up_sum, down_sum, column = weight_terms(place, [got3], rows, early, True)
    tokens_grad = combine(mine.reshape(1, -1), blocks, tok_rows)
    return (tokens_grad, up_sum[None], down_sum[None], column.reshape(-1, 1))


def on_any(tokens, out_grad, route_slots, expert_counts, router_weight, up_weight, down_weight):
    experts = lax.axis_size("expert")
    me = lax.axis_index("expert")
    tok_rows = tokens.shape[0]
    width = tokens.shape[1]
    slots = route_slots[0, 0]
    per_slot = slots.shape[1]
    received = experts * per_slot
    contract = (((0,), (0,)), ((), ()))
    trailing = (((1,), (1,)), ((), ()))
    picks = slots[:, :, None] == jnp.arange(tok_rows, dtype=jnp.int32)[None, None, :]
    pick_half = picks.astype(jnp.bfloat16).reshape(received, tok_rows)
    gates = jax.nn.sigmoid(gate_logits(tokens, router_weight)).T
    counts = jnp.maximum(expert_counts, 1).astype(jnp.float32)[None, :]
    weight_slot = jnp.sum(jnp.where(picks, (gates / counts)[:, None, :], 0.0), axis=2)
    slope_slot = jnp.sum(jnp.where(picks, (gates * (1.0 - gates) / counts)[:, None, :], 0.0), axis=2)
    swap = lambda block: lax.all_to_all(block, "expert", split_axis=0, concat_axis=0, tiled=True)
    send_rows = jnp.dot(pick_half, tokens, preferred_element_type=jnp.float32).astype(jnp.bfloat16)
    send_grads = jnp.dot(pick_half, out_grad, preferred_element_type=jnp.float32).astype(jnp.bfloat16)
    rows_in = swap(send_rows)
    grads_in = swap(send_grads)
    facts = swap(jnp.concatenate([weight_slot, slope_slot], axis=1))
    weight_in = facts[:, :per_slot].reshape(received)
    slope_in = facts[:, per_slot:].reshape(received)
    w_up = up_weight[0]
    w_down = down_weight[0]
    pre = jnp.dot(rows_in, w_up, preferred_element_type=jnp.float32)
    active, slope = gelu_pair(pre)
    grad = jnp.dot(grads_in, w_down, preferred_element_type=jnp.float32)
    score = jnp.sum(active.astype(jnp.bfloat16).astype(jnp.float32) * grad, axis=1)
    logit_grad = score * slope_in
    pre_grad = (weight_in[:, None] * grad * slope).astype(jnp.bfloat16)
    scaled = (weight_in[:, None] * active).astype(jnp.bfloat16)
    router_row = lax.dynamic_index_in_dim(router_weight.T, me, 0, True)
    row_grad = lax.dot_general(pre_grad, w_up, trailing, preferred_element_type=jnp.float32)
    back = swap((row_grad + logit_grad[:, None] * router_row).astype(jnp.bfloat16))
    up_term = lax.dot_general(rows_in, pre_grad, contract, preferred_element_type=jnp.float32)
    down_term = lax.dot_general(grads_in, scaled, contract, preferred_element_type=jnp.float32)
    spread = lambda term: lax.psum_scatter(
        term.astype(jnp.bfloat16), "dp", scatter_dimension=0, tiled=True
    )
    tokens_grad = lax.dot_general(pick_half, back, contract, preferred_element_type=jnp.float32)
    column = jnp.sum(logit_grad[:, None] * rows_in.astype(jnp.float32), axis=0, keepdims=True)
    router_grad = lax.psum(column, "dp").T
    return (tokens_grad.astype(jnp.bfloat16), spread(up_term)[None], spread(down_term)[None], router_grad)


def solution(mesh):
    line = mesh.shape["expert"] == 8 and mesh.shape["dp"] == 4
    return jax.shard_map(
        on_line if line else on_any,
        mesh=mesh,
        in_specs=(
            P(("dp", "expert"), None),
            P(("dp", "expert"), None),
            P("dp", "expert", None, None),
            P(("dp", "expert")),
            P(),
            P("expert", None, None),
            P("expert", None, None),
        ),
        out_specs=(
            P(("dp", "expert"), None),
            P("expert", "dp", None),
            P("expert", "dp", None),
            P(None, "expert"),
        ),
        check_vma=False,
    )
```

time: 374 us -> 278 us (0.74); the launches traced: 368 us -> 277 us
  waiting for transfers between devices: 132 us -> 91.7 us
  blocking collectives: 31.9 us -> 0 us
  starting transfers between devices: 82.2 us -> 52.6 us
  Pallas kernels: 88.8 us -> 98.5 us
    all_to_all x5, waiting for transfers between devices: 36.8 us -> 1.5 us  [the longest x4 0.88 us: exchange(): return lax.all_to_all(block, 'dp', 0, 0, tiled=True)]
    psum x1 -> x0, blocking collectives: 31.9 us -> none  [on_line(): router_grad = lax.psum(sum(columns), 'dp').T]
    ppermute x39 -> x19, starting transfers between devices: 55.8 us -> 26.2 us  [the longest x5 16.7 us: between(): return lax.ppermute(block, 'expert', pairs)]
    pallas_call x10 -> x11, Pallas kernels: 84.5 us -> 94.2 us  [the longest x4 44.8 us: hidden(): pl.pallas_call(functools.partial(hidden_kernel, ready), grid=(dp,), in_sp...]
    ppermute x39 -> x19, waiting for transfers between devices: 94.9 us -> 90.2 us  [the longest x5 57.1 us: between(): return lax.ppermute(block, 'expert', pairs)]
    concatenate x0 -> x4, other arithmetic: none -> 4.03 us  [the longest x1 2.26 us: chunk(): return (got, jnp.concatenate([near, across(far, 1)], axis=0))]
    select_n x5 -> x4, other arithmetic: 7.58 us -> 3.64 us  [the longest x2 3.62 us: settle(): jnp.where(middle, pair[0], pair[1])]
    unnamed x65 -> x33, local copies, waits for them, and re-layouts: 17.1 us -> 19.8 us
  transfers between devices with their start and end apart: 44 -> 24, of which waited for: 14 -> 12; matrix products, arithmetic and copies ran while one was open for 4% -> 5% of each run, Pallas kernels for 22% -> 34%
where the time goes in v2:
time: 278 us; the launch traced here: 277 us
  Pallas kernels  98.5 us (35%)
  waiting for transfers between devices  91.7 us (33%)
  starting transfers between devices  52.6 us (19%)
  local copies, waits for them, and re-layouts  22.6 us (8%)
  other arithmetic  10.3 us (4%)
    ppermute x5, waiting for transfers between devices, between(): return lax.ppermute(block, 'expert', pairs)  57.1 us
    pallas_call x4, Pallas kernels, hidden(): pl.pallas_call(functools.partial(hidden_kernel, ready), grid=(dp,), in_sp...  44.8 us
    pallas_call x4, Pallas kernels, back_rows(): pl.pallas_call(rows_kernel, grid=(steps,), in_specs=[pl.BlockSpec((1, row...  24.4 us
    ppermute x11, waiting for transfers between devices, across(): lax.ppermute(block, 'expert', [(e, e ^ mask) for e in range(experts)])  23.8 us
    all_to_all x4, starting transfers between devices, exchange(): return lax.all_to_all(block, 'dp', 0, 0, tiled=True)  21.2 us
    pallas_call x2, Pallas kernels, weight_terms(): pl.pallas_call(functools.partial(weights_kernel, sizes, start is not None...  20.5 us
    unnamed x33, local copies, waits for them, and re-layouts  19.8 us
    ppermute x5, starting transfers between devices, between(): return lax.ppermute(block, 'expert', pairs)  16.7 us
  transfers between devices with their start and end apart: 24, of which 12 were waited for; matrix products, arithmetic and copies ran while one was open for 5% of the time, Pallas kernels for 34%

profile of v2, /device:TPU:22, one launch (start us, length us, event | category | flops | bytes accessed | tf_op | source)
XLA Modules:
  0.0 276.6 jit_solution(13839955031121820764)
XLA Ops:
  2.7 5.2 %all-to-all-start = ((f32[8,1,192]{2,1,0:T(1,128)}), f32[8,1,192]{2,1,0:T(1,128)S(1)}, u32[]{:S(2)}, u32[]{:S(2)}) async-start(f32[8,1,192]{2,1,0:T(1,128)} %all_to_all.20), calls=%async_computation | async-start | bytes 16384 | tf_op jit(solution)/shard_map/all_to_all | solution.py:326
  12.3 3.7 %collective-permute-start.7 = (bf16[256,4096]{1,0:T(8,128)(2,1)S(1)}, bf16[256,4096]{1,0:T(8,128)(2,1)}, u32[]{:S(2)}, u32[]{:S(2)}) collective-permute-start(bf16[256,4096]{1,0:T(8,128)(2,1)S(1)} %pad_maximum_fusion.refs_0_), channel_id=1, source_target_pairs={{2,4},{3,5},{4,2},{5,3},{10,12},{11,13},{12,10},{13,11},{18,20},{1... | collective-permute-start | bytes 6291464 | tf_op jit(solution)/shard_map/ppermute | solution.py:318
  16.9 12.0 %hidden.4 = (bf16[4,528,1024]{2,1,0:T(8,128)(2,1)}, f32[128,128]{1,0:T(8,128)S(1)}) custom-call(f32[128,2]{1,0:T(8,128)S(1)} %get-tuple-element.63.meta_ref, bf16[16,4096]{1,0:T(8,128)(2,1)S(1)} %maximum_maximum_fusion.router_ref, bf16[256,4096]{1,0:T(8,128)(2,1)S(1)} %pad_maximum_fusion.refs_0_, bf16[256,4096]{1,0:T(8,128)(2,1)} %collective-permute-done.refs_1_, ...), custom_call_target="tpu_custom_call" | custom-call | flops 1024 | bytes 1024 | tf_op jit(solution)/shard_map/hidden/pallas_call | solution.py:158
  28.8 5.3 %all-to-all-start.2 = ((bf16[4,528,1024]{2,1,0:T(8,128)(2,1)}), bf16[4,528,1024]{2,1,0:T(8,128)(2,1)}, u32[]{:S(2)}, u32[]{:S(2)}) async-start(bf16[4,528,1024]{2,1,0:T(8,128)(2,1)} %get-tuple-element.32.grad_ref), calls=%async_computation.2 | async-start | bytes 8650752 | tf_op jit(solution)/shard_map/all_to_all | solution.py:358
  34.2 25.2 %collective-permute-done.2.refs_0_ = bf16[256,4096]{1,0:T(8,128)(2,1)} collective-permute-done((bf16[256,4096]{1,0:T(8,128)(2,1)S(1)}, bf16[256,4096]{1,0:T(8,128)(2,1)}, u32[]{:S(2)}, u32[]{:S(2)}) %collective-permute-start.2) | collective-permute-done | bytes 2097184 | tf_op jit(solution)/shard_map/ppermute | solution.py:318
  59.4 3.4 %collective-permute-start.6 = (bf16[256,4096]{1,0:T(8,128)(2,1)}, bf16[256,4096]{1,0:T(8,128)(2,1)}, u32[]{:S(2)}, u32[]{:S(2)}) collective-permute-start(bf16[256,4096]{1,0:T(8,128)(2,1)} %collective-permute-done.2.refs_0_), channel_id=1, source_target_pairs={{2,4},{3,5},{4,2},{5,3},{10,12},{11,13},{12,10},{13,11},{18,20},{1... | collective-permute-start | bytes 6291464 | tf_op jit(solution)/shard_map/ppermute | solution.py:318
  62.8 2.7 collective-permute-start.8
  65.6 2.2 copy-done.2
  67.8 5.9 %back_rows.4 = (bf16[64,4096]{1,0:T(8,128)(2,1)S(1)}, bf16[64,4096]{1,0:T(8,128)(2,1)S(1)}) custom-call(bf16[4,528,1024]{2,1,0:T(8,128)(2,1)S(1)} %copy-done.2, f32[128,128]{1,0:T(8,128)S(1)} %get-tuple-element.33.lg_ref, bf16[4096,1024]{1,0:T(8,128)(2,1)} %bitcast.42, f32[1,4096]{1,0:T(1,128)S(1)} %get-tuple-element.59.router_ref), custom_call_target="tpu_custom_call" | custom-call | flops 1024 | bytes 1024 | tf_op jit(solution)/shard_map/back_rows/pallas_call | solution.py:194
  75.7 12.0 %hidden.5 = (bf16[4,528,1024]{2,1,0:T(8,128)(2,1)}, f32[128,128]{1,0:T(8,128)S(1)}) custom-call(f32[128,2]{1,0:T(8,128)S(1)} %get-tuple-element.36.meta_ref, bf16[16,4096]{1,0:T(8,128)(2,1)S(1)} %maximum_maximum_fusion.router_ref, bf16[256,4096]{1,0:T(8,128)(2,1)} %collective-permute-done.2.refs_0_, bf16[256,4096]{1,0:T(8,128)(2,1)S(1)} %collective-permute-done.3.refs_1_, ...), custom_call_target="tpu_custom_call" | custom-call | flops 1024 | bytes 1024 | tf_op jit(solution)/shard_map/hidden/pallas_call | solution.py:158
  87.7 5.3 %all-to-all-start.3 = ((bf16[4,528,1024]{2,1,0:T(8,128)(2,1)}), bf16[4,528,1024]{2,1,0:T(8,128)(2,1)}, u32[]{:S(2)}, u32[]{:S(2)}) async-start(bf16[4,528,1024]{2,1,0:T(8,128)(2,1)} %get-tuple-element.37.grad_ref), calls=%async_computation.3 | async-start | bytes 8650752 | tf_op jit(solution)/shard_map/all_to_all | solution.py:358
  93.0 16.6 %collective-permute-done.6 = bf16[256,4096]{1,0:T(8,128)(2,1)} collective-permute-done((bf16[256,4096]{1,0:T(8,128)(2,1)}, bf16[256,4096]{1,0:T(8,128)(2,1)}, u32[]{:S(2)}, u32[]{:S(2)}) %collective-permute-start.6) | collective-permute-done | bytes 2097184 | tf_op jit(solution)/shard_map/ppermute | solution.py:318
  112.0 5.7 %collective-permute-start.12 = (bf16[256,4096]{1,0:T(8,128)(2,1)}, bf16[256,4096]{1,0:T(8,128)(2,1)}, u32[]{:S(2)}, u32[]{:S(2)}) collective-permute-start(bf16[256,4096]{1,0:T(8,128)(2,1)} %collective-permute-done.6), channel_id=1, source_target_pairs={{2,0},{3,1},{4,6},{5,7},{10,8},{11,9},{12,14},{13,15},{18,16},{19,... | collective-permute-start | bytes 6291464 | tf_op jit(solution)/shard_map/ppermute | solution.py:318
  120.0 5.9 %back_rows.5 = (bf16[64,4096]{1,0:T(8,128)(2,1)S(1)}, bf16[64,4096]{1,0:T(8,128)(2,1)S(1)}) custom-call(bf16[4,528,1024]{2,1,0:T(8,128)(2,1)S(1)} %copy-done.1, f32[128,128]{1,0:T(8,128)S(1)} %get-tuple-element.38.lg_ref, bf16[4096,1024]{1,0:T(8,128)(2,1)} %bitcast.44, f32[1,4096]{1,0:T(1,128)S(1)} %get-tuple-element.59.router_ref), custom_call_target="tpu_custom_call" | custom-call | flops 1024 | bytes 1024 | tf_op jit(solution)/shard_map/back_rows/pallas_call | solution.py:194
  128.7 11.5 %hidden.6 = (bf16[4,528,1024]{2,1,0:T(8,128)(2,1)}, f32[128,128]{1,0:T(8,128)S(1)}) custom-call(f32[128,2]{1,0:T(8,128)S(1)} %get-tuple-element.41.meta_ref, bf16[16,4096]{1,0:T(8,128)(2,1)S(1)} %maximum_maximum_fusion.router_ref, bf16[256,4096]{1,0:T(8,128)(2,1)S(1)} %broadcast_select_fusion.1.refs_0_, ...), custom_call_target="tpu_custom_call" | custom-call | flops 1024 | bytes 1024 | tf_op jit(solution)/shard_map/hidden/pallas_call | solution.py:158
  141.1 6.3 %all-to-all-start.4 = ((bf16[4,528,1024]{2,1,0:T(8,128)(2,1)}), bf16[4,528,1024]{2,1,0:T(8,128)(2,1)}, u32[]{:S(2)}, u32[]{:S(2)}) async-start(bf16[4,528,1024]{2,1,0:T(8,128)(2,1)} %get-tuple-element.42.grad_ref), calls=%async_computation.4 | async-start | bytes 8650752 | tf_op jit(solution)/shard_map/all_to_all | solution.py:358
  147.4 14.9 %collective-permute-done.12 = bf16[256,4096]{1,0:T(8,128)(2,1)} collective-permute-done((bf16[256,4096]{1,0:T(8,128)(2,1)}, bf16[256,4096]{1,0:T(8,128)(2,1)}, u32[]{:S(2)}, u32[]{:S(2)}) %collective-permute-start.12) | collective-permute-done | bytes 2097184 | tf_op jit(solution)/shard_map/ppermute | solution.py:318
  166.4 5.9 %back_rows.6 = (bf16[64,4096]{1,0:T(8,128)(2,1)S(1)}, bf16[64,4096]{1,0:T(8,128)(2,1)S(1)}) custom-call(bf16[4,528,1024]{2,1,0:T(8,128)(2,1)S(1)} %copy-done, f32[128,128]{1,0:T(8,128)S(1)} %get-tuple-element.43.lg_ref, bf16[4096,1024]{1,0:T(8,128)(2,1)} %bitcast.46, f32[1,4096]{1,0:T(1,128)S(1)} %get-tuple-element.59.router_ref), custom_call_target="tpu_custom_call" | custom-call | flops 1024 | bytes 1024 | tf_op jit(solution)/shard_map/back_rows/pallas_call | solution.py:194
  172.8 2.5 collective-permute-start.5
  180.4 4.5 %pick_rows.1.refs_0_ = bf16[4,256,1024]{2,1,0:T(8,128)(2,1)} custom-call(f32[128,2]{1,0:T(8,128)S(1)} %get-tuple-element.46.meta_ref, bf16[256,4096]{1,0:T(8,128)(2,1)S(1)} %broadcast_select_fusion.near_ref, bf16[256,4096]{1,0:T(8,128)(2,1)} %copy-done.13), custom_call_target="tpu_custom_call" | custom-call | flops 1024 | bytes 1024 | tf_op jit(solution)/shard_map/pick_rows/pallas_call | solution.py:68
  184.9 9.4 %hidden.7 = (bf16[1,272,1024]{2,1,0:T(8,128)(2,1)S(1)}, f32[128,128]{1,0:T(8,128)S(1)}) custom-call(f32[128,2]{1,0:T(8,128)S(1)} %get-tuple-element.46.meta_ref, bf16[16,4096]{1,0:T(8,128)(2,1)S(1)} %maximum_maximum_fusion.router_ref, bf16[4,256,1024]{2,1,0:T(8,128)(2,1)} %pick_rows.1.refs_0_, bf16[4096,1024]{1,0:T(8,128)(2,1)} %bitcast.47, ...), custom_call_target="tpu_custom_call" | custom-call | flops 1024 | bytes 1024 | tf_op jit(solution)/shard_map/hidden/pallas_call | solution.py:158
  194.3 6.8 %back_rows.7 = (bf16[64,4096]{1,0:T(8,128)(2,1)S(1)}, bf16[64,4096]{1,0:T(8,128)(2,1)}) custom-call(bf16[1,272,1024]{2,1,0:T(8,128)(2,1)S(1)} %get-tuple-element.47.grad_ref.refs_1_, f32[128,128]{1,0:T(8,128)S(1)} %get-tuple-element.48.lg_ref, bf16[4096,1024]{1,0:T(8,128)(2,1)} %bitcast.48, f32[1,4096]{1,0:T(1,128)S(1)} %get-tuple-element.59.router_ref), custom_call_target="tpu_custom_call" | custom-call | flops 1024 | bytes 1024 | tf_op jit(solution)/shard_map/back_rows/pallas_call | solution.py:194
  202.0 4.2 %all-to-all-start.1 = ((bf16[4,256,1024]{2,1,0:T(8,128)(2,1)}), bf16[4,256,1024]{2,1,0:T(8,128)(2,1)S(1)}, u32[]{:S(2)}, u32[]{:S(2)}) async-start(bf16[4,256,1024]{2,1,0:T(8,128)(2,1)} %pick_rows.1.refs_0_), calls=%async_computation.1 | async-start | bytes 4194304 | tf_op jit(solution)/shard_map/all_to_all | solution.py:358
  206.2 2.3 pad_maximum_fusion.1
  208.5 10.0 %collective-permute-done.5.refs_1_ = bf16[128,4096]{1,0:T(8,128)(2,1)} collective-permute-done((bf16[128,4096]{1,0:T(8,128)(2,1)}, bf16[128,4096]{1,0:T(8,128)(2,1)}, u32[]{:S(2)}, u32[]{:S(2)}) %collective-permute-start.5) | collective-permute-done | bytes 1048608 | tf_op jit(solution)/shard_map/ppermute | solution.py:321
  218.4 6.5 %collective-permute-done.11.refs_2_ = bf16[128,4096]{1,0:T(8,128)(2,1)} collective-permute-done((bf16[128,4096]{1,0:T(8,128)(2,1)}, bf16[128,4096]{1,0:T(8,128)(2,1)}, u32[]{:S(2)}, u32[]{:S(2)}) %collective-permute-start.11) | collective-permute-done | bytes 1048608 | tf_op jit(solution)/shard_map/ppermute | solution.py:321
  226.0 2.4 collective-permute-start.18
  228.5 13.7 %weight_terms.2 = (f32[1024,1024]{1,0:T(8,128)S(1)}, f32[1024,1024]{1,0:T(8,128)}, f32[4,1024]{1,0:T(4,128)S(1)}) custom-call(s32[1]{0:T(128)} %bitcast.16.place_ref, bf16[4,528,1024]{2,1,0:T(8,128)(2,1)} %all-to-all-done.2.refs_0_.refs_1_, bf16[4,528,1024]{2,1,0:T(8,128)(2,1)} %all-to-all-done.2.refs_0_.refs_1_, ...), custom_call_target="tpu_custom_call" | custom-call | flops 10000000000 | bytes 1024 | tf_op jit(solution)/shard_map/weight_terms/pallas_call | solution.py:260
  245.0 9.2 %collective-permute-done.17.refs_3_ = bf16[1,272,1024]{2,1,0:T(8,128)(2,1)S(1)} collective-permute-done((bf16[1,272,1024]{2,1,0:T(8,128)(2,1)}, bf16[1,272,1024]{2,1,0:T(8,128)(2,1)S(1)}, u32[]{:S(2)}, u32[]{:S(2)}) %collective-permute-start.17) | collective-permute-done | bytes 557088 | tf_op jit(solution)/shard_map/ppermute | solution.py:370
  260.0 6.8 %weight_terms.3 = (bf16[1024,1024]{1,0:T(8,128)(2,1)}, bf16[1024,1024]{1,0:T(8,128)(2,1)}, f32[4,1024]{1,0:T(4,128)S(1)}) custom-call(s32[1]{0:T(128)} %bitcast.16.place_ref, bf16[4,256,1024]{2,1,0:T(8,128)(2,1)S(1)} %all-to-all-done.1.refs_0_, bf16[1,272,1024]{2,1,0:T(8,128)(2,1)S(1)} %copy-done.5, bf16[1,272,1024]{2,1,0:T(8,128)(2,1)S(1)} %copy-done.7, ...), custom_call_target="tpu_custom_call" | custom-call | flops 1024 | bytes 1024 | tf_op jit(solution)/shard_map/weight_terms/pallas_call | solution.py:260
  267.4 4.9 %collective-permute-done.15.refs_3_ = bf16[128,4096]{1,0:T(8,128)(2,1)} collective-permute-done((bf16[128,4096]{1,0:T(8,128)(2,1)}, bf16[128,4096]{1,0:T(8,128)(2,1)}, u32[]{:S(2)}, u32[]{:S(2)}) %collective-permute-start.15) | collective-permute-done | bytes 1048608 | tf_op jit(solution)/shard_map/ppermute | solution.py:321
  272.3 4.3 %combine.1 = bf16[128,4096]{1,0:T(8,128)(2,1)} custom-call(f32[1,512]{1,0:T(1,128)S(1)} %reshape.79.slots_ref, bf16[128,4096]{1,0:T(8,128)(2,1)S(1)} %constant_dynamic-update-slice_fusion.refs_0_, bf16[128,4096]{1,0:T(8,128)(2,1)} %collective-permute-done.5.refs_1_, bf16[128,4096]{1,0:T(8,128)(2,1)} %collective-permute-done.11.refs_2_, ...), custom_call_target="tpu_custom_call" | custom-call | flops 1024 | bytes 1024 | tf_op jit(solution)/shard_map/combine/pallas_call | solution.py:286
  (92 shorter events, 38.6 us)
Async XLA Ops:
  2.7 8.4 %all-to-all-start = ((f32[8,1,192]{2,1,0:T(1,128)}), f32[8,1,192]{2,1,0:T(1,128)S(1)}, u32[]{:S(2)}, u32[]{:S(2)}) async-start(f32[8,1,192]{2,1,0:T(1,128)} %all_to_all.20), calls=%async_computation | async-start | bytes 16384 | tf_op jit(solution)/shard_map/all_to_all | solution.py:326
  11.1 5.7 %collective-permute-start = (bf16[256,4096]{1,0:T(8,128)(2,1)S(1)}, bf16[256,4096]{1,0:T(8,128)(2,1)}, u32[]{:S(2)}, u32[]{:S(2)}) collective-permute-start(bf16[256,4096]{1,0:T(8,128)(2,1)S(1)} %pad_maximum_fusion.refs_0_), channel_id=1, source_target_pairs={{0,1},{1,0},{2,3},{3,2},{4,5},{5,4},{6,7},{7,6},{8,9},{9,8},{10,11... | collective-permute-start | bytes 6291464 | tf_op jit(solution)/shard_map/ppermute | solution.py:321
  11.2 48.2 %collective-permute-start.2 = (bf16[256,4096]{1,0:T(8,128)(2,1)S(1)}, bf16[256,4096]{1,0:T(8,128)(2,1)}, u32[]{:S(2)}, u32[]{:S(2)}) collective-permute-start(bf16[256,4096]{1,0:T(8,128)(2,1)S(1)} %pad_maximum_fusion.refs_0_), channel_id=1, source_target_pairs={{0,2},{1,3},{2,0},{3,1},{4,6},{5,7},{6,4},{7,5},{8,10},{9,11},{10,... | collective-permute-start | bytes 6291464 | tf_op jit(solution)/shard_map/ppermute | solution.py:318
  12.3 50.5 %collective-permute-start.7 = (bf16[256,4096]{1,0:T(8,128)(2,1)S(1)}, bf16[256,4096]{1,0:T(8,128)(2,1)}, u32[]{:S(2)}, u32[]{:S(2)}) collective-permute-start(bf16[256,4096]{1,0:T(8,128)(2,1)S(1)} %pad_maximum_fusion.refs_0_), channel_id=1, source_target_pairs={{2,4},{3,5},{4,2},{5,3},{10,12},{11,13},{12,10},{13,11},{18,20},{1... | collective-permute-start | bytes 6291464 | tf_op jit(solution)/shard_map/ppermute | solution.py:318
  28.8 58.9 %all-to-all-start.2 = ((bf16[4,528,1024]{2,1,0:T(8,128)(2,1)}), bf16[4,528,1024]{2,1,0:T(8,128)(2,1)}, u32[]{:S(2)}, u32[]{:S(2)}) async-start(bf16[4,528,1024]{2,1,0:T(8,128)(2,1)} %get-tuple-element.32.grad_ref), calls=%async_computation.2 | async-start | bytes 8650752 | tf_op jit(solution)/shard_map/all_to_all | solution.py:358
  59.4 16.3 %collective-permute-start.3 = (bf16[256,4096]{1,0:T(8,128)(2,1)}, bf16[256,4096]{1,0:T(8,128)(2,1)S(1)}, u32[]{:S(2)}, u32[]{:S(2)}) collective-permute-start(bf16[256,4096]{1,0:T(8,128)(2,1)} %collective-permute-done.2.refs_0_), channel_id=1, source_target_pairs={{0,1},{1,0},{2,3},{3,2},{4,5},{5,4},{6,7},{7,6},{8,9},{9,8},{10,11... | collective-permute-start | bytes 6291464 | tf_op jit(solution)/shard_map/ppermute | solution.py:321
  59.4 50.2 %collective-permute-start.6 = (bf16[256,4096]{1,0:T(8,128)(2,1)}, bf16[256,4096]{1,0:T(8,128)(2,1)}, u32[]{:S(2)}, u32[]{:S(2)}) collective-permute-start(bf16[256,4096]{1,0:T(8,128)(2,1)} %collective-permute-done.2.refs_0_), channel_id=1, source_target_pairs={{2,4},{3,5},{4,2},{5,3},{10,12},{11,13},{12,10},{13,11},{18,20},{1... | collective-permute-start | bytes 6291464 | tf_op jit(solution)/shard_map/ppermute | solution.py:318
  62.8 47.3 %collective-permute-start.8 = (bf16[256,4096]{1,0:T(8,128)(2,1)}, bf16[256,4096]{1,0:T(8,128)(2,1)}, u32[]{:S(2)}, u32[]{:S(2)}) collective-permute-start(bf16[256,4096]{1,0:T(8,128)(2,1)} %collective-permute-done.7), channel_id=1, source_target_pairs={{2,0},{3,1},{4,6},{5,7},{10,8},{11,9},{12,14},{13,15},{18,16},{19,... | collective-permute-start | bytes 6291464 | tf_op jit(solution)/shard_map/ppermute | solution.py:318
  65.6 2.2 copy-start.2
  73.7 2.0 collective-permute-start.1
  87.7 53.4 %all-to-all-start.3 = ((bf16[4,528,1024]{2,1,0:T(8,128)(2,1)}), bf16[4,528,1024]{2,1,0:T(8,128)(2,1)}, u32[]{:S(2)}, u32[]{:S(2)}) async-start(bf16[4,528,1024]{2,1,0:T(8,128)(2,1)} %get-tuple-element.37.grad_ref), calls=%async_computation.3 | async-start | bytes 8650752 | tf_op jit(solution)/shard_map/all_to_all | solution.py:358
  111.9 16.7 %collective-permute-start.9 = (bf16[256,4096]{1,0:T(8,128)(2,1)S(1)}, bf16[256,4096]{1,0:T(8,128)(2,1)S(1)}, u32[]{:S(2)}, u32[]{:S(2)}) collective-permute-start(bf16[256,4096]{1,0:T(8,128)(2,1)S(1)} %broadcast_select_fusion.1.refs_0_), channel_id=1, source_target_pairs={{0,1},{1,0},{2,3},{3,2},{4,5},{5,4},{6,7},{7,6},{8,9},{9,8},{10,11... | collective-permute-start | bytes 6291464 | tf_op jit(solution)/shard_map/ppermute | solution.py:321
  112.0 50.2 %collective-permute-start.12 = (bf16[256,4096]{1,0:T(8,128)(2,1)}, bf16[256,4096]{1,0:T(8,128)(2,1)}, u32[]{:S(2)}, u32[]{:S(2)}) collective-permute-start(bf16[256,4096]{1,0:T(8,128)(2,1)} %collective-permute-done.6), channel_id=1, source_target_pairs={{2,0},{3,1},{4,6},{5,7},{10,8},{11,9},{12,14},{13,15},{18,16},{19,... | collective-permute-start | bytes 6291464 | tf_op jit(solution)/shard_map/ppermute | solution.py:318
  117.7 2.2 copy-start.1
  125.9 2.0 collective-permute-start.4
  141.1 60.9 %all-to-all-start.4 = ((bf16[4,528,1024]{2,1,0:T(8,128)(2,1)}), bf16[4,528,1024]{2,1,0:T(8,128)(2,1)}, u32[]{:S(2)}, u32[]{:S(2)}) async-start(bf16[4,528,1024]{2,1,0:T(8,128)(2,1)} %get-tuple-element.42.grad_ref), calls=%async_computation.4 | async-start | bytes 8650752 | tf_op jit(solution)/shard_map/all_to_all | solution.py:358
  164.1 15.1 %collective-permute-start.13 = (bf16[256,4096]{1,0:T(8,128)(2,1)S(1)}, bf16[256,4096]{1,0:T(8,128)(2,1)S(1)}, u32[]{:S(2)}, u32[]{:S(2)}) collective-permute-start(bf16[256,4096]{1,0:T(8,128)(2,1)S(1)} %broadcast_select_fusion.near_ref), channel_id=1, source_target_pairs={{0,1},{1,0},{2,3},{3,2},{4,5},{5,4},{6,7},{7,6},{8,9},{9,8},{10,11... | collective-permute-start | bytes 6291464 | tf_op jit(solution)/shard_map/ppermute | solution.py:321
  164.1 2.2 copy-start
  172.2 3.9 %collective-permute-start.10 = (bf16[64,4096]{1,0:T(8,128)(2,1)S(1)}, bf16[64,4096]{1,0:T(8,128)(2,1)S(1)}, u32[]{:S(2)}, u32[]{:S(2)}) collective-permute-start(bf16[64,4096]{1,0:T(8,128)(2,1)S(1)} %get-tuple-element.45), channel_id=1, source_target_pairs={{0,1},{1,0},{2,3},{3,2},{4,5},{5,4},{6,7},{7,6},{8,9},{9,8},{10,11... | collective-permute-start | bytes 1572872 | tf_op jit(solution)/shard_map/ppermute | solution.py:321
  172.8 45.6 %collective-permute-start.5 = (bf16[128,4096]{1,0:T(8,128)(2,1)}, bf16[128,4096]{1,0:T(8,128)(2,1)}, u32[]{:S(2)}, u32[]{:S(2)}) collective-permute-start(bf16[128,4096]{1,0:T(8,128)(2,1)} %constant_dynamic-update-slice_fusion.2), channel_id=1, source_target_pairs={{0,2},{1,3},{2,0},{3,1},{4,6},{5,7},{6,4},{7,5},{8,10},{9,11},{10,... | collective-permute-start | bytes 3145736 | tf_op jit(solution)/shard_map/ppermute | solution.py:321
  176.9 47.9 %collective-permute-start.11 = (bf16[128,4096]{1,0:T(8,128)(2,1)}, bf16[128,4096]{1,0:T(8,128)(2,1)}, u32[]{:S(2)}, u32[]{:S(2)}) collective-permute-start(bf16[128,4096]{1,0:T(8,128)(2,1)} %constant_dynamic-update-slice_fusion.4), channel_id=1, source_target_pairs={{0,4},{1,5},{2,6},{3,7},{4,0},{5,1},{6,2},{7,3},{8,12},{9,13},{10,... | collective-permute-start | bytes 3145736 | tf_op jit(solution)/shard_map/ppermute | solution.py:321
  179.1 1.3 copy-start.13
  194.3 6.8 %copy-start.4 = (bf16[1,272,1024]{2,1,0:T(8,128)(2,1)}, bf16[1,272,1024]{2,1,0:T(8,128)(2,1)S(1)}, u32[]{:S(2)}) copy-start(bf16[1,272,1024]{2,1,0:T(8,128)(2,1)S(1)} %get-tuple-element.47.grad_ref.refs_1_) | copy-start | bytes 1671172
  201.9 4.3 %collective-permute-start.14 = (bf16[64,4096]{1,0:T(8,128)(2,1)}, bf16[64,4096]{1,0:T(8,128)(2,1)}, u32[]{:S(2)}, u32[]{:S(2)}) collective-permute-start(bf16[64,4096]{1,0:T(8,128)(2,1)} %get-tuple-element.50), channel_id=1, source_target_pairs={{0,1},{1,0},{2,3},{3,2},{4,5},{5,4},{6,7},{7,6},{8,9},{9,8},{10,11... | collective-permute-start | bytes 1572872 | tf_op jit(solution)/shard_map/ppermute | solution.py:321
  202.0 53.8 %all-to-all-start.1 = ((bf16[4,256,1024]{2,1,0:T(8,128)(2,1)}), bf16[4,256,1024]{2,1,0:T(8,128)(2,1)S(1)}, u32[]{:S(2)}, u32[]{:S(2)}) async-start(bf16[4,256,1024]{2,1,0:T(8,128)(2,1)} %pick_rows.1.refs_0_), calls=%async_computation.1 | async-start | bytes 4194304 | tf_op jit(solution)/shard_map/all_to_all | solution.py:358
  224.9 47.4 %collective-permute-start.15 = (bf16[128,4096]{1,0:T(8,128)(2,1)}, bf16[128,4096]{1,0:T(8,128)(2,1)}, u32[]{:S(2)}, u32[]{:S(2)}) collective-permute-start(bf16[128,4096]{1,0:T(8,128)(2,1)} %pad_maximum_fusion.1), channel_id=1, source_target_pairs={{0,6},{1,7},{2,4},{3,5},{4,2},{5,3},{6,0},{7,1},{8,14},{9,15},{10,... | collective-permute-start | bytes 3145736 | tf_op jit(solution)/shard_map/ppermute | solution.py:321
  225.0 19.2 %collective-permute-start.16 = (bf16[1,272,1024]{2,1,0:T(8,128)(2,1)}, bf16[1,272,1024]{2,1,0:T(8,128)(2,1)S(1)}, u32[]{:S(2)}, u32[]{:S(2)}) collective-permute-start(bf16[1,272,1024]{2,1,0:T(8,128)(2,1)} %copy-done.4), channel_id=1, source_target_pairs={{0,8},{8,0},{16,24},{24,16},{1,9},{9,1},{17,25},{25,17},{2,10},{10... | collective-permute-start | bytes 1671176 | tf_op jit(solution)/shard_map/ppermute | solution.py:370
  225.5 28.6 %collective-permute-start.17 = (bf16[1,272,1024]{2,1,0:T(8,128)(2,1)}, bf16[1,272,1024]{2,1,0:T(8,128)(2,1)S(1)}, u32[]{:S(2)}, u32[]{:S(2)}) collective-permute-start(bf16[1,272,1024]{2,1,0:T(8,128)(2,1)} %copy-done.4), channel_id=1, source_target_pairs={{0,16},{8,24},{16,0},{24,8},{1,17},{9,25},{17,1},{25,9},{2,18},{10... | collective-permute-start | bytes 1671176 | tf_op jit(solution)/shard_map/ppermute | solution.py:370
  226.0 29.0 %collective-permute-start.18 = (bf16[1,272,1024]{2,1,0:T(8,128)(2,1)}, bf16[1,272,1024]{2,1,0:T(8,128)(2,1)S(1)}, u32[]{:S(2)}, u32[]{:S(2)}) collective-permute-start(bf16[1,272,1024]{2,1,0:T(8,128)(2,1)} %copy-done.4), channel_id=1, source_target_pairs={{0,24},{8,16},{16,8},{24,0},{1,25},{9,17},{17,9},{25,1},{2,26},{10... | collective-permute-start | bytes 1671176 | tf_op jit(solution)/shard_map/ppermute | solution.py:370
  242.2 2.0 copy-start.3
  255.8 1.1 copy-start.5
  256.9 1.1 copy-start.7
  (6 other events, 5.4 us)

commit v3 on v2

--- a/solution.py
+++ b/solution.py
@@ -7,8 +7,8 @@
 from jax.experimental.pallas import tpu as pltpu
 from jax.sharding import PartitionSpec as P
 
-SPLIT = True
-VMEM_LIMIT = 48 * 1024 * 1024
+STRIP = 1024
+VMEM_LIMIT = 56 * 1024 * 1024
 SMALL = pl.CostEstimate(flops=1024, bytes_accessed=1024, transcendentals=0)
 
 
@@ -52,62 +52,51 @@
     return jnp.concatenate([top, bottom], axis=0).astype(jnp.bfloat16)
 
 
-def pick_kernel(meta_ref, near_ref, far_ref, out_ref):
+def expert_kernel(apart, steps, place_ref, meta_ref, router_ref, *refs):
+    sources, (up_ref, down_ref, row_ref), messages = refs[:2], refs[2:5], refs[5:-8]
+    near_ref, far_ref, pre, back, logit, held, held_up, lgs = refs[-8:]
+    step = pl.program_id(0)
     rows = meta_ref.shape[0]
-    tok_rows = near_ref.shape[0] // 2
-    picks = picks_of(meta_ref, tok_rows)
-    out_ref[0, :rows] = pick(picks, near_ref, far_ref, 0)
-    out_ref[0, rows:] = pick(picks, near_ref, far_ref, tok_rows)
-
-
-def pick_rows(meta, near, far, dp):
-    rows = meta.shape[0]
-    both_rows, width = near.shape
-    piece = width // dp
-    block = pl.BlockSpec((both_rows, piece), lambda k: (0, k))
-    return pl.pallas_call(
-        pick_kernel,
-        grid=(dp,),
-        in_specs=[pl.BlockSpec(meta.shape, lambda k: (0, 0)), block, block],
-        out_specs=pl.BlockSpec((1, 2 * rows, piece), lambda k: (k, 0, 0)),
-        out_shape=jax.ShapeDtypeStruct((dp, 2 * rows, piece), jnp.bfloat16),
-        compiler_params=pltpu.CompilerParams(vmem_limit_bytes=VMEM_LIMIT),
-        cost_estimate=SMALL,
-        name="pick_rows",
-    )(meta, near, far)
-
-
-def hidden_kernel(ready, meta_ref, router_ref, *refs):
-    sources, refs = (refs[:1], refs[1:]) if ready else (refs[:2], refs[2:])
-    up_ref, down_ref, message_ref, lg_ref, pre, back, logit, held = refs
-    step = pl.program_id(0)
-    steps = pl.num_programs(0)
-    rows = meta_ref.shape[0]
+    half = rows // 2
     trailing = (((1,), (1,)), ((), ()))
-    if ready:
-        x, g = sources[0][0, :rows], sources[0][0, rows:]
-    else:
-        tok_rows = sources[0].shape[0] // 2
+    tok_rows = sources[0].shape[0] // 2
+    dp, _, piece = held.shape
+    strip = up_ref.shape[0]
+    per_piece = piece // strip
+
+    @pl.when(step < steps)
+    def _():
         picks = picks_of(meta_ref, tok_rows)
         x, g = pick(picks, *sources, 0), pick(picks, *sources, tok_rows)
-        message_ref[step, :rows] = x
-        message_ref[step, rows : 2 * rows] = g
-    held[step] = x
-    pre_term = jnp.dot(x, up_ref[...], preferred_element_type=jnp.float32)
-    back_term = jnp.dot(g, down_ref[...], preferred_element_type=jnp.float32)
-    logit_term = lax.dot_general(x, router_ref[...], trailing, preferred_element_type=jnp.float32)
-
-    @pl.when(step == 0)
-    def _():
-        pre[...] = pre_term
-        back[...] = back_term
-        logit[...] = logit_term
-
-    @pl.when(step > 0)
-    def _():
-        pre[...] += pre_term
-        back[...] += back_term
-        logit[...] += logit_term
+        shard = step // per_piece
+        lanes = pl.ds(pl.multiple_of(step % per_piece * strip, strip), strip)
+        if apart:
+            for k, message_ref in enumerate(messages):
+
+                @pl.when(shard ^ place_ref[0] == k)
+                def _():
+                    message_ref[0, :rows, lanes] = x
+                    message_ref[0, rows : 2 * rows, lanes] = g
+        else:
+            messages[0][shard, :rows, lanes] = x
+            messages[0][shard, rows : 2 * rows, lanes] = g
+        held[shard, :, lanes] = x
+        held_up[step] = up_ref[...]
+        pre_term = jnp.dot(x, up_ref[...], preferred_element_type=jnp.float32)
+        back_term = jnp.dot(g, down_ref[...], preferred_element_type=jnp.float32)
+        logit_term = lax.dot_general(x, router_ref[...], trailing, preferred_element_type=jnp.float32)
+
+        @pl.when(step == 0)
+        def _():
+            pre[...] = pre_term
+            back[...] = back_term
+            logit[...] = logit_term
+
+        @pl.when(step > 0)
+        def _():
+            pre[...] += pre_term
+            back[...] += back_term
+            logit[...] += logit_term
 
     @pl.when(step == steps - 1)
     def _():
@@ -119,14 +108,14 @@
         pre_grad = (weight * grad * slope).astype(jnp.bfloat16)
         scaled = (weight * active).astype(jnp.bfloat16)
         lg = score * weight * (1.0 - gate)
-        lg_ref[...] = jnp.broadcast_to(lg, lg_ref.shape)
+        lgs[...] = jnp.broadcast_to(lg, lgs.shape)
         flat = jnp.transpose(jnp.broadcast_to(lg, (rows, rows)))[:8]
         high = flat.astype(jnp.bfloat16)
         rest = flat - high.astype(jnp.float32)
         middle = rest.astype(jnp.bfloat16)
         low = (rest - middle.astype(jnp.float32)).astype(jnp.bfloat16)
         columns = []
-        for k in range(held.shape[0]):
+        for k in range(dp):
             terms = [jnp.dot(part, held[k], preferred_element_type=jnp.float32) for part in (high, middle, low)]
             columns.append((terms[0] + terms[1] + terms[2])[0:1])
         column = jnp.concatenate(columns, axis=0)
@@ -136,91 +125,74 @@
         extra = jnp.concatenate(
             [first.astype(jnp.float32), second.astype(jnp.float32), empty], axis=0
         ).astype(jnp.bfloat16)
-        base = 0 if ready else 2 * rows
-        for k in range(message_ref.shape[0]):
-            message_ref[k, base : base + rows] = pre_grad
-            message_ref[k, base + rows : base + 2 * rows] = scaled
-            message_ref[k, base + 2 * rows :] = extra
-
-
-def hidden(meta, router, sources, w_up, w_down, dp):
+        for k in range(dp):
+            message_ref = messages[k].at[0] if apart else messages[0].at[k]
+            message_ref[2 * rows : 3 * rows] = pre_grad
+            message_ref[3 * rows : 4 * rows] = scaled
+            message_ref[4 * rows :] = extra
+
+    @pl.when(step >= steps)
+    def _():
+        pre_grad = messages[0][0, 2 * rows : 3 * rows]
+        out = lax.dot_general(pre_grad, held_up[step - steps], trailing, preferred_element_type=jnp.float32)
+        out = (out + lgs[:, 0:1] * row_ref[...]).astype(jnp.bfloat16)
+        near_ref[...] = out[:half]
+        far_ref[...] = out[half:]
+
+
+def expert_rows(place, meta, router, router_row, near, far, w_up, w_down, dp, apart):
     rows = meta.shape[0]
     width, hid = w_up.shape
     piece = width // dp
-    ready = len(sources) == 1
-    shape = (1, 2 * rows + EXTRA, piece) if ready else (dp, 4 * rows + EXTRA, piece)
-    weight = pl.BlockSpec((piece, hid), lambda k: (k, 0))
-    whole = lambda shape: pl.BlockSpec(shape, lambda k: (0,) * len(shape))
-    if ready:
-        blocks = [pl.BlockSpec((1, 2 * rows, piece), lambda k: (k, 0, 0))]
-    else:
-        blocks = [pl.BlockSpec((sources[0].shape[0], piece), lambda k: (0, k))] * 2
+    strip = STRIP if piece % STRIP == 0 else piece
+    steps = width // strip
+    held = 4 * rows + EXTRA
+    shapes = [(1, held, piece)] * dp if apart else [(dp, held, piece)]
+    first = lambda k: jnp.minimum(k, steps - 1)
+    second = lambda k: jnp.maximum(k - steps, 0)
+    weight = pl.BlockSpec((strip, hid), lambda k, place: (first(k), 0))
+    block = pl.BlockSpec((near.shape[0], strip), lambda k, place: (0, first(k)))
+    back = pl.BlockSpec((rows // 2, strip), lambda k, place: (0, second(k)))
+    whole = lambda shape: pl.BlockSpec(shape, lambda k, place: (0,) * len(shape))
     return pl.pallas_call(
-        functools.partial(hidden_kernel, ready),
-        grid=(dp,),
-        in_specs=[whole(meta.shape), pl.BlockSpec((router.shape[0], piece), lambda k: (0, k))]
-        + blocks
-        + [weight, weight],
-        out_specs=[whole(shape), whole((rows, 128))],
-        out_shape=[
-            jax.ShapeDtypeStruct(shape, jnp.bfloat16),
-            jax.ShapeDtypeStruct((rows, 128), jnp.float32),
-        ],
-        scratch_shapes=[pltpu.VMEM((rows, hid), jnp.float32)] * 2
-        + [pltpu.VMEM((rows, router.shape[0]), jnp.float32), pltpu.VMEM((dp, rows, piece), jnp.bfloat16)],
+        functools.partial(expert_kernel, apart, steps),
+        grid_spec=pltpu.PrefetchScalarGridSpec(
+            num_scalar_prefetch=1,
+            grid=(2 * steps,),
+            in_specs=[
+                whole(meta.shape),
+                pl.BlockSpec((router.shape[0], strip), lambda k, place: (0, first(k))),
+                block, block, weight, weight,
+                pl.BlockSpec((1, strip), lambda k, place: (0, second(k))),
+            ],
+            out_specs=[whole(shape) for shape in shapes] + [back, back],
+            scratch_shapes=[
+                pltpu.VMEM((rows, hid), jnp.float32),
+                pltpu.VMEM((rows, hid), jnp.float32),
+                pltpu.VMEM((rows, router.shape[0]), jnp.float32),
+                pltpu.VMEM((dp, rows, piece), jnp.bfloat16),
+                pltpu.VMEM((steps, strip, hid), jnp.bfloat16),
+                pltpu.VMEM((rows, 128), jnp.float32),
+            ],
+        ),
+        out_shape=[jax.ShapeDtypeStruct(shape, jnp.bfloat16) for shape in shapes + [(rows // 2, width)] * 2],
         compiler_params=pltpu.CompilerParams(vmem_limit_bytes=VMEM_LIMIT),
         cost_estimate=SMALL,
-        name="hidden",
-    )(meta, router, *sources, w_up, w_down)
-
-
-def rows_kernel(grad_ref, lg_ref, up_ref, router_ref, near_ref, far_ref):
-    rows = lg_ref.shape[0]
-    half = rows // 2
-    trailing = (((1,), (1,)), ((), ()))
-    out = lax.dot_general(grad_ref[...].reshape(rows, -1), up_ref[...], trailing, preferred_element_type=jnp.float32)
-    out = (out + lg_ref[:, 0:1] * router_ref[...]).astype(jnp.bfloat16)
-    near_ref[...] = out[:half]
-    far_ref[...] = out[half:]
-
-
-def back_rows(message, lg, w_up, router_row, steps):
-    first = 0 if message.shape[0] == 1 else 2
-    rows = lg.shape[0]
-    width, hid = w_up.shape
-    piece = width // steps
-    whole = lambda shape: pl.BlockSpec(shape, lambda k: (0, 0))
-    half = pl.BlockSpec((rows // 2, piece), lambda k: (0, k))
-    return pl.pallas_call(
-        rows_kernel,
-        grid=(steps,),
-        in_specs=[
-            pl.BlockSpec((1, rows, hid), lambda k: (0, first, 0)),
-            whole(lg.shape),
-            pl.BlockSpec((piece, hid), lambda k: (k, 0)),
-            pl.BlockSpec((1, piece), lambda k: (0, k)),
-        ],
-        out_specs=[half, half],
-        out_shape=[jax.ShapeDtypeStruct((rows // 2, width), jnp.bfloat16)] * 2,
-        compiler_params=pltpu.CompilerParams(vmem_limit_bytes=VMEM_LIMIT),
-        cost_estimate=SMALL,
-        name="back_rows",
-    )(message, lg, w_up, router_row)
-
-
-def weights_kernel(sizes, has_start, place_ref, *refs):
+        name="expert_rows",
+    )(place, meta, router, near, far, w_up, w_down, router_row)
+
+
+def weights_kernel(sizes, has_start, *refs):
     refs = list(refs)
     chunks = []
     for size in sizes:
-        left = refs.pop(0)
-        dp, double = left.shape[:2]
-        rows = double // 2
+        lefts = [refs.pop(0) for _ in range(size)]
         rights = [refs.pop(0) for _ in range(size)]
-        if size == 1:
-            pairs = [(left.at[k], rights[0].at[k], 2 * rows) for k in range(dp)]
-        else:
-            pairs = [(left.at[place_ref[0] ^ k], rights[k].at[0], 0) for k in range(dp)]
-        chunks.append(pairs)
+        rows = lefts[0].shape[1] // 2
+        chunks.append(
+            [(left.at[k], right.at[k]) for left, right in zip(lefts, rights) for k in range(left.shape[0])]
+        )
+    dp = len(chunks[0])
     start = [refs.pop(0) for _ in range(3)] if has_start else None
     outs = refs
     contract = (((0,), (0,)), ((), ()))
@@ -228,46 +200,47 @@
         total = start[which][...] if has_start else None
         low = which * rows
         for pairs in chunks:
-            left = jnp.concatenate([ref[low : low + rows] for ref, _, _ in pairs], axis=0)
-            right = jnp.concatenate([ref[base + low : base + low + rows] for _, ref, base in pairs], axis=0)
+            left = jnp.concatenate([ref[low : low + rows] for ref, _ in pairs], axis=0)
+            right = jnp.concatenate(
+                [ref[2 * rows + low : 3 * rows + low] for _, ref in pairs], axis=0
+            )
             term = lax.dot_general(left, right, contract, preferred_element_type=jnp.float32)
             total = term if total is None else total + term
         outs[which][...] = total.astype(outs[which].dtype)
     column = start[2][...] if has_start else jnp.zeros(outs[2].shape, jnp.float32)
     for pairs in chunks:
-        for _, ref, base in pairs:
-            both = ref[base + 2 * rows :].astype(jnp.float32)
+        for _, ref in pairs:
+            both = ref[4 * rows :].astype(jnp.float32)
             column = column + both[:dp] + both[dp : 2 * dp]
     outs[2][...] = column
 
 
-def weight_terms(place, chunks, rows, start, last):
-    dp, _, piece = chunks[0][0].shape
+def weight_terms(chunks, rows, start, last):
+    dp = sum(block.shape[0] for block in chunks[0])
+    piece = chunks[0][0].shape[2]
     tile = min(piece, 256)
     kind = jnp.bfloat16 if last else jnp.float32
-    strip = pl.BlockSpec((tile, piece), lambda i, place: (i, 0))
-    column = pl.BlockSpec((dp, piece), lambda i, place: (0, 0))
+    strip = pl.BlockSpec((tile, piece), lambda i: (i, 0))
+    column = pl.BlockSpec((dp, piece), lambda i: (0, 0))
     specs, arrays = [], []
     for blocks in chunks:
-        rights = blocks if len(blocks) == 1 else blocks[1:]
-        specs.append(pl.BlockSpec((dp, 2 * rows, tile), lambda i, place: (0, 0, i)))
-        specs += [pl.BlockSpec(block.shape, lambda i, place: (0, 0, 0)) for block in rights]
-        arrays += [blocks[0], *rights]
+        specs += [pl.BlockSpec((block.shape[0], 2 * rows, tile), lambda i: (0, 0, i)) for block in blocks]
+        specs += [pl.BlockSpec(block.shape, lambda i: (0, 0, 0)) for block in blocks]
+        arrays += list(blocks) * 2
     if start is not None:
         specs += [strip, strip, column]
         arrays += list(start)
-    sizes = [1 if len(blocks) == 1 else len(blocks) - 1 for blocks in chunks]
     return pl.pallas_call(
-        functools.partial(weights_kernel, sizes, start is not None),
-        grid_spec=pltpu.PrefetchScalarGridSpec(
-            num_scalar_prefetch=1, grid=(piece // tile,), in_specs=specs, out_specs=[strip, strip, column]
-        ),
+        functools.partial(weights_kernel, [len(blocks) for blocks in chunks], start is not None),
+        grid=(piece // tile,),
+        in_specs=specs,
+        out_specs=[strip, strip, column],
         out_shape=[jax.ShapeDtypeStruct((piece, piece), kind)] * 2
         + [jax.ShapeDtypeStruct((dp, piece), jnp.float32)],
         compiler_params=pltpu.CompilerParams(vmem_limit_bytes=VMEM_LIMIT),
         cost_estimate=SMALL if last else LARGE,
         name="weight_terms",
-    )(place, *arrays)
+    )(*arrays)
 
 
 def combine_kernel(slots_ref, *refs):
@@ -357,21 +330,16 @@
     def exchange(block):
         return lax.all_to_all(block, "dp", 0, 0, tiled=True)
 
-    def chunk(j, pair, before, split=False):
+    def chunk(j, pair, before, apart=False):
         near_block = settle(pair)
         far_block = across(near_block, 1)
-        meta = lax.dynamic_index_in_dim(metas, order[j], 0, False)
-        meta = after(meta, *before)
-        if split:
-            rows = pick_rows(meta, near_block, far_block, dp)
-            message, lg = hidden(meta, router, (rows,), w_up, w_down, dp)
-            got = [exchange(rows), message]
-            for k in range(1, dp):
-                got.append(lax.ppermute(message, "dp", [(q, q ^ k) for q in range(dp)]))
-        else:
-            message, lg = hidden(meta, router, (near_block, far_block), w_up, w_down, dp)
-            got = [exchange(message)]
-        near, far = back_rows(message, lg, w_up, router_row, dp)
+        meta = after(lax.dynamic_index_in_dim(metas, order[j], 0, False), *before)
+        *messages, near, far = expert_rows(
+            place, meta, router, router_row, near_block, far_block, w_up, w_down, dp, apart
+        )
+        got = messages[:1] if apart else [exchange(messages[0])]
+        for k in range(1, len(messages)):
+            got.append(lax.ppermute(messages[k], "dp", [(q, q ^ k) for q in range(dp)]))
         return got, jnp.concatenate([near, across(far, 1)], axis=0)
 
     got0, back0 = chunk(0, own, ())
@@ -379,13 +347,13 @@
     got1, back1 = chunk(1, one, (back0,))
     out_three = between(inside_two, outward)
     got2, back2 = chunk(2, (inside_two, out_two), (back1,))
-    got3, back3 = chunk(3, (inside, out_three), (back2,), split=SPLIT)
+    got3, back3 = chunk(3, (inside, out_three), (back2,), apart=True)
     back1, back2 = across(back1, 2), across(back2, 4)
     back3 = across(after(back3, back1, back2), 6)
     rows = 2 * per_slot
-    early = weight_terms(place, [got0, got1, got2], rows, None, False)
+    early = weight_terms([got0, got1, got2], rows, None, False)
     blocks = [back0, back1, back2, back3]
-    up_sum, down_sum, column = weight_terms(place, [got3], rows, early, True)
+    up_sum, down_sum, column = weight_terms([got3], rows, early, True)
     tokens_grad = combine(mine.reshape(1, -1), blocks, tok_rows)
     return (tokens_grad, up_sum[None], down_sum[None], column.reshape(-1, 1))
 

time: 278 us -> 269 us (0.968)
  waiting for transfers between devices: 91.7 us -> 103 us
  starting transfers between devices: 52.6 us -> 43.1 us
  local copies, waits for them, and re-layouts: 22.6 us -> 14.9 us
  Pallas kernels: 98.5 us -> 95.2 us
    ppermute x11, waiting for transfers between devices: 23.8 us -> 36.2 us  [across(): lax.ppermute(block, 'expert', [(e, e ^ mask) for e in range(experts)])]
    ppermute x5, waiting for transfers between devices: 57.1 us -> 47.3 us  [between(): return lax.ppermute(block, 'expert', pairs)]
    unnamed x33 -> x39, local copies, waits for them, and re-layouts: 19.8 us -> 9.96 us
    all_to_all x4 -> x3, waiting for transfers between devices: 0.88 us -> 8.07 us  [exchange(): return lax.all_to_all(block, 'dp', 0, 0, tiled=True)]
    ppermute x5, starting transfers between devices: 16.7 us -> 12.8 us  [between(): return lax.ppermute(block, 'expert', pairs)]
    pallas_call x11 -> x6, Pallas kernels: 94.2 us -> 90.6 us  [the longest x4 68.2 us: expert_rows(): pl.pallas_call(functools.partial(expert_kernel, apart, steps), grid_spec=...]
    all_to_all x4 -> x3, starting transfers between devices: 21.2 us -> 18.2 us  [exchange(): return lax.all_to_all(block, 'dp', 0, 0, tiled=True)]
  transfers between devices with their start and end apart: 24 -> 23, of which waited for: 12 -> 15; matrix products, arithmetic and copies ran while one was open for 5% -> 7% of each run, Pallas kernels for 34% -> 34%
where the time goes in v3:
time: 269 us; the launch traced here: 268 us
  waiting for transfers between devices  103 us (38%)
  Pallas kernels  95.2 us (35%)
  starting transfers between devices  43.1 us (16%)
  local copies, waits for them, and re-layouts  14.9 us (6%)
  other arithmetic  11.1 us (4%)
    pallas_call x4, Pallas kernels, expert_rows(): pl.pallas_call(functools.partial(expert_kernel, apart, steps), grid_spec=...  68.2 us
    ppermute x5, waiting for transfers between devices, between(): return lax.ppermute(block, 'expert', pairs)  47.3 us
    ppermute x11, waiting for transfers between devices, across(): lax.ppermute(block, 'expert', [(e, e ^ mask) for e in range(experts)])  36.2 us
    pallas_call x2, Pallas kernels, weight_terms(): pl.pallas_call(functools.partial(weights_kernel, [len(blocks) for blocks...  22.3 us
    all_to_all x3, starting transfers between devices, exchange(): return lax.all_to_all(block, 'dp', 0, 0, tiled=True)  18.2 us
    ppermute x5, starting transfers between devices, between(): return lax.ppermute(block, 'expert', pairs)  12.8 us
    ppermute x3, waiting for transfers between devices, chunk(): got.append(lax.ppermute(messages[k], 'dp', [(q, q ^ k) for q in range(dp)]))  10.5 us
    unnamed x39, local copies, waits for them, and re-layouts  9.96 us
  transfers between devices with their start and end apart: 23, of which 15 were waited for; matrix products, arithmetic and copies ran while one was open for 7% of the time, Pallas kernels for 34%

profile of v3, /device:TPU:22, one launch (start us, length us, event | category | flops | bytes accessed | tf_op | source)
XLA Modules:
  0.0 267.8 jit_solution(15191415777019775190)
XLA Ops:
  2.7 5.2 %all-to-all-start = ((f32[8,1,192]{2,1,0:T(1,128)}), f32[8,1,192]{2,1,0:T(1,128)S(1)}, u32[]{:S(2)}, u32[]{:S(2)}) async-start(f32[8,1,192]{2,1,0:T(1,128)} %all_to_all.17), calls=%async_computation | async-start | bytes 16384 | tf_op jit(solution)/shard_map/all_to_all | solution.py:299
  7.9 1.7 pad_maximum_fusion.refs_0_
  12.5 3.6 %collective-permute-start.7 = (bf16[256,4096]{1,0:T(8,128)(2,1)S(1)}, bf16[256,4096]{1,0:T(8,128)(2,1)}, u32[]{:S(2)}, u32[]{:S(2)}) collective-permute-start(bf16[256,4096]{1,0:T(8,128)(2,1)S(1)} %pad_maximum_fusion.refs_0_), channel_id=1, source_target_pairs={{2,4},{3,5},{4,2},{5,3},{10,12},{11,13},{12,10},{13,11},{18,20},{1... | collective-permute-start | bytes 6291464 | tf_op jit(solution)/shard_map/ppermute | solution.py:291
  18.1 16.9 %expert_rows.4 = (bf16[4,528,1024]{2,1,0:T(8,128)(2,1)}, bf16[64,4096]{1,0:T(8,128)(2,1)}, bf16[64,4096]{1,0:T(8,128)(2,1)}) custom-call(s32[1]{0:T(128)} %bitcast.5.place_ref, f32[128,2]{1,0:T(8,128)} %get-tuple-element.61.meta_ref, bf16[16,4096]{1,0:T(8,128)(2,1)} %maximum_maximum_fusion.router_ref, bf16[256,4096]{1,0:T(8,128)(2,1)} %copy-done.2, ...), custom_call_target="tpu_custom_call" | custom-call | flops 1024 | bytes 1024 | tf_op jit(solution)/shard_map/expert_rows/pallas_call | solution.py:157
  35.1 5.5 %all-to-all-start.1 = ((bf16[4,528,1024]{2,1,0:T(8,128)(2,1)}), bf16[4,528,1024]{2,1,0:T(8,128)(2,1)}, u32[]{:S(2)}, u32[]{:S(2)}) async-start(bf16[4,528,1024]{2,1,0:T(8,128)(2,1)} %get-tuple-element.47), calls=%async_computation.1 | async-start | bytes 8650752 | tf_op jit(solution)/shard_map/all_to_all | solution.py:331
  40.5 18.9 %collective-permute-done.2.refs_0_ = bf16[256,4096]{1,0:T(8,128)(2,1)} collective-permute-done((bf16[256,4096]{1,0:T(8,128)(2,1)S(1)}, bf16[256,4096]{1,0:T(8,128)(2,1)}, u32[]{:S(2)}, u32[]{:S(2)}) %collective-permute-start.2) | collective-permute-done | bytes 2097184 | tf_op jit(solution)/shard_map/ppermute | solution.py:291
  59.4 3.4 %collective-permute-start.6 = (bf16[256,4096]{1,0:T(8,128)(2,1)}, bf16[256,4096]{1,0:T(8,128)(2,1)}, u32[]{:S(2)}, u32[]{:S(2)}) collective-permute-start(bf16[256,4096]{1,0:T(8,128)(2,1)} %collective-permute-done.2.refs_0_), channel_id=1, source_target_pairs={{2,4},{3,5},{4,2},{5,3},{10,12},{11,13},{12,10},{13,11},{18,20},{1... | collective-permute-start | bytes 6291464 | tf_op jit(solution)/shard_map/ppermute | solution.py:291
  62.8 1.8 collective-permute-start.8
  68.7 16.9 %expert_rows.5 = (bf16[4,528,1024]{2,1,0:T(8,128)(2,1)}, bf16[64,4096]{1,0:T(8,128)(2,1)}, bf16[64,4096]{1,0:T(8,128)(2,1)}) custom-call(s32[1]{0:T(128)} %bitcast.5.place_ref, f32[128,2]{1,0:T(8,128)} %get-tuple-element.33.meta_ref, bf16[16,4096]{1,0:T(8,128)(2,1)} %maximum_maximum_fusion.router_ref, bf16[256,4096]{1,0:T(8,128)(2,1)} %collective-permute-done.2.refs_0_, ...), custom_call_target="tpu_custom_call" | custom-call | flops 1024 | bytes 1024 | tf_op jit(solution)/shard_map/expert_rows/pallas_call | solution.py:157
  85.7 2.6 all-to-all-done.1.refs_0_.refs_1_
  88.3 6.4 %all-to-all-start.2 = ((bf16[4,528,1024]{2,1,0:T(8,128)(2,1)}), bf16[4,528,1024]{2,1,0:T(8,128)(2,1)}, u32[]{:S(2)}, u32[]{:S(2)}) async-start(bf16[4,528,1024]{2,1,0:T(8,128)(2,1)} %get-tuple-element.48), calls=%async_computation.2 | async-start | bytes 8650752 | tf_op jit(solution)/shard_map/all_to_all | solution.py:331
  94.7 15.0 %collective-permute-done.6 = bf16[256,4096]{1,0:T(8,128)(2,1)} collective-permute-done((bf16[256,4096]{1,0:T(8,128)(2,1)}, bf16[256,4096]{1,0:T(8,128)(2,1)}, u32[]{:S(2)}, u32[]{:S(2)}) %collective-permute-start.6) | collective-permute-done | bytes 2097184 | tf_op jit(solution)/shard_map/ppermute | solution.py:291
  110.3 1.8 broadcast_select_fusion.1.refs_0_
  112.2 2.8 %collective-permute-start.12 = (bf16[256,4096]{1,0:T(8,128)(2,1)}, bf16[256,4096]{1,0:T(8,128)(2,1)S(1)}, u32[]{:S(2)}, u32[]{:S(2)}) collective-permute-start(bf16[256,4096]{1,0:T(8,128)(2,1)} %collective-permute-done.6), channel_id=1, source_target_pairs={{2,0},{3,1},{4,6},{5,7},{10,8},{11,9},{12,14},{13,15},{18,16},{19,... | collective-permute-start | bytes 6291464 | tf_op jit(solution)/shard_map/ppermute | solution.py:291
  119.3 16.9 %expert_rows.6 = (bf16[4,528,1024]{2,1,0:T(8,128)(2,1)}, bf16[64,4096]{1,0:T(8,128)(2,1)}, bf16[64,4096]{1,0:T(8,128)(2,1)}) custom-call(s32[1]{0:T(128)} %bitcast.5.place_ref, f32[128,2]{1,0:T(8,128)} %get-tuple-element.36.meta_ref, bf16[16,4096]{1,0:T(8,128)(2,1)} %maximum_maximum_fusion.router_ref, bf16[256,4096]{1,0:T(8,128)(2,1)} %copy-done.1, ...), custom_call_target="tpu_custom_call" | custom-call | flops 1024 | bytes 1024 | tf_op jit(solution)/shard_map/expert_rows/pallas_call | solution.py:157
  136.1 5.4 %all-to-all-done.2.refs_2_.refs_3_ = bf16[4,528,1024]{2,1,0:T(8,128)(2,1)} async-done(((bf16[4,528,1024]{2,1,0:T(8,128)(2,1)}), bf16[4,528,1024]{2,1,0:T(8,128)(2,1)}, u32[]{:S(2)}, u32[]{:S(2)}) %all-to-all-start.2) | async-done | bytes 4325408 | tf_op jit(solution)/shard_map/all_to_all | solution.py:331
  141.6 6.3 %all-to-all-start.3 = ((bf16[4,528,1024]{2,1,0:T(8,128)(2,1)}), bf16[4,528,1024]{2,1,0:T(8,128)(2,1)}, u32[]{:S(2)}, u32[]{:S(2)}) async-start(bf16[4,528,1024]{2,1,0:T(8,128)(2,1)} %get-tuple-element.49), calls=%async_computation.3 | async-start | bytes 8650752 | tf_op jit(solution)/shard_map/all_to_all | solution.py:331
  147.9 12.8 %collective-permute-done.12 = bf16[256,4096]{1,0:T(8,128)(2,1)S(1)} collective-permute-done((bf16[256,4096]{1,0:T(8,128)(2,1)}, bf16[256,4096]{1,0:T(8,128)(2,1)S(1)}, u32[]{:S(2)}, u32[]{:S(2)}) %collective-permute-start.12) | collective-permute-done | bytes 2097184 | tf_op jit(solution)/shard_map/ppermute | solution.py:291
  160.7 1.8 broadcast_select_fusion.refs_0_
  164.8 2.8 %collective-permute-done.10 = bf16[64,4096]{1,0:T(8,128)(2,1)S(1)} collective-permute-done((bf16[64,4096]{1,0:T(8,128)(2,1)S(1)}, bf16[64,4096]{1,0:T(8,128)(2,1)S(1)}, u32[]{:S(2)}, u32[]{:S(2)}) %collective-permute-start.10) | collective-permute-done | bytes 524320 | tf_op jit(solution)/shard_map/ppermute | solution.py:294
  168.4 2.0 collective-permute-start.11
  171.8 17.5 %expert_rows.7 = (bf16[1,528,1024]{2,1,0:T(8,128)(2,1)}, bf16[1,528,1024]{2,1,0:T(8,128)(2,1)}, bf16[1,528,1024]{2,1,0:T(8,128)(2,1)}, bf16[1,528,1024]{2,1,0:T(...) custom-call(s32[1]{0:T(128)} %bitcast.5.place_ref, f32[128,2]{1,0:T(8,128)} %get-tuple-element.39.meta_ref, ...), custom_call_target="tpu_custom_call" | custom-call | flops 1024 | bytes 1024 | tf_op jit(solution)/shard_map/expert_rows/pallas_call | solution.py:157
  192.2 1.5 collective-permute-start.18
  193.7 2.3 pad_maximum_fusion.1
  196.1 9.1 %collective-permute-done.5.refs_1_ = bf16[128,4096]{1,0:T(8,128)(2,1)} collective-permute-done((bf16[128,4096]{1,0:T(8,128)(2,1)}, bf16[128,4096]{1,0:T(8,128)(2,1)}, u32[]{:S(2)}, u32[]{:S(2)}) %collective-permute-start.5) | collective-permute-done | bytes 1048608 | tf_op jit(solution)/shard_map/ppermute | solution.py:294
  205.2 10.8 %collective-permute-done.11.refs_2_ = bf16[128,4096]{1,0:T(8,128)(2,1)} collective-permute-done((bf16[128,4096]{1,0:T(8,128)(2,1)}, bf16[128,4096]{1,0:T(8,128)(2,1)}, u32[]{:S(2)}, u32[]{:S(2)}) %collective-permute-start.11) | collective-permute-done | bytes 1048608 | tf_op jit(solution)/shard_map/ppermute | solution.py:294
  216.9 13.6 %weight_terms.2 = (f32[1024,1024]{1,0:T(8,128)}, f32[1024,1024]{1,0:T(8,128)}, f32[4,1024]{1,0:T(4,128)}) custom-call(bf16[4,528,1024]{2,1,0:T(8,128)(2,1)} %all-to-all-done.1.refs_0_.refs_1_, bf16[4,528,1024]{2,1,0:T(8,128)(2,1)} %all-to-all-done.1.refs_0_.refs_1_, bf16[4,528,1024]{2,1,0:T(8,128)(2,1)} %all-to-all-done.2.refs_2_.refs_3_, ...), custom_call_target="tpu_custom_call" | custom-call | flops 10000000000 | bytes 1024 | tf_op jit(solution)/shard_map/weight_terms/pallas_call | solution.py:233
  230.5 10.5 %collective-permute-done.17.refs_2_.refs_6_ = bf16[1,528,1024]{2,1,0:T(8,128)(2,1)S(1)} collective-permute-done((bf16[1,528,1024]{2,1,0:T(8,128)(2,1)}, bf16[1,528,1024]{2,1,0:T(8,128)(2,1)S(1)}, u32[]{:S(2)}, u32[]{:S(2)}) %collective-permute-start.17) | collective-permute-done | bytes 1081376 | tf_op jit(solution)/shard_map/ppermute | solution.py:342
  242.3 8.7 %weight_terms.3 = (bf16[1024,1024]{1,0:T(8,128)(2,1)}, bf16[1024,1024]{1,0:T(8,128)(2,1)}, f32[4,1024]{1,0:T(4,128)}) custom-call(bf16[1,528,1024]{2,1,0:T(8,128)(2,1)} %get-tuple-element.43.refs_0_.refs_4_, bf16[1,528,1024]{2,1,0:T(8,128)(2,1)} %copy-done.3, bf16[1,528,1024]{2,1,0:T(8,128)(2,1)} %copy-done.4, bf16[1,528,1024]{2,1,0:T(8,128)(2,1)} %copy-done.5, ...), custom_call_target="tpu_custom_call" | custom-call | flops 1024 | bytes 1024 | tf_op jit(solution)/shard_map/weight_terms/pallas_call | solution.py:233
  251.1 1.3 copy.25
  252.4 10.7 %collective-permute-done.15.refs_3_ = bf16[128,4096]{1,0:T(8,128)(2,1)} collective-permute-done((bf16[128,4096]{1,0:T(8,128)(2,1)}, bf16[128,4096]{1,0:T(8,128)(2,1)}, u32[]{:S(2)}, u32[]{:S(2)}) %collective-permute-start.15) | collective-permute-done | bytes 1048608 | tf_op jit(solution)/shard_map/ppermute | solution.py:294
  263.1 4.6 %combine.1 = bf16[128,4096]{1,0:T(8,128)(2,1)} custom-call(f32[1,512]{1,0:T(1,128)} %reshape.79.slots_ref, bf16[128,4096]{1,0:T(8,128)(2,1)} %constant_dynamic-update-slice_fusion.refs_0_, bf16[128,4096]{1,0:T(8,128)(2,1)} %collective-permute-done.5.refs_1_, bf16[128,4096]{1,0:T(8,128)(2,1)} %collective-permute-done.11.refs_2_, ...), custom_call_target="tpu_custom_call" | custom-call | flops 1024 | bytes 1024 | tf_op jit(solution)/shard_map/combine/pallas_call | solution.py:259
  (91 shorter events, 25.6 us)
Async XLA Ops:
  2.7 8.4 %all-to-all-start = ((f32[8,1,192]{2,1,0:T(1,128)}), f32[8,1,192]{2,1,0:T(1,128)S(1)}, u32[]{:S(2)}, u32[]{:S(2)}) async-start(f32[8,1,192]{2,1,0:T(1,128)} %all_to_all.17), calls=%async_computation | async-start | bytes 16384 | tf_op jit(solution)/shard_map/all_to_all | solution.py:299
  9.6 8.6 %copy-start.2 = (bf16[256,4096]{1,0:T(8,128)(2,1)}, bf16[256,4096]{1,0:T(8,128)(2,1)S(1)}, u32[]{:S(2)}) copy-start(bf16[256,4096]{1,0:T(8,128)(2,1)S(1)} %pad_maximum_fusion.refs_0_) | copy-start | bytes 6291460
  11.1 7.0 %collective-permute-start = (bf16[256,4096]{1,0:T(8,128)(2,1)S(1)}, bf16[256,4096]{1,0:T(8,128)(2,1)}, u32[]{:S(2)}, u32[]{:S(2)}) collective-permute-start(bf16[256,4096]{1,0:T(8,128)(2,1)S(1)} %pad_maximum_fusion.refs_0_), channel_id=1, source_target_pairs={{0,1},{1,0},{2,3},{3,2},{4,5},{5,4},{6,7},{7,6},{8,9},{9,8},{10,11... | collective-permute-start | bytes 6291464 | tf_op jit(solution)/shard_map/ppermute | solution.py:294
  11.2 48.2 %collective-permute-start.2 = (bf16[256,4096]{1,0:T(8,128)(2,1)S(1)}, bf16[256,4096]{1,0:T(8,128)(2,1)}, u32[]{:S(2)}, u32[]{:S(2)}) collective-permute-start(bf16[256,4096]{1,0:T(8,128)(2,1)S(1)} %pad_maximum_fusion.refs_0_), channel_id=1, source_target_pairs={{0,2},{1,3},{2,0},{3,1},{4,6},{5,7},{6,4},{7,5},{8,10},{9,11},{10,... | collective-permute-start | bytes 6291464 | tf_op jit(solution)/shard_map/ppermute | solution.py:291
  12.5 50.3 %collective-permute-start.7 = (bf16[256,4096]{1,0:T(8,128)(2,1)S(1)}, bf16[256,4096]{1,0:T(8,128)(2,1)}, u32[]{:S(2)}, u32[]{:S(2)}) collective-permute-start(bf16[256,4096]{1,0:T(8,128)(2,1)S(1)} %pad_maximum_fusion.refs_0_), channel_id=1, source_target_pairs={{2,4},{3,5},{4,2},{5,3},{10,12},{11,13},{12,10},{13,11},{18,20},{1... | collective-permute-start | bytes 6291464 | tf_op jit(solution)/shard_map/ppermute | solution.py:291
  35.1 29.5 %copy-start.16 = (bf16[64,4096]{1,0:T(8,128)(2,1)S(1)}, bf16[64,4096]{1,0:T(8,128)(2,1)}, u32[]{:S(2)}) copy-start(bf16[64,4096]{1,0:T(8,128)(2,1)} %get-tuple-element.32) | copy-start | bytes 1572868
  35.1 29.8 %copy-start.12 = (bf16[64,4096]{1,0:T(8,128)(2,1)S(1)}, bf16[64,4096]{1,0:T(8,128)(2,1)}, u32[]{:S(2)}) copy-start(bf16[64,4096]{1,0:T(8,128)(2,1)} %get-tuple-element.31) | copy-start | bytes 1572868
  35.1 53.2 %all-to-all-start.1 = ((bf16[4,528,1024]{2,1,0:T(8,128)(2,1)}), bf16[4,528,1024]{2,1,0:T(8,128)(2,1)}, u32[]{:S(2)}, u32[]{:S(2)}) async-start(bf16[4,528,1024]{2,1,0:T(8,128)(2,1)} %get-tuple-element.47), calls=%async_computation.1 | async-start | bytes 8650752 | tf_op jit(solution)/shard_map/all_to_all | solution.py:331
  59.4 8.0 %collective-permute-start.3 = (bf16[256,4096]{1,0:T(8,128)(2,1)}, bf16[256,4096]{1,0:T(8,128)(2,1)S(1)}, u32[]{:S(2)}, u32[]{:S(2)}) collective-permute-start(bf16[256,4096]{1,0:T(8,128)(2,1)} %collective-permute-done.2.refs_0_), channel_id=1, source_target_pairs={{0,1},{1,0},{2,3},{3,2},{4,5},{5,4},{6,7},{7,6},{8,9},{9,8},{10,11... | collective-permute-start | bytes 6291464 | tf_op jit(solution)/shard_map/ppermute | solution.py:294
  59.4 50.2 %collective-permute-start.6 = (bf16[256,4096]{1,0:T(8,128)(2,1)}, bf16[256,4096]{1,0:T(8,128)(2,1)}, u32[]{:S(2)}, u32[]{:S(2)}) collective-permute-start(bf16[256,4096]{1,0:T(8,128)(2,1)} %collective-permute-done.2.refs_0_), channel_id=1, source_target_pairs={{2,4},{3,5},{4,2},{5,3},{10,12},{11,13},{12,10},{13,11},{18,20},{1... | collective-permute-start | bytes 6291464 | tf_op jit(solution)/shard_map/ppermute | solution.py:291
  62.8 47.5 %collective-permute-start.8 = (bf16[256,4096]{1,0:T(8,128)(2,1)}, bf16[256,4096]{1,0:T(8,128)(2,1)S(1)}, u32[]{:S(2)}, u32[]{:S(2)}) collective-permute-start(bf16[256,4096]{1,0:T(8,128)(2,1)} %collective-permute-done.7), channel_id=1, source_target_pairs={{2,0},{3,1},{4,6},{5,7},{10,8},{11,9},{12,14},{13,15},{18,16},{19,... | collective-permute-start | bytes 6291464 | tf_op jit(solution)/shard_map/ppermute | solution.py:291
  64.6 2.0 collective-permute-start.1
  88.3 53.3 %all-to-all-start.2 = ((bf16[4,528,1024]{2,1,0:T(8,128)(2,1)}), bf16[4,528,1024]{2,1,0:T(8,128)(2,1)}, u32[]{:S(2)}, u32[]{:S(2)}) async-start(bf16[4,528,1024]{2,1,0:T(8,128)(2,1)} %get-tuple-element.48), calls=%async_computation.2 | async-start | bytes 8650752 | tf_op jit(solution)/shard_map/all_to_all | solution.py:331
  94.6 20.4 %copy-start.14 = (bf16[64,4096]{1,0:T(8,128)(2,1)S(1)}, bf16[64,4096]{1,0:T(8,128)(2,1)}, u32[]{:S(2)}) copy-start(bf16[64,4096]{1,0:T(8,128)(2,1)} %get-tuple-element.35) | copy-start | bytes 1572868
  94.7 20.7 %copy-start.10 = (bf16[64,4096]{1,0:T(8,128)(2,1)S(1)}, bf16[64,4096]{1,0:T(8,128)(2,1)}, u32[]{:S(2)}) copy-start(bf16[64,4096]{1,0:T(8,128)(2,1)} %get-tuple-element.34) | copy-start | bytes 1572868
  112.1 5.8 %collective-permute-start.9 = (bf16[256,4096]{1,0:T(8,128)(2,1)S(1)}, bf16[256,4096]{1,0:T(8,128)(2,1)S(1)}, u32[]{:S(2)}, u32[]{:S(2)}) collective-permute-start(bf16[256,4096]{1,0:T(8,128)(2,1)S(1)} %broadcast_select_fusion.1.refs_0_), channel_id=1, source_target_pairs={{0,1},{1,0},{2,3},{3,2},{4,5},{5,4},{6,7},{7,6},{8,9},{9,8},{10,11... | collective-permute-start | bytes 6291464 | tf_op jit(solution)/shard_map/ppermute | solution.py:294
  112.2 48.5 %collective-permute-start.12 = (bf16[256,4096]{1,0:T(8,128)(2,1)}, bf16[256,4096]{1,0:T(8,128)(2,1)S(1)}, u32[]{:S(2)}, u32[]{:S(2)}) collective-permute-start(bf16[256,4096]{1,0:T(8,128)(2,1)} %collective-permute-done.6), channel_id=1, source_target_pairs={{2,0},{3,1},{4,6},{5,7},{10,8},{11,9},{12,14},{13,15},{18,16},{19,... | collective-permute-start | bytes 6291464 | tf_op jit(solution)/shard_map/ppermute | solution.py:291
  115.0 2.1 collective-permute-start.4
  141.6 75.3 %all-to-all-start.3 = ((bf16[4,528,1024]{2,1,0:T(8,128)(2,1)}), bf16[4,528,1024]{2,1,0:T(8,128)(2,1)}, u32[]{:S(2)}, u32[]{:S(2)}) async-start(bf16[4,528,1024]{2,1,0:T(8,128)(2,1)} %get-tuple-element.49), calls=%async_computation.3 | async-start | bytes 8650752 | tf_op jit(solution)/shard_map/all_to_all | solution.py:331
  147.9 14.7 %copy-start.15 = (bf16[64,4096]{1,0:T(8,128)(2,1)S(1)}, bf16[64,4096]{1,0:T(8,128)(2,1)}, u32[]{:S(2)}) copy-start(bf16[64,4096]{1,0:T(8,128)(2,1)} %get-tuple-element.38) | copy-start | bytes 1572868
  147.9 16.0 %copy-start.11 = (bf16[64,4096]{1,0:T(8,128)(2,1)S(1)}, bf16[64,4096]{1,0:T(8,128)(2,1)}, u32[]{:S(2)}) copy-start(bf16[64,4096]{1,0:T(8,128)(2,1)} %get-tuple-element.37) | copy-start | bytes 1572868
  162.6 7.9 %copy-start = (bf16[256,4096]{1,0:T(8,128)(2,1)}, bf16[256,4096]{1,0:T(8,128)(2,1)S(1)}, u32[]{:S(2)}) copy-start(bf16[256,4096]{1,0:T(8,128)(2,1)S(1)} %broadcast_select_fusion.refs_0_) | copy-start | bytes 6291460
  162.6 7.9 %collective-permute-start.13 = (bf16[256,4096]{1,0:T(8,128)(2,1)S(1)}, bf16[256,4096]{1,0:T(8,128)(2,1)S(1)}, u32[]{:S(2)}, u32[]{:S(2)}) collective-permute-start(bf16[256,4096]{1,0:T(8,128)(2,1)S(1)} %broadcast_select_fusion.refs_0_), channel_id=1, source_target_pairs={{0,1},{1,0},{2,3},{3,2},{4,5},{5,4},{6,7},{7,6},{8,9},{9,8},{10,11... | collective-permute-start | bytes 6291464 | tf_op jit(solution)/shard_map/ppermute | solution.py:294
  162.7 4.9 %collective-permute-start.10 = (bf16[64,4096]{1,0:T(8,128)(2,1)S(1)}, bf16[64,4096]{1,0:T(8,128)(2,1)S(1)}, u32[]{:S(2)}, u32[]{:S(2)}) collective-permute-start(bf16[64,4096]{1,0:T(8,128)(2,1)S(1)} %copy-done.15), channel_id=1, source_target_pairs={{0,1},{1,0},{2,3},{3,2},{4,5},{5,4},{6,7},{7,6},{8,9},{9,8},{10,11... | collective-permute-start | bytes 1572872 | tf_op jit(solution)/shard_map/ppermute | solution.py:294
  163.1 42.0 %collective-permute-start.5 = (bf16[128,4096]{1,0:T(8,128)(2,1)}, bf16[128,4096]{1,0:T(8,128)(2,1)}, u32[]{:S(2)}, u32[]{:S(2)}) collective-permute-start(bf16[128,4096]{1,0:T(8,128)(2,1)} %constant_dynamic-update-slice_fusion.2), channel_id=1, source_target_pairs={{0,2},{1,3},{2,0},{3,1},{4,6},{5,7},{6,4},{7,5},{8,10},{9,11},{10,... | collective-permute-start | bytes 3145736 | tf_op jit(solution)/shard_map/ppermute | solution.py:294
  168.4 47.6 %collective-permute-start.11 = (bf16[128,4096]{1,0:T(8,128)(2,1)}, bf16[128,4096]{1,0:T(8,128)(2,1)}, u32[]{:S(2)}, u32[]{:S(2)}) collective-permute-start(bf16[128,4096]{1,0:T(8,128)(2,1)} %constant_dynamic-update-slice_fusion.4), channel_id=1, source_target_pairs={{0,4},{1,5},{2,6},{3,7},{4,0},{5,1},{6,2},{7,3},{8,12},{9,13},{10,... | collective-permute-start | bytes 3145736 | tf_op jit(solution)/shard_map/ppermute | solution.py:294
  189.3 2.2 collective-permute-start.14
  189.4 41.1 %collective-permute-start.16 = (bf16[1,528,1024]{2,1,0:T(8,128)(2,1)}, bf16[1,528,1024]{2,1,0:T(8,128)(2,1)S(1)}, u32[]{:S(2)}, u32[]{:S(2)}) collective-permute-start(bf16[1,528,1024]{2,1,0:T(8,128)(2,1)} %get-tuple-element.44), channel_id=1, source_target_pairs={{0,8},{8,0},{16,24},{24,16},{1,9},{9,1},{17,25},{25,17},{2,10},{10... | collective-permute-start | bytes 3244040 | tf_op jit(solution)/shard_map/ppermute | solution.py:342
  190.0 51.0 %collective-permute-start.17 = (bf16[1,528,1024]{2,1,0:T(8,128)(2,1)}, bf16[1,528,1024]{2,1,0:T(8,128)(2,1)S(1)}, u32[]{:S(2)}, u32[]{:S(2)}) collective-permute-start(bf16[1,528,1024]{2,1,0:T(8,128)(2,1)} %get-tuple-element.45), channel_id=1, source_target_pairs={{0,16},{8,24},{16,0},{24,8},{1,17},{9,25},{17,1},{25,9},{2,18},{10... | collective-permute-start | bytes 3244040 | tf_op jit(solution)/shard_map/ppermute | solution.py:342
  192.2 48.8 %collective-permute-start.18 = (bf16[1,528,1024]{2,1,0:T(8,128)(2,1)}, bf16[1,528,1024]{2,1,0:T(8,128)(2,1)S(1)}, u32[]{:S(2)}, u32[]{:S(2)}) collective-permute-start(bf16[1,528,1024]{2,1,0:T(8,128)(2,1)} %get-tuple-element.46), channel_id=1, source_target_pairs={{0,24},{8,16},{16,8},{24,0},{1,25},{9,17},{17,9},{25,1},{2,26},{10... | collective-permute-start | bytes 3244040 | tf_op jit(solution)/shard_map/ppermute | solution.py:342
  216.0 47.2 %collective-permute-start.15 = (bf16[128,4096]{1,0:T(8,128)(2,1)}, bf16[128,4096]{1,0:T(8,128)(2,1)}, u32[]{:S(2)}, u32[]{:S(2)}) collective-permute-start(bf16[128,4096]{1,0:T(8,128)(2,1)} %pad_maximum_fusion.1), channel_id=1, source_target_pairs={{0,6},{1,7},{2,4},{3,5},{4,2},{5,3},{6,0},{7,1},{8,14},{9,15},{10,... | collective-permute-start | bytes 3145736 | tf_op jit(solution)/shard_map/ppermute | solution.py:294
  230.5 10.5 %copy-start.3 = (bf16[1,528,1024]{2,1,0:T(8,128)(2,1)}, bf16[1,528,1024]{2,1,0:T(8,128)(2,1)S(1)}, u32[]{:S(2)}) copy-start(bf16[1,528,1024]{2,1,0:T(8,128)(2,1)S(1)} %collective-permute-done.16.refs_1_.refs_5_) | copy-start | bytes 3244036
  (8 other events, 20.4 us)

commit v4 on v3

--- a/solution.py
+++ b/solution.py
@@ -218,7 +218,7 @@
 def weight_terms(chunks, rows, start, last):
     dp = sum(block.shape[0] for block in chunks[0])
     piece = chunks[0][0].shape[2]
-    tile = min(piece, 256)
+    tile = min(piece, 512)
     kind = jnp.bfloat16 if last else jnp.float32
     strip = pl.BlockSpec((tile, piece), lambda i: (i, 0))
     column = pl.BlockSpec((dp, piece), lambda i: (0, 0))
@@ -243,29 +243,34 @@
     )(*arrays)
 
 
-def combine_kernel(slots_ref, *refs):
-    blocks, out_ref = refs[:-1], refs[-1]
+def combine_kernel(has_start, slots_ref, *refs):
+    blocks, start, out_ref = refs[: len(refs) - 1 - has_start], refs[-2], refs[-1]
     tok_rows = out_ref.shape[0]
     places = lax.broadcasted_iota(jnp.int32, (tok_rows, slots_ref.shape[1]), 0).astype(jnp.float32)
     picks = jnp.where(slots_ref[...] == places, 1.0, 0.0).astype(jnp.bfloat16)
     rows = jnp.concatenate([block[...] for block in blocks], axis=0)
-    out_ref[...] = jnp.dot(picks, rows, preferred_element_type=jnp.float32).astype(out_ref.dtype)
-
-
-def combine(slots, blocks, tok_rows):
-    per_slot, width = blocks[0].shape
-    tile = 1024 if width % 1024 == 0 else width
-    block = pl.BlockSpec((per_slot, tile), lambda k: (0, k))
+    total = jnp.dot(picks, rows, preferred_element_type=jnp.float32)
+    if has_start:
+        total = total + start[...]
+    out_ref[...] = total.astype(out_ref.dtype)
+
+
+def combine(slots, blocks, tok_rows, start, kind):
+    count, width = blocks[0].shape
+    tile = 2048 if width % 2048 == 0 else width
+    block = pl.BlockSpec((count, tile), lambda k: (0, k))
+    strip = pl.BlockSpec((tok_rows, tile), lambda k: (0, k))
+    starts = [] if start is None else [start]
     return pl.pallas_call(
-        combine_kernel,
+        functools.partial(combine_kernel, len(starts)),
         grid=(width // tile,),
-        in_specs=[pl.BlockSpec(slots.shape, lambda k: (0, 0))] + [block] * len(blocks),
-        out_specs=pl.BlockSpec((tok_rows, tile), lambda k: (0, k)),
-        out_shape=jax.ShapeDtypeStruct((tok_rows, width), jnp.bfloat16),
+        in_specs=[pl.BlockSpec(slots.shape, lambda k: (0, 0))] + [block] * len(blocks) + [strip] * len(starts),
+        out_specs=strip,
+        out_shape=jax.ShapeDtypeStruct((tok_rows, width), kind),
         compiler_params=pltpu.CompilerParams(vmem_limit_bytes=VMEM_LIMIT),
         cost_estimate=SMALL,
         name="combine",
-    )(slots, *blocks)
+    )(slots, *blocks, *starts)
 
 
 def after(block, *others):
@@ -352,9 +357,12 @@
     back3 = across(after(back3, back1, back2), 6)
     rows = 2 * per_slot
     early = weight_terms([got0, got1, got2], rows, None, False)
-    blocks = [back0, back1, back2, back3]
-    up_sum, down_sum, column = weight_terms([got3], rows, early, True)
-    tokens_grad = combine(mine.reshape(1, -1), blocks, tok_rows)
+    lists = mine.reshape(1, -1)
+    most = 3 * rows
+    partial = combine(lists[:, :most], [back0, back1, back2], tok_rows, None, jnp.float32)
+    partial, first = lax.optimization_barrier((partial, early[0]))
+    up_sum, down_sum, column = weight_terms([got3], rows, (first, early[1], early[2]), True)
+    tokens_grad = combine(lists[:, most:], [back3], tok_rows, partial, jnp.bfloat16)
     return (tokens_grad, up_sum[None], down_sum[None], column.reshape(-1, 1))
 
 

time: 269 us -> 267 us (level)
  waiting for transfers between devices: 103 us -> 99.6 us
    ppermute x3, waiting for transfers between devices: 10.5 us -> 6.24 us  [chunk(): got.append(lax.ppermute(messages[k], 'dp', [(q, q ^ k) for q in range(dp)]))]
    pallas_call x1 -> x2, Pallas kernels: 4.61 us -> 6.33 us  [combine(): pl.pallas_call(functools.partial(combine_kernel, len(starts)), grid=(widt...]
  transfers between devices with their start and end apart: 23 -> 23, of which waited for: 15 -> 15; matrix products, arithmetic and copies ran while one was open for 7% -> 7% of each run, Pallas kernels for 34% -> 35%
where the time goes in v4:
time: 267 us; the launch traced here: 266 us
  waiting for transfers between devices  99.6 us (37%)
  Pallas kernels  96.2 us (36%)
  starting transfers between devices  43.1 us (16%)
  local copies, waits for them, and re-layouts  15.1 us (6%)
  other arithmetic  11.1 us (4%)
    pallas_call x4, Pallas kernels, expert_rows(): pl.pallas_call(functools.partial(expert_kernel, apart, steps), grid_spec=...  68.3 us
    ppermute x5, waiting for transfers between devices, between(): return lax.ppermute(block, 'expert', pairs)  47.3 us
    ppermute x11, waiting for transfers between devices, across(): lax.ppermute(block, 'expert', [(e, e ^ mask) for e in range(experts)])  37.6 us
    pallas_call x2, Pallas kernels, weight_terms(): pl.pallas_call(functools.partial(weights_kernel, [len(blocks) for blocks...  21.6 us
    all_to_all x3, starting transfers between devices, exchange(): return lax.all_to_all(block, 'dp', 0, 0, tiled=True)  18.2 us
    ppermute x5, starting transfers between devices, between(): return lax.ppermute(block, 'expert', pairs)  12.8 us
    unnamed x39, local copies, waits for them, and re-layouts  9.66 us
    all_to_all x3, waiting for transfers between devices, exchange(): return lax.all_to_all(block, 'dp', 0, 0, tiled=True)  7.99 us
  transfers between devices with their start and end apart: 23, of which 15 were waited for; matrix products, arithmetic and copies ran while one was open for 7% of the time, Pallas kernels for 35%

profile of v4, /device:TPU:22, one launch (start us, length us, event | category | flops | bytes accessed | tf_op | source)
XLA Modules:
  0.0 266.1 jit_solution(16964518614447814465)
XLA Ops:
  2.7 5.2 %all-to-all-start = ((f32[8,1,192]{2,1,0:T(1,128)}), f32[8,1,192]{2,1,0:T(1,128)S(1)}, u32[]{:S(2)}, u32[]{:S(2)}) async-start(f32[8,1,192]{2,1,0:T(1,128)} %all_to_all.17), calls=%async_computation | async-start | bytes 16384 | tf_op jit(solution)/shard_map/all_to_all | solution.py:304
  7.9 1.7 pad_maximum_fusion.refs_0_
  12.5 3.6 %collective-permute-start.6 = (bf16[256,4096]{1,0:T(8,128)(2,1)S(1)}, bf16[256,4096]{1,0:T(8,128)(2,1)}, u32[]{:S(2)}, u32[]{:S(2)}) collective-permute-start(bf16[256,4096]{1,0:T(8,128)(2,1)S(1)} %pad_maximum_fusion.refs_0_), channel_id=1, source_target_pairs={{2,4},{3,5},{4,2},{5,3},{10,12},{11,13},{12,10},{13,11},{18,20},{1... | collective-permute-start | bytes 6291464 | tf_op jit(solution)/shard_map/ppermute | solution.py:296
  18.2 16.9 %expert_rows.4 = (bf16[4,528,1024]{2,1,0:T(8,128)(2,1)}, bf16[64,4096]{1,0:T(8,128)(2,1)}, bf16[64,4096]{1,0:T(8,128)(2,1)}) custom-call(s32[1]{0:T(128)} %bitcast.5.place_ref, f32[128,2]{1,0:T(8,128)} %get-tuple-element.62.meta_ref, bf16[16,4096]{1,0:T(8,128)(2,1)} %maximum_maximum_fusion.router_ref, bf16[256,4096]{1,0:T(8,128)(2,1)} %copy-done.2, ...), custom_call_target="tpu_custom_call" | custom-call | flops 1024 | bytes 1024 | tf_op jit(solution)/shard_map/expert_rows/pallas_call | solution.py:157
  35.1 5.5 %all-to-all-start.1 = ((bf16[4,528,1024]{2,1,0:T(8,128)(2,1)}), bf16[4,528,1024]{2,1,0:T(8,128)(2,1)}, u32[]{:S(2)}, u32[]{:S(2)}) async-start(bf16[4,528,1024]{2,1,0:T(8,128)(2,1)} %get-tuple-element.45), calls=%async_computation.1 | async-start | bytes 8650752 | tf_op jit(solution)/shard_map/all_to_all | solution.py:336
  40.6 18.8 %collective-permute-done.2.refs_0_ = bf16[256,4096]{1,0:T(8,128)(2,1)} collective-permute-done((bf16[256,4096]{1,0:T(8,128)(2,1)S(1)}, bf16[256,4096]{1,0:T(8,128)(2,1)}, u32[]{:S(2)}, u32[]{:S(2)}) %collective-permute-start.2) | collective-permute-done | bytes 2097184 | tf_op jit(solution)/shard_map/ppermute | solution.py:296
  59.4 3.4 %collective-permute-start.5 = (bf16[256,4096]{1,0:T(8,128)(2,1)}, bf16[256,4096]{1,0:T(8,128)(2,1)}, u32[]{:S(2)}, u32[]{:S(2)}) collective-permute-start(bf16[256,4096]{1,0:T(8,128)(2,1)} %collective-permute-done.2.refs_0_), channel_id=1, source_target_pairs={{2,4},{3,5},{4,2},{5,3},{10,12},{11,13},{12,10},{13,11},{18,20},{1... | collective-permute-start | bytes 6291464 | tf_op jit(solution)/shard_map/ppermute | solution.py:296
  62.8 1.8 collective-permute-start.7
  68.7 17.0 %expert_rows.5 = (bf16[4,528,1024]{2,1,0:T(8,128)(2,1)}, bf16[64,4096]{1,0:T(8,128)(2,1)}, bf16[64,4096]{1,0:T(8,128)(2,1)}) custom-call(s32[1]{0:T(128)} %bitcast.5.place_ref, f32[128,2]{1,0:T(8,128)} %get-tuple-element.35.meta_ref, bf16[16,4096]{1,0:T(8,128)(2,1)} %maximum_maximum_fusion.router_ref, bf16[256,4096]{1,0:T(8,128)(2,1)} %collective-permute-done.2.refs_0_, ...), custom_call_target="tpu_custom_call" | custom-call | flops 1024 | bytes 1024 | tf_op jit(solution)/shard_map/expert_rows/pallas_call | solution.py:157
  85.7 2.6 all-to-all-done.1.refs_0_.refs_1_
  88.3 6.4 %all-to-all-start.2 = ((bf16[4,528,1024]{2,1,0:T(8,128)(2,1)}), bf16[4,528,1024]{2,1,0:T(8,128)(2,1)}, u32[]{:S(2)}, u32[]{:S(2)}) async-start(bf16[4,528,1024]{2,1,0:T(8,128)(2,1)} %get-tuple-element.46), calls=%async_computation.2 | async-start | bytes 8650752 | tf_op jit(solution)/shard_map/all_to_all | solution.py:336
  94.7 15.0 %collective-permute-done.5 = bf16[256,4096]{1,0:T(8,128)(2,1)} collective-permute-done((bf16[256,4096]{1,0:T(8,128)(2,1)}, bf16[256,4096]{1,0:T(8,128)(2,1)}, u32[]{:S(2)}, u32[]{:S(2)}) %collective-permute-start.5) | collective-permute-done | bytes 2097184 | tf_op jit(solution)/shard_map/ppermute | solution.py:296
  110.3 1.8 broadcast_select_fusion.1.refs_0_
  112.2 2.8 %collective-permute-start.10 = (bf16[256,4096]{1,0:T(8,128)(2,1)}, bf16[256,4096]{1,0:T(8,128)(2,1)S(1)}, u32[]{:S(2)}, u32[]{:S(2)}) collective-permute-start(bf16[256,4096]{1,0:T(8,128)(2,1)} %collective-permute-done.5), channel_id=1, source_target_pairs={{2,0},{3,1},{4,6},{5,7},{10,8},{11,9},{12,14},{13,15},{18,16},{19,... | collective-permute-start | bytes 6291464 | tf_op jit(solution)/shard_map/ppermute | solution.py:296
  119.3 16.9 %expert_rows.6 = (bf16[4,528,1024]{2,1,0:T(8,128)(2,1)}, bf16[64,4096]{1,0:T(8,128)(2,1)}, bf16[64,4096]{1,0:T(8,128)(2,1)}) custom-call(s32[1]{0:T(128)} %bitcast.5.place_ref, f32[128,2]{1,0:T(8,128)} %get-tuple-element.38.meta_ref, bf16[16,4096]{1,0:T(8,128)(2,1)} %maximum_maximum_fusion.router_ref, bf16[256,4096]{1,0:T(8,128)(2,1)} %copy-done.1, ...), custom_call_target="tpu_custom_call" | custom-call | flops 1024 | bytes 1024 | tf_op jit(solution)/shard_map/expert_rows/pallas_call | solution.py:157
  136.2 5.4 %all-to-all-done.2.refs_2_.refs_3_ = bf16[4,528,1024]{2,1,0:T(8,128)(2,1)} async-done(((bf16[4,528,1024]{2,1,0:T(8,128)(2,1)}), bf16[4,528,1024]{2,1,0:T(8,128)(2,1)}, u32[]{:S(2)}, u32[]{:S(2)}) %all-to-all-start.2) | async-done | bytes 4325408 | tf_op jit(solution)/shard_map/all_to_all | solution.py:336
  141.6 6.3 %all-to-all-start.3 = ((bf16[4,528,1024]{2,1,0:T(8,128)(2,1)}), bf16[4,528,1024]{2,1,0:T(8,128)(2,1)}, u32[]{:S(2)}, u32[]{:S(2)}) async-start(bf16[4,528,1024]{2,1,0:T(8,128)(2,1)} %get-tuple-element.47), calls=%async_computation.3 | async-start | bytes 8650752 | tf_op jit(solution)/shard_map/all_to_all | solution.py:336
  147.9 12.8 %collective-permute-done.10 = bf16[256,4096]{1,0:T(8,128)(2,1)S(1)} collective-permute-done((bf16[256,4096]{1,0:T(8,128)(2,1)}, bf16[256,4096]{1,0:T(8,128)(2,1)S(1)}, u32[]{:S(2)}, u32[]{:S(2)}) %collective-permute-start.10) | collective-permute-done | bytes 2097184 | tf_op jit(solution)/shard_map/ppermute | solution.py:296
  160.7 1.8 broadcast_select_fusion.refs_0_
  164.8 2.8 %collective-permute-done.9 = bf16[64,4096]{1,0:T(8,128)(2,1)S(1)} collective-permute-done((bf16[64,4096]{1,0:T(8,128)(2,1)S(1)}, bf16[64,4096]{1,0:T(8,128)(2,1)S(1)}, u32[]{:S(2)}, u32[]{:S(2)}) %collective-permute-start.9) | collective-permute-done | bytes 524320 | tf_op jit(solution)/shard_map/ppermute | solution.py:299
  168.4 2.0 collective-permute-start.14
  171.7 17.5 %expert_rows.7 = (bf16[1,528,1024]{2,1,0:T(8,128)(2,1)}, bf16[1,528,1024]{2,1,0:T(8,128)(2,1)}, bf16[1,528,1024]{2,1,0:T(8,128)(2,1)}, bf16[1,528,1024]{2,1,0:T(...) custom-call(s32[1]{0:T(128)} %bitcast.5.place_ref, f32[128,2]{1,0:T(8,128)} %get-tuple-element.41.meta_ref, ...), custom_call_target="tpu_custom_call" | custom-call | flops 1024 | bytes 1024 | tf_op jit(solution)/shard_map/expert_rows/pallas_call | solution.py:157
  192.2 1.5 collective-permute-start.18
  193.7 2.3 pad_maximum_fusion.1
  196.0 9.2 %collective-permute-done.13.refs_1_ = bf16[128,4096]{1,0:T(8,128)(2,1)} collective-permute-done((bf16[128,4096]{1,0:T(8,128)(2,1)}, bf16[128,4096]{1,0:T(8,128)(2,1)}, u32[]{:S(2)}, u32[]{:S(2)}) %collective-permute-start.13) | collective-permute-done | bytes 1048608 | tf_op jit(solution)/shard_map/ppermute | solution.py:299
  205.2 10.8 %collective-permute-done.14.refs_2_ = bf16[128,4096]{1,0:T(8,128)(2,1)} collective-permute-done((bf16[128,4096]{1,0:T(8,128)(2,1)}, bf16[128,4096]{1,0:T(8,128)(2,1)}, u32[]{:S(2)}, u32[]{:S(2)}) %collective-permute-start.14) | collective-permute-done | bytes 1048608 | tf_op jit(solution)/shard_map/ppermute | solution.py:299
  217.4 3.4 %combine.2.refs_1_ = f32[128,4096]{1,0:T(8,128)} custom-call(f32[1,384]{1,0:T(1,128)} %slice.19.slots_ref, bf16[128,4096]{1,0:T(8,128)(2,1)} %constant_dynamic-update-slice_fusion.refs_0_, bf16[128,4096]{1,0:T(8,128)(2,1)} %collective-permute-done.13.refs_1_, bf16[128,4096]{1,0:T(8,128)(2,1)} %collective-permute-done.14.refs_2_), custom_call_target="tpu_custom_call" | custom-call | flops 1024 | bytes 1024 | tf_op jit(solution)/shard_map/combine/pallas_call | solution.py:264
  220.7 14.0 %weight_terms.2 = (f32[1024,1024]{1,0:T(8,128)}, f32[1024,1024]{1,0:T(8,128)}, f32[4,1024]{1,0:T(4,128)}) custom-call(bf16[4,528,1024]{2,1,0:T(8,128)(2,1)} %all-to-all-done.1.refs_0_.refs_1_, bf16[4,528,1024]{2,1,0:T(8,128)(2,1)} %all-to-all-done.1.refs_0_.refs_1_, bf16[4,528,1024]{2,1,0:T(8,128)(2,1)} %all-to-all-done.2.refs_2_.refs_3_, ...), custom_call_target="tpu_custom_call" | custom-call | flops 10000000000 | bytes 1024 | tf_op jit(solution)/shard_map/weight_terms/pallas_call | solution.py:233
  234.8 6.2 %collective-permute-done.18.refs_3_.refs_7_ = bf16[1,528,1024]{2,1,0:T(8,128)(2,1)S(1)} collective-permute-done((bf16[1,528,1024]{2,1,0:T(8,128)(2,1)}, bf16[1,528,1024]{2,1,0:T(8,128)(2,1)S(1)}, u32[]{:S(2)}, u32[]{:S(2)}) %collective-permute-start.18) | collective-permute-done | bytes 1081376 | tf_op jit(solution)/shard_map/ppermute | solution.py:347
  242.0 7.7 %weight_terms.3 = (bf16[1024,1024]{1,0:T(8,128)(2,1)}, bf16[1024,1024]{1,0:T(8,128)(2,1)}, f32[4,1024]{1,0:T(4,128)}) custom-call(bf16[1,528,1024]{2,1,0:T(8,128)(2,1)} %get-tuple-element.50.refs_0_.refs_4_, bf16[1,528,1024]{2,1,0:T(8,128)(2,1)} %copy-done.3, bf16[1,528,1024]{2,1,0:T(8,128)(2,1)} %copy-done.4, bf16[1,528,1024]{2,1,0:T(8,128)(2,1)} %copy-done.5, ...), custom_call_target="tpu_custom_call" | custom-call | flops 1024 | bytes 1024 | tf_op jit(solution)/shard_map/weight_terms/pallas_call | solution.py:233
  251.0 12.2 %collective-permute-done.15.refs_0_ = bf16[128,4096]{1,0:T(8,128)(2,1)} collective-permute-done((bf16[128,4096]{1,0:T(8,128)(2,1)}, bf16[128,4096]{1,0:T(8,128)(2,1)}, u32[]{:S(2)}, u32[]{:S(2)}) %collective-permute-start.15) | collective-permute-done | bytes 1048608 | tf_op jit(solution)/shard_map/ppermute | solution.py:299
  263.1 3.0 %combine.3 = bf16[128,4096]{1,0:T(8,128)(2,1)} custom-call(f32[1,128]{1,0:T(1,128)} %slice.16.slots_ref, bf16[128,4096]{1,0:T(8,128)(2,1)} %collective-permute-done.15.refs_0_, f32[128,4096]{1,0:T(8,128)} %combine.2.refs_1_), custom_call_target="tpu_custom_call" | custom-call | flops 1024 | bytes 1024 | tf_op jit(solution)/shard_map/combine/pallas_call | solution.py:264
  (94 shorter events, 27.2 us)
Async XLA Ops:
  2.7 8.4 %all-to-all-start = ((f32[8,1,192]{2,1,0:T(1,128)}), f32[8,1,192]{2,1,0:T(1,128)S(1)}, u32[]{:S(2)}, u32[]{:S(2)}) async-start(f32[8,1,192]{2,1,0:T(1,128)} %all_to_all.17), calls=%async_computation | async-start | bytes 16384 | tf_op jit(solution)/shard_map/all_to_all | solution.py:304
  9.6 8.6 %copy-start.2 = (bf16[256,4096]{1,0:T(8,128)(2,1)}, bf16[256,4096]{1,0:T(8,128)(2,1)S(1)}, u32[]{:S(2)}) copy-start(bf16[256,4096]{1,0:T(8,128)(2,1)S(1)} %pad_maximum_fusion.refs_0_) | copy-start | bytes 6291460
  10.7 7.5 %copy-start.9 = (f32[1,4096]{1,0:T(1,128)}, f32[1,4096]{1,0:T(1,128)S(1)}, u32[]{:S(2)}) copy-start(f32[1,4096]{1,0:T(1,128)S(1)} %get-tuple-element.61.refs_4_) | copy-start | bytes 49156
  11.1 7.0 %collective-permute-start = (bf16[256,4096]{1,0:T(8,128)(2,1)S(1)}, bf16[256,4096]{1,0:T(8,128)(2,1)}, u32[]{:S(2)}, u32[]{:S(2)}) collective-permute-start(bf16[256,4096]{1,0:T(8,128)(2,1)S(1)} %pad_maximum_fusion.refs_0_), channel_id=1, source_target_pairs={{0,1},{1,0},{2,3},{3,2},{4,5},{5,4},{6,7},{7,6},{8,9},{9,8},{10,11... | collective-permute-start | bytes 6291464 | tf_op jit(solution)/shard_map/ppermute | solution.py:299
  11.2 48.2 %collective-permute-start.2 = (bf16[256,4096]{1,0:T(8,128)(2,1)S(1)}, bf16[256,4096]{1,0:T(8,128)(2,1)}, u32[]{:S(2)}, u32[]{:S(2)}) collective-permute-start(bf16[256,4096]{1,0:T(8,128)(2,1)S(1)} %pad_maximum_fusion.refs_0_), channel_id=1, source_target_pairs={{0,2},{1,3},{2,0},{3,1},{4,6},{5,7},{6,4},{7,5},{8,10},{9,11},{10,... | collective-permute-start | bytes 6291464 | tf_op jit(solution)/shard_map/ppermute | solution.py:296
  12.5 50.3 %collective-permute-start.6 = (bf16[256,4096]{1,0:T(8,128)(2,1)S(1)}, bf16[256,4096]{1,0:T(8,128)(2,1)}, u32[]{:S(2)}, u32[]{:S(2)}) collective-permute-start(bf16[256,4096]{1,0:T(8,128)(2,1)S(1)} %pad_maximum_fusion.refs_0_), channel_id=1, source_target_pairs={{2,4},{3,5},{4,2},{5,3},{10,12},{11,13},{12,10},{13,11},{18,20},{1... | collective-permute-start | bytes 6291464 | tf_op jit(solution)/shard_map/ppermute | solution.py:296
  35.1 29.5 %copy-start.16 = (bf16[64,4096]{1,0:T(8,128)(2,1)S(1)}, bf16[64,4096]{1,0:T(8,128)(2,1)}, u32[]{:S(2)}) copy-start(bf16[64,4096]{1,0:T(8,128)(2,1)} %get-tuple-element.34) | copy-start | bytes 1572868
  35.1 29.8 %copy-start.12 = (bf16[64,4096]{1,0:T(8,128)(2,1)S(1)}, bf16[64,4096]{1,0:T(8,128)(2,1)}, u32[]{:S(2)}) copy-start(bf16[64,4096]{1,0:T(8,128)(2,1)} %get-tuple-element.33) | copy-start | bytes 1572868
  35.1 53.2 %all-to-all-start.1 = ((bf16[4,528,1024]{2,1,0:T(8,128)(2,1)}), bf16[4,528,1024]{2,1,0:T(8,128)(2,1)}, u32[]{:S(2)}, u32[]{:S(2)}) async-start(bf16[4,528,1024]{2,1,0:T(8,128)(2,1)} %get-tuple-element.45), calls=%async_computation.1 | async-start | bytes 8650752 | tf_op jit(solution)/shard_map/all_to_all | solution.py:336
  59.4 8.0 %collective-permute-start.3 = (bf16[256,4096]{1,0:T(8,128)(2,1)}, bf16[256,4096]{1,0:T(8,128)(2,1)S(1)}, u32[]{:S(2)}, u32[]{:S(2)}) collective-permute-start(bf16[256,4096]{1,0:T(8,128)(2,1)} %collective-permute-done.2.refs_0_), channel_id=1, source_target_pairs={{0,1},{1,0},{2,3},{3,2},{4,5},{5,4},{6,7},{7,6},{8,9},{9,8},{10,11... | collective-permute-start | bytes 6291464 | tf_op jit(solution)/shard_map/ppermute | solution.py:299
  59.4 50.2 %collective-permute-start.5 = (bf16[256,4096]{1,0:T(8,128)(2,1)}, bf16[256,4096]{1,0:T(8,128)(2,1)}, u32[]{:S(2)}, u32[]{:S(2)}) collective-permute-start(bf16[256,4096]{1,0:T(8,128)(2,1)} %collective-permute-done.2.refs_0_), channel_id=1, source_target_pairs={{2,4},{3,5},{4,2},{5,3},{10,12},{11,13},{12,10},{13,11},{18,20},{1... | collective-permute-start | bytes 6291464 | tf_op jit(solution)/shard_map/ppermute | solution.py:296
  62.8 47.5 %collective-permute-start.7 = (bf16[256,4096]{1,0:T(8,128)(2,1)}, bf16[256,4096]{1,0:T(8,128)(2,1)S(1)}, u32[]{:S(2)}, u32[]{:S(2)}) collective-permute-start(bf16[256,4096]{1,0:T(8,128)(2,1)} %collective-permute-done.6), channel_id=1, source_target_pairs={{2,0},{3,1},{4,6},{5,7},{10,8},{11,9},{12,14},{13,15},{18,16},{19,... | collective-permute-start | bytes 6291464 | tf_op jit(solution)/shard_map/ppermute | solution.py:296
  64.6 2.0 collective-permute-start.1
  88.3 53.3 %all-to-all-start.2 = ((bf16[4,528,1024]{2,1,0:T(8,128)(2,1)}), bf16[4,528,1024]{2,1,0:T(8,128)(2,1)}, u32[]{:S(2)}, u32[]{:S(2)}) async-start(bf16[4,528,1024]{2,1,0:T(8,128)(2,1)} %get-tuple-element.46), calls=%async_computation.2 | async-start | bytes 8650752 | tf_op jit(solution)/shard_map/all_to_all | solution.py:336
  94.7 20.4 %copy-start.14 = (bf16[64,4096]{1,0:T(8,128)(2,1)S(1)}, bf16[64,4096]{1,0:T(8,128)(2,1)}, u32[]{:S(2)}) copy-start(bf16[64,4096]{1,0:T(8,128)(2,1)} %get-tuple-element.37) | copy-start | bytes 1572868
  94.7 20.7 %copy-start.10 = (bf16[64,4096]{1,0:T(8,128)(2,1)S(1)}, bf16[64,4096]{1,0:T(8,128)(2,1)}, u32[]{:S(2)}) copy-start(bf16[64,4096]{1,0:T(8,128)(2,1)} %get-tuple-element.36) | copy-start | bytes 1572868
  112.1 5.8 %collective-permute-start.8 = (bf16[256,4096]{1,0:T(8,128)(2,1)S(1)}, bf16[256,4096]{1,0:T(8,128)(2,1)S(1)}, u32[]{:S(2)}, u32[]{:S(2)}) collective-permute-start(bf16[256,4096]{1,0:T(8,128)(2,1)S(1)} %broadcast_select_fusion.1.refs_0_), channel_id=1, source_target_pairs={{0,1},{1,0},{2,3},{3,2},{4,5},{5,4},{6,7},{7,6},{8,9},{9,8},{10,11... | collective-permute-start | bytes 6291464 | tf_op jit(solution)/shard_map/ppermute | solution.py:299
  112.2 48.5 %collective-permute-start.10 = (bf16[256,4096]{1,0:T(8,128)(2,1)}, bf16[256,4096]{1,0:T(8,128)(2,1)S(1)}, u32[]{:S(2)}, u32[]{:S(2)}) collective-permute-start(bf16[256,4096]{1,0:T(8,128)(2,1)} %collective-permute-done.5), channel_id=1, source_target_pairs={{2,0},{3,1},{4,6},{5,7},{10,8},{11,9},{12,14},{13,15},{18,16},{19,... | collective-permute-start | bytes 6291464 | tf_op jit(solution)/shard_map/ppermute | solution.py:296
  115.0 2.1 collective-permute-start.4
  141.6 79.2 %all-to-all-start.3 = ((bf16[4,528,1024]{2,1,0:T(8,128)(2,1)}), bf16[4,528,1024]{2,1,0:T(8,128)(2,1)}, u32[]{:S(2)}, u32[]{:S(2)}) async-start(bf16[4,528,1024]{2,1,0:T(8,128)(2,1)} %get-tuple-element.47), calls=%async_computation.3 | async-start | bytes 8650752 | tf_op jit(solution)/shard_map/all_to_all | solution.py:336
  147.9 14.7 %copy-start.15 = (bf16[64,4096]{1,0:T(8,128)(2,1)S(1)}, bf16[64,4096]{1,0:T(8,128)(2,1)}, u32[]{:S(2)}) copy-start(bf16[64,4096]{1,0:T(8,128)(2,1)} %get-tuple-element.40) | copy-start | bytes 1572868
  147.9 16.0 %copy-start.11 = (bf16[64,4096]{1,0:T(8,128)(2,1)S(1)}, bf16[64,4096]{1,0:T(8,128)(2,1)}, u32[]{:S(2)}) copy-start(bf16[64,4096]{1,0:T(8,128)(2,1)} %get-tuple-element.39) | copy-start | bytes 1572868
  162.6 7.9 %copy-start = (bf16[256,4096]{1,0:T(8,128)(2,1)}, bf16[256,4096]{1,0:T(8,128)(2,1)S(1)}, u32[]{:S(2)}) copy-start(bf16[256,4096]{1,0:T(8,128)(2,1)S(1)} %broadcast_select_fusion.refs_0_) | copy-start | bytes 6291460
  162.6 7.8 %collective-permute-start.11 = (bf16[256,4096]{1,0:T(8,128)(2,1)S(1)}, bf16[256,4096]{1,0:T(8,128)(2,1)S(1)}, u32[]{:S(2)}, u32[]{:S(2)}) collective-permute-start(bf16[256,4096]{1,0:T(8,128)(2,1)S(1)} %broadcast_select_fusion.refs_0_), channel_id=1, source_target_pairs={{0,1},{1,0},{2,3},{3,2},{4,5},{5,4},{6,7},{7,6},{8,9},{9,8},{10,11... | collective-permute-start | bytes 6291464 | tf_op jit(solution)/shard_map/ppermute | solution.py:299
  162.7 4.9 %collective-permute-start.9 = (bf16[64,4096]{1,0:T(8,128)(2,1)S(1)}, bf16[64,4096]{1,0:T(8,128)(2,1)S(1)}, u32[]{:S(2)}, u32[]{:S(2)}) collective-permute-start(bf16[64,4096]{1,0:T(8,128)(2,1)S(1)} %copy-done.15), channel_id=1, source_target_pairs={{0,1},{1,0},{2,3},{3,2},{4,5},{5,4},{6,7},{7,6},{8,9},{9,8},{10,11... | collective-permute-start | bytes 1572872 | tf_op jit(solution)/shard_map/ppermute | solution.py:299
  163.1 42.1 %collective-permute-start.13 = (bf16[128,4096]{1,0:T(8,128)(2,1)}, bf16[128,4096]{1,0:T(8,128)(2,1)}, u32[]{:S(2)}, u32[]{:S(2)}) collective-permute-start(bf16[128,4096]{1,0:T(8,128)(2,1)} %constant_dynamic-update-slice_fusion.2), channel_id=1, source_target_pairs={{0,2},{1,3},{2,0},{3,1},{4,6},{5,7},{6,4},{7,5},{8,10},{9,11},{10,... | collective-permute-start | bytes 3145736 | tf_op jit(solution)/shard_map/ppermute | solution.py:299
  168.4 47.6 %collective-permute-start.14 = (bf16[128,4096]{1,0:T(8,128)(2,1)}, bf16[128,4096]{1,0:T(8,128)(2,1)}, u32[]{:S(2)}, u32[]{:S(2)}) collective-permute-start(bf16[128,4096]{1,0:T(8,128)(2,1)} %constant_dynamic-update-slice_fusion.4), channel_id=1, source_target_pairs={{0,4},{1,5},{2,6},{3,7},{4,0},{5,1},{6,2},{7,3},{8,12},{9,13},{10,... | collective-permute-start | bytes 3145736 | tf_op jit(solution)/shard_map/ppermute | solution.py:299
  189.2 2.2 collective-permute-start.12
  189.3 45.4 %collective-permute-start.16 = (bf16[1,528,1024]{2,1,0:T(8,128)(2,1)}, bf16[1,528,1024]{2,1,0:T(8,128)(2,1)S(1)}, u32[]{:S(2)}, u32[]{:S(2)}) collective-permute-start(bf16[1,528,1024]{2,1,0:T(8,128)(2,1)} %get-tuple-element.51), channel_id=1, source_target_pairs={{0,8},{8,0},{16,24},{24,16},{1,9},{9,1},{17,25},{25,17},{2,10},{10... | collective-permute-start | bytes 3244040 | tf_op jit(solution)/shard_map/ppermute | solution.py:347
  190.0 44.8 %collective-permute-start.17 = (bf16[1,528,1024]{2,1,0:T(8,128)(2,1)}, bf16[1,528,1024]{2,1,0:T(8,128)(2,1)S(1)}, u32[]{:S(2)}, u32[]{:S(2)}) collective-permute-start(bf16[1,528,1024]{2,1,0:T(8,128)(2,1)} %get-tuple-element.52), channel_id=1, source_target_pairs={{0,16},{8,24},{16,0},{24,8},{1,17},{9,25},{17,1},{25,9},{2,18},{10... | collective-permute-start | bytes 3244040 | tf_op jit(solution)/shard_map/ppermute | solution.py:347
  192.2 48.8 %collective-permute-start.18 = (bf16[1,528,1024]{2,1,0:T(8,128)(2,1)}, bf16[1,528,1024]{2,1,0:T(8,128)(2,1)S(1)}, u32[]{:S(2)}, u32[]{:S(2)}) collective-permute-start(bf16[1,528,1024]{2,1,0:T(8,128)(2,1)} %get-tuple-element.53), channel_id=1, source_target_pairs={{0,24},{8,16},{16,8},{24,0},{1,25},{9,17},{17,9},{25,1},{2,26},{10... | collective-permute-start | bytes 3244040 | tf_op jit(solution)/shard_map/ppermute | solution.py:347
  216.0 47.2 %collective-permute-start.15 = (bf16[128,4096]{1,0:T(8,128)(2,1)}, bf16[128,4096]{1,0:T(8,128)(2,1)}, u32[]{:S(2)}, u32[]{:S(2)}) collective-permute-start(bf16[128,4096]{1,0:T(8,128)(2,1)} %pad_maximum_fusion.1), channel_id=1, source_target_pairs={{0,6},{1,7},{2,4},{3,5},{4,2},{5,3},{6,0},{7,1},{8,14},{9,15},{10,... | collective-permute-start | bytes 3145736 | tf_op jit(solution)/shard_map/ppermute | solution.py:299
  (8 other events, 24.1 us)

commit v5 on v4

--- a/solution.py
+++ b/solution.py
@@ -192,9 +192,9 @@
         chunks.append(
             [(left.at[k], right.at[k]) for left, right in zip(lefts, rights) for k in range(left.shape[0])]
         )
-    dp = len(chunks[0])
     start = [refs.pop(0) for _ in range(3)] if has_start else None
     outs = refs
+    pieces = outs[2].shape[0]
     contract = (((0,), (0,)), ((), ()))
     for which in range(2):
         total = start[which][...] if has_start else None
@@ -211,17 +211,17 @@
     for pairs in chunks:
         for _, ref in pairs:
             both = ref[4 * rows :].astype(jnp.float32)
-            column = column + both[:dp] + both[dp : 2 * dp]
+            column = column + both[:pieces] + both[pieces : 2 * pieces]
     outs[2][...] = column
 
 
 def weight_terms(chunks, rows, start, last):
-    dp = sum(block.shape[0] for block in chunks[0])
     piece = chunks[0][0].shape[2]
     tile = min(piece, 512)
     kind = jnp.bfloat16 if last else jnp.float32
     strip = pl.BlockSpec((tile, piece), lambda i: (i, 0))
-    column = pl.BlockSpec((dp, piece), lambda i: (0, 0))
+    pieces = sum(block.shape[0] for block in chunks[0]) if start is None else start[2].shape[0]
+    column = pl.BlockSpec((pieces, piece), lambda i: (0, 0))
     specs, arrays = [], []
     for blocks in chunks:
         specs += [pl.BlockSpec((block.shape[0], 2 * rows, tile), lambda i: (0, 0, i)) for block in blocks]
@@ -236,7 +236,7 @@
         in_specs=specs,
         out_specs=[strip, strip, column],
         out_shape=[jax.ShapeDtypeStruct((piece, piece), kind)] * 2
-        + [jax.ShapeDtypeStruct((dp, piece), jnp.float32)],
+        + [jax.ShapeDtypeStruct((pieces, piece), jnp.float32)],
         compiler_params=pltpu.CompilerParams(vmem_limit_bytes=VMEM_LIMIT),
         cost_estimate=SMALL if last else LARGE,
         name="weight_terms",
@@ -356,12 +356,12 @@
     back1, back2 = across(back1, 2), across(back2, 4)
     back3 = across(after(back3, back1, back2), 6)
     rows = 2 * per_slot
-    early = weight_terms([got0, got1, got2], rows, None, False)
+    early = weight_terms([got0, got1, got2, got3[:1]], rows, None, False)
     lists = mine.reshape(1, -1)
     most = 3 * rows
     partial = combine(lists[:, :most], [back0, back1, back2], tok_rows, None, jnp.float32)
     partial, first = lax.optimization_barrier((partial, early[0]))
-    up_sum, down_sum, column = weight_terms([got3], rows, (first, early[1], early[2]), True)
+    up_sum, down_sum, column = weight_terms([got3[1:]], rows, (first, early[1], early[2]), True)
     tokens_grad = combine(lists[:, most:], [back3], tok_rows, partial, jnp.bfloat16)
     return (tokens_grad, up_sum[None], down_sum[None], column.reshape(-1, 1))
 

time: 267 us -> 267 us (level)
  transfers between devices with their start and end apart: 23 -> 23, of which waited for: 15 -> 15; matrix products, arithmetic and copies ran while one was open for 7% -> 7% of each run, Pallas kernels for 35% -> 36%
where the time goes in v5:
time: 267 us; the launch traced here: 266 us
  waiting for transfers between devices  98.2 us (37%)
  Pallas kernels  97.6 us (37%)
  starting transfers between devices  43.1 us (16%)
  local copies, waits for them, and re-layouts  15.1 us (6%)
  other arithmetic  11.1 us (4%)
    pallas_call x4, Pallas kernels, expert_rows(): pl.pallas_call(functools.partial(expert_kernel, apart, steps), grid_spec=...  68.2 us
    ppermute x5, waiting for transfers between devices, between(): return lax.ppermute(block, 'expert', pairs)  47.3 us
    ppermute x11, waiting for transfers between devices, across(): lax.ppermute(block, 'expert', [(e, e ^ mask) for e in range(experts)])  37.7 us
    pallas_call x2, Pallas kernels, weight_terms(): pl.pallas_call(functools.partial(weights_kernel, [len(blocks) for blocks...  23.1 us
    all_to_all x3, starting transfers between devices, exchange(): return lax.all_to_all(block, 'dp', 0, 0, tiled=True)  18.2 us
    ppermute x5, starting transfers between devices, between(): return lax.ppermute(block, 'expert', pairs)  12.8 us
    unnamed x39, local copies, waits for them, and re-layouts  9.66 us
    all_to_all x3, waiting for transfers between devices, exchange(): return lax.all_to_all(block, 'dp', 0, 0, tiled=True)  7.99 us
  transfers between devices with their start and end apart: 23, of which 15 were waited for; matrix products, arithmetic and copies ran while one was open for 7% of the time, Pallas kernels for 36%

profile of v5, /device:TPU:22, one launch (start us, length us, event | category | flops | bytes accessed | tf_op | source)
XLA Modules:
  0.0 266.1 jit_solution(17732590736682226663)
XLA Ops:
  2.7 5.2 %all-to-all-start = ((f32[8,1,192]{2,1,0:T(1,128)}), f32[8,1,192]{2,1,0:T(1,128)S(1)}, u32[]{:S(2)}, u32[]{:S(2)}) async-start(f32[8,1,192]{2,1,0:T(1,128)} %all_to_all.17), calls=%async_computation | async-start | bytes 16384 | tf_op jit(solution)/shard_map/all_to_all | solution.py:304
  7.9 1.7 pad_maximum_fusion.refs_0_
  12.5 3.6 %collective-permute-start.6 = (bf16[256,4096]{1,0:T(8,128)(2,1)S(1)}, bf16[256,4096]{1,0:T(8,128)(2,1)}, u32[]{:S(2)}, u32[]{:S(2)}) collective-permute-start(bf16[256,4096]{1,0:T(8,128)(2,1)S(1)} %pad_maximum_fusion.refs_0_), channel_id=1, source_target_pairs={{2,4},{3,5},{4,2},{5,3},{10,12},{11,13},{12,10},{13,11},{18,20},{1... | collective-permute-start | bytes 6291464 | tf_op jit(solution)/shard_map/ppermute | solution.py:296
  18.2 16.9 %expert_rows.4 = (bf16[4,528,1024]{2,1,0:T(8,128)(2,1)}, bf16[64,4096]{1,0:T(8,128)(2,1)}, bf16[64,4096]{1,0:T(8,128)(2,1)}) custom-call(s32[1]{0:T(128)} %bitcast.5.place_ref, f32[128,2]{1,0:T(8,128)} %get-tuple-element.62.meta_ref, bf16[16,4096]{1,0:T(8,128)(2,1)} %maximum_maximum_fusion.router_ref, bf16[256,4096]{1,0:T(8,128)(2,1)} %copy-done.2, ...), custom_call_target="tpu_custom_call" | custom-call | flops 1024 | bytes 1024 | tf_op jit(solution)/shard_map/expert_rows/pallas_call | solution.py:157
  35.1 5.5 %all-to-all-start.1 = ((bf16[4,528,1024]{2,1,0:T(8,128)(2,1)}), bf16[4,528,1024]{2,1,0:T(8,128)(2,1)}, u32[]{:S(2)}, u32[]{:S(2)}) async-start(bf16[4,528,1024]{2,1,0:T(8,128)(2,1)} %get-tuple-element.45), calls=%async_computation.1 | async-start | bytes 8650752 | tf_op jit(solution)/shard_map/all_to_all | solution.py:336
  40.6 18.8 %collective-permute-done.2.refs_0_ = bf16[256,4096]{1,0:T(8,128)(2,1)} collective-permute-done((bf16[256,4096]{1,0:T(8,128)(2,1)S(1)}, bf16[256,4096]{1,0:T(8,128)(2,1)}, u32[]{:S(2)}, u32[]{:S(2)}) %collective-permute-start.2) | collective-permute-done | bytes 2097184 | tf_op jit(solution)/shard_map/ppermute | solution.py:296
  59.4 3.4 %collective-permute-start.5 = (bf16[256,4096]{1,0:T(8,128)(2,1)}, bf16[256,4096]{1,0:T(8,128)(2,1)}, u32[]{:S(2)}, u32[]{:S(2)}) collective-permute-start(bf16[256,4096]{1,0:T(8,128)(2,1)} %collective-permute-done.2.refs_0_), channel_id=1, source_target_pairs={{2,4},{3,5},{4,2},{5,3},{10,12},{11,13},{12,10},{13,11},{18,20},{1... | collective-permute-start | bytes 6291464 | tf_op jit(solution)/shard_map/ppermute | solution.py:296
  62.8 1.8 collective-permute-start.7
  68.7 17.0 %expert_rows.5 = (bf16[4,528,1024]{2,1,0:T(8,128)(2,1)}, bf16[64,4096]{1,0:T(8,128)(2,1)}, bf16[64,4096]{1,0:T(8,128)(2,1)}) custom-call(s32[1]{0:T(128)} %bitcast.5.place_ref, f32[128,2]{1,0:T(8,128)} %get-tuple-element.35.meta_ref, bf16[16,4096]{1,0:T(8,128)(2,1)} %maximum_maximum_fusion.router_ref, bf16[256,4096]{1,0:T(8,128)(2,1)} %collective-permute-done.2.refs_0_, ...), custom_call_target="tpu_custom_call" | custom-call | flops 1024 | bytes 1024 | tf_op jit(solution)/shard_map/expert_rows/pallas_call | solution.py:157
  85.7 2.6 all-to-all-done.1.refs_0_.refs_1_
  88.3 6.4 %all-to-all-start.2 = ((bf16[4,528,1024]{2,1,0:T(8,128)(2,1)}), bf16[4,528,1024]{2,1,0:T(8,128)(2,1)}, u32[]{:S(2)}, u32[]{:S(2)}) async-start(bf16[4,528,1024]{2,1,0:T(8,128)(2,1)} %get-tuple-element.46), calls=%async_computation.2 | async-start | bytes 8650752 | tf_op jit(solution)/shard_map/all_to_all | solution.py:336
  94.7 15.0 %collective-permute-done.5 = bf16[256,4096]{1,0:T(8,128)(2,1)} collective-permute-done((bf16[256,4096]{1,0:T(8,128)(2,1)}, bf16[256,4096]{1,0:T(8,128)(2,1)}, u32[]{:S(2)}, u32[]{:S(2)}) %collective-permute-start.5) | collective-permute-done | bytes 2097184 | tf_op jit(solution)/shard_map/ppermute | solution.py:296
  110.3 1.8 broadcast_select_fusion.1.refs_0_
  112.2 2.8 %collective-permute-start.10 = (bf16[256,4096]{1,0:T(8,128)(2,1)}, bf16[256,4096]{1,0:T(8,128)(2,1)S(1)}, u32[]{:S(2)}, u32[]{:S(2)}) collective-permute-start(bf16[256,4096]{1,0:T(8,128)(2,1)} %collective-permute-done.5), channel_id=1, source_target_pairs={{2,0},{3,1},{4,6},{5,7},{10,8},{11,9},{12,14},{13,15},{18,16},{19,... | collective-permute-start | bytes 6291464 | tf_op jit(solution)/shard_map/ppermute | solution.py:296
  119.3 16.9 %expert_rows.6 = (bf16[4,528,1024]{2,1,0:T(8,128)(2,1)}, bf16[64,4096]{1,0:T(8,128)(2,1)}, bf16[64,4096]{1,0:T(8,128)(2,1)}) custom-call(s32[1]{0:T(128)} %bitcast.5.place_ref, f32[128,2]{1,0:T(8,128)} %get-tuple-element.38.meta_ref, bf16[16,4096]{1,0:T(8,128)(2,1)} %maximum_maximum_fusion.router_ref, bf16[256,4096]{1,0:T(8,128)(2,1)} %copy-done.1, ...), custom_call_target="tpu_custom_call" | custom-call | flops 1024 | bytes 1024 | tf_op jit(solution)/shard_map/expert_rows/pallas_call | solution.py:157
  136.2 5.4 %all-to-all-done.2.refs_2_.refs_3_ = bf16[4,528,1024]{2,1,0:T(8,128)(2,1)} async-done(((bf16[4,528,1024]{2,1,0:T(8,128)(2,1)}), bf16[4,528,1024]{2,1,0:T(8,128)(2,1)}, u32[]{:S(2)}, u32[]{:S(2)}) %all-to-all-start.2) | async-done | bytes 4325408 | tf_op jit(solution)/shard_map/all_to_all | solution.py:336
  141.6 6.3 %all-to-all-start.3 = ((bf16[4,528,1024]{2,1,0:T(8,128)(2,1)}), bf16[4,528,1024]{2,1,0:T(8,128)(2,1)}, u32[]{:S(2)}, u32[]{:S(2)}) async-start(bf16[4,528,1024]{2,1,0:T(8,128)(2,1)} %get-tuple-element.47), calls=%async_computation.3 | async-start | bytes 8650752 | tf_op jit(solution)/shard_map/all_to_all | solution.py:336
  147.9 12.8 %collective-permute-done.10 = bf16[256,4096]{1,0:T(8,128)(2,1)S(1)} collective-permute-done((bf16[256,4096]{1,0:T(8,128)(2,1)}, bf16[256,4096]{1,0:T(8,128)(2,1)S(1)}, u32[]{:S(2)}, u32[]{:S(2)}) %collective-permute-start.10) | collective-permute-done | bytes 2097184 | tf_op jit(solution)/shard_map/ppermute | solution.py:296
  160.7 1.8 broadcast_select_fusion.refs_0_
  164.8 2.8 %collective-permute-done.9 = bf16[64,4096]{1,0:T(8,128)(2,1)S(1)} collective-permute-done((bf16[64,4096]{1,0:T(8,128)(2,1)S(1)}, bf16[64,4096]{1,0:T(8,128)(2,1)S(1)}, u32[]{:S(2)}, u32[]{:S(2)}) %collective-permute-start.9) | collective-permute-done | bytes 524320 | tf_op jit(solution)/shard_map/ppermute | solution.py:299
  168.4 2.0 collective-permute-start.14
  171.7 17.4 %expert_rows.7 = (bf16[1,528,1024]{2,1,0:T(8,128)(2,1)}, bf16[1,528,1024]{2,1,0:T(8,128)(2,1)}, bf16[1,528,1024]{2,1,0:T(8,128)(2,1)}, bf16[1,528,1024]{2,1,0:T(...) custom-call(s32[1]{0:T(128)} %bitcast.5.place_ref, f32[128,2]{1,0:T(8,128)} %get-tuple-element.41.meta_ref, ...), custom_call_target="tpu_custom_call" | custom-call | flops 1024 | bytes 1024 | tf_op jit(solution)/shard_map/expert_rows/pallas_call | solution.py:157
  192.2 1.5 collective-permute-start.18
  193.7 2.3 pad_maximum_fusion.1
  195.9 9.3 %collective-permute-done.13.refs_1_ = bf16[128,4096]{1,0:T(8,128)(2,1)} collective-permute-done((bf16[128,4096]{1,0:T(8,128)(2,1)}, bf16[128,4096]{1,0:T(8,128)(2,1)}, u32[]{:S(2)}, u32[]{:S(2)}) %collective-permute-start.13) | collective-permute-done | bytes 1048608 | tf_op jit(solution)/shard_map/ppermute | solution.py:299
  205.2 10.8 %collective-permute-done.14.refs_2_ = bf16[128,4096]{1,0:T(8,128)(2,1)} collective-permute-done((bf16[128,4096]{1,0:T(8,128)(2,1)}, bf16[128,4096]{1,0:T(8,128)(2,1)}, u32[]{:S(2)}, u32[]{:S(2)}) %collective-permute-start.14) | collective-permute-done | bytes 1048608 | tf_op jit(solution)/shard_map/ppermute | solution.py:299
  217.4 3.4 %combine.2.refs_1_ = f32[128,4096]{1,0:T(8,128)} custom-call(f32[1,384]{1,0:T(1,128)} %slice.19.slots_ref, bf16[128,4096]{1,0:T(8,128)(2,1)} %constant_dynamic-update-slice_fusion.refs_0_, bf16[128,4096]{1,0:T(8,128)(2,1)} %collective-permute-done.13.refs_1_, bf16[128,4096]{1,0:T(8,128)(2,1)} %collective-permute-done.14.refs_2_), custom_call_target="tpu_custom_call" | custom-call | flops 1024 | bytes 1024 | tf_op jit(solution)/shard_map/combine/pallas_call | solution.py:264
  220.7 15.4 %weight_terms.2 = (f32[1024,1024]{1,0:T(8,128)}, f32[1024,1024]{1,0:T(8,128)}, f32[4,1024]{1,0:T(4,128)}) custom-call(bf16[4,528,1024]{2,1,0:T(8,128)(2,1)} %all-to-all-done.1.refs_0_.refs_1_, bf16[4,528,1024]{2,1,0:T(8,128)(2,1)} %all-to-all-done.1.refs_0_.refs_1_, bf16[4,528,1024]{2,1,0:T(8,128)(2,1)} %all-to-all-done.2.refs_2_.refs_3_, ...), custom_call_target="tpu_custom_call" | custom-call | flops 10000000000 | bytes 1024 | tf_op jit(solution)/shard_map/weight_terms/pallas_call | solution.py:233
  236.2 4.8 %collective-permute-done.18.refs_2_.refs_5_ = bf16[1,528,1024]{2,1,0:T(8,128)(2,1)S(1)} collective-permute-done((bf16[1,528,1024]{2,1,0:T(8,128)(2,1)}, bf16[1,528,1024]{2,1,0:T(8,128)(2,1)S(1)}, u32[]{:S(2)}, u32[]{:S(2)}) %collective-permute-start.18) | collective-permute-done | bytes 1081376 | tf_op jit(solution)/shard_map/ppermute | solution.py:347
  242.0 7.6 %weight_terms.3 = (bf16[1024,1024]{1,0:T(8,128)(2,1)}, bf16[1024,1024]{1,0:T(8,128)(2,1)}, f32[4,1024]{1,0:T(4,128)}) custom-call(bf16[1,528,1024]{2,1,0:T(8,128)(2,1)} %copy-done.3, bf16[1,528,1024]{2,1,0:T(8,128)(2,1)} %copy-done.4, bf16[1,528,1024]{2,1,0:T(8,128)(2,1)} %copy-done.5, bf16[1,528,1024]{2,1,0:T(8,128)(2,1)} %copy-done.3, ...), custom_call_target="tpu_custom_call" | custom-call | flops 1024 | bytes 1024 | tf_op jit(solution)/shard_map/weight_terms/pallas_call | solution.py:233
  250.9 12.2 %collective-permute-done.15.refs_0_ = bf16[128,4096]{1,0:T(8,128)(2,1)} collective-permute-done((bf16[128,4096]{1,0:T(8,128)(2,1)}, bf16[128,4096]{1,0:T(8,128)(2,1)}, u32[]{:S(2)}, u32[]{:S(2)}) %collective-permute-start.15) | collective-permute-done | bytes 1048608 | tf_op jit(solution)/shard_map/ppermute | solution.py:299
  263.1 3.0 %combine.3 = bf16[128,4096]{1,0:T(8,128)(2,1)} custom-call(f32[1,128]{1,0:T(1,128)} %slice.16.slots_ref, bf16[128,4096]{1,0:T(8,128)(2,1)} %collective-permute-done.15.refs_0_, f32[128,4096]{1,0:T(8,128)} %combine.2.refs_1_), custom_call_target="tpu_custom_call" | custom-call | flops 1024 | bytes 1024 | tf_op jit(solution)/shard_map/combine/pallas_call | solution.py:264
  (94 shorter events, 27.2 us)
Async XLA Ops:
  2.7 8.4 %all-to-all-start = ((f32[8,1,192]{2,1,0:T(1,128)}), f32[8,1,192]{2,1,0:T(1,128)S(1)}, u32[]{:S(2)}, u32[]{:S(2)}) async-start(f32[8,1,192]{2,1,0:T(1,128)} %all_to_all.17), calls=%async_computation | async-start | bytes 16384 | tf_op jit(solution)/shard_map/all_to_all | solution.py:304
  9.6 8.6 %copy-start.2 = (bf16[256,4096]{1,0:T(8,128)(2,1)}, bf16[256,4096]{1,0:T(8,128)(2,1)S(1)}, u32[]{:S(2)}) copy-start(bf16[256,4096]{1,0:T(8,128)(2,1)S(1)} %pad_maximum_fusion.refs_0_) | copy-start | bytes 6291460
  10.7 7.5 %copy-start.9 = (f32[1,4096]{1,0:T(1,128)}, f32[1,4096]{1,0:T(1,128)S(1)}, u32[]{:S(2)}) copy-start(f32[1,4096]{1,0:T(1,128)S(1)} %get-tuple-element.61.refs_4_) | copy-start | bytes 49156
  11.1 7.0 %collective-permute-start = (bf16[256,4096]{1,0:T(8,128)(2,1)S(1)}, bf16[256,4096]{1,0:T(8,128)(2,1)}, u32[]{:S(2)}, u32[]{:S(2)}) collective-permute-start(bf16[256,4096]{1,0:T(8,128)(2,1)S(1)} %pad_maximum_fusion.refs_0_), channel_id=1, source_target_pairs={{0,1},{1,0},{2,3},{3,2},{4,5},{5,4},{6,7},{7,6},{8,9},{9,8},{10,11... | collective-permute-start | bytes 6291464 | tf_op jit(solution)/shard_map/ppermute | solution.py:299
  11.2 48.2 %collective-permute-start.2 = (bf16[256,4096]{1,0:T(8,128)(2,1)S(1)}, bf16[256,4096]{1,0:T(8,128)(2,1)}, u32[]{:S(2)}, u32[]{:S(2)}) collective-permute-start(bf16[256,4096]{1,0:T(8,128)(2,1)S(1)} %pad_maximum_fusion.refs_0_), channel_id=1, source_target_pairs={{0,2},{1,3},{2,0},{3,1},{4,6},{5,7},{6,4},{7,5},{8,10},{9,11},{10,... | collective-permute-start | bytes 6291464 | tf_op jit(solution)/shard_map/ppermute | solution.py:296
  12.5 50.3 %collective-permute-start.6 = (bf16[256,4096]{1,0:T(8,128)(2,1)S(1)}, bf16[256,4096]{1,0:T(8,128)(2,1)}, u32[]{:S(2)}, u32[]{:S(2)}) collective-permute-start(bf16[256,4096]{1,0:T(8,128)(2,1)S(1)} %pad_maximum_fusion.refs_0_), channel_id=1, source_target_pairs={{2,4},{3,5},{4,2},{5,3},{10,12},{11,13},{12,10},{13,11},{18,20},{1... | collective-permute-start | bytes 6291464 | tf_op jit(solution)/shard_map/ppermute | solution.py:296
  35.1 29.5 %copy-start.16 = (bf16[64,4096]{1,0:T(8,128)(2,1)S(1)}, bf16[64,4096]{1,0:T(8,128)(2,1)}, u32[]{:S(2)}) copy-start(bf16[64,4096]{1,0:T(8,128)(2,1)} %get-tuple-element.34) | copy-start | bytes 1572868
  35.1 29.8 %copy-start.12 = (bf16[64,4096]{1,0:T(8,128)(2,1)S(1)}, bf16[64,4096]{1,0:T(8,128)(2,1)}, u32[]{:S(2)}) copy-start(bf16[64,4096]{1,0:T(8,128)(2,1)} %get-tuple-element.33) | copy-start | bytes 1572868
  35.1 53.2 %all-to-all-start.1 = ((bf16[4,528,1024]{2,1,0:T(8,128)(2,1)}), bf16[4,528,1024]{2,1,0:T(8,128)(2,1)}, u32[]{:S(2)}, u32[]{:S(2)}) async-start(bf16[4,528,1024]{2,1,0:T(8,128)(2,1)} %get-tuple-element.45), calls=%async_computation.1 | async-start | bytes 8650752 | tf_op jit(solution)/shard_map/all_to_all | solution.py:336
  59.4 8.0 %collective-permute-start.3 = (bf16[256,4096]{1,0:T(8,128)(2,1)}, bf16[256,4096]{1,0:T(8,128)(2,1)S(1)}, u32[]{:S(2)}, u32[]{:S(2)}) collective-permute-start(bf16[256,4096]{1,0:T(8,128)(2,1)} %collective-permute-done.2.refs_0_), channel_id=1, source_target_pairs={{0,1},{1,0},{2,3},{3,2},{4,5},{5,4},{6,7},{7,6},{8,9},{9,8},{10,11... | collective-permute-start | bytes 6291464 | tf_op jit(solution)/shard_map/ppermute | solution.py:299
  59.4 50.2 %collective-permute-start.5 = (bf16[256,4096]{1,0:T(8,128)(2,1)}, bf16[256,4096]{1,0:T(8,128)(2,1)}, u32[]{:S(2)}, u32[]{:S(2)}) collective-permute-start(bf16[256,4096]{1,0:T(8,128)(2,1)} %collective-permute-done.2.refs_0_), channel_id=1, source_target_pairs={{2,4},{3,5},{4,2},{5,3},{10,12},{11,13},{12,10},{13,11},{18,20},{1... | collective-permute-start | bytes 6291464 | tf_op jit(solution)/shard_map/ppermute | solution.py:296
  62.8 47.5 %collective-permute-start.7 = (bf16[256,4096]{1,0:T(8,128)(2,1)}, bf16[256,4096]{1,0:T(8,128)(2,1)S(1)}, u32[]{:S(2)}, u32[]{:S(2)}) collective-permute-start(bf16[256,4096]{1,0:T(8,128)(2,1)} %collective-permute-done.6), channel_id=1, source_target_pairs={{2,0},{3,1},{4,6},{5,7},{10,8},{11,9},{12,14},{13,15},{18,16},{19,... | collective-permute-start | bytes 6291464 | tf_op jit(solution)/shard_map/ppermute | solution.py:296
  64.6 2.0 collective-permute-start.1
  88.3 53.3 %all-to-all-start.2 = ((bf16[4,528,1024]{2,1,0:T(8,128)(2,1)}), bf16[4,528,1024]{2,1,0:T(8,128)(2,1)}, u32[]{:S(2)}, u32[]{:S(2)}) async-start(bf16[4,528,1024]{2,1,0:T(8,128)(2,1)} %get-tuple-element.46), calls=%async_computation.2 | async-start | bytes 8650752 | tf_op jit(solution)/shard_map/all_to_all | solution.py:336
  94.7 20.4 %copy-start.14 = (bf16[64,4096]{1,0:T(8,128)(2,1)S(1)}, bf16[64,4096]{1,0:T(8,128)(2,1)}, u32[]{:S(2)}) copy-start(bf16[64,4096]{1,0:T(8,128)(2,1)} %get-tuple-element.37) | copy-start | bytes 1572868
  94.7 20.7 %copy-start.10 = (bf16[64,4096]{1,0:T(8,128)(2,1)S(1)}, bf16[64,4096]{1,0:T(8,128)(2,1)}, u32[]{:S(2)}) copy-start(bf16[64,4096]{1,0:T(8,128)(2,1)} %get-tuple-element.36) | copy-start | bytes 1572868
  112.1 5.8 %collective-permute-start.8 = (bf16[256,4096]{1,0:T(8,128)(2,1)S(1)}, bf16[256,4096]{1,0:T(8,128)(2,1)S(1)}, u32[]{:S(2)}, u32[]{:S(2)}) collective-permute-start(bf16[256,4096]{1,0:T(8,128)(2,1)S(1)} %broadcast_select_fusion.1.refs_0_), channel_id=1, source_target_pairs={{0,1},{1,0},{2,3},{3,2},{4,5},{5,4},{6,7},{7,6},{8,9},{9,8},{10,11... | collective-permute-start | bytes 6291464 | tf_op jit(solution)/shard_map/ppermute | solution.py:299
  112.2 48.5 %collective-permute-start.10 = (bf16[256,4096]{1,0:T(8,128)(2,1)}, bf16[256,4096]{1,0:T(8,128)(2,1)S(1)}, u32[]{:S(2)}, u32[]{:S(2)}) collective-permute-start(bf16[256,4096]{1,0:T(8,128)(2,1)} %collective-permute-done.5), channel_id=1, source_target_pairs={{2,0},{3,1},{4,6},{5,7},{10,8},{11,9},{12,14},{13,15},{18,16},{19,... | collective-permute-start | bytes 6291464 | tf_op jit(solution)/shard_map/ppermute | solution.py:296
  115.0 2.1 collective-permute-start.4
  141.6 79.2 %all-to-all-start.3 = ((bf16[4,528,1024]{2,1,0:T(8,128)(2,1)}), bf16[4,528,1024]{2,1,0:T(8,128)(2,1)}, u32[]{:S(2)}, u32[]{:S(2)}) async-start(bf16[4,528,1024]{2,1,0:T(8,128)(2,1)} %get-tuple-element.47), calls=%async_computation.3 | async-start | bytes 8650752 | tf_op jit(solution)/shard_map/all_to_all | solution.py:336
  147.9 14.7 %copy-start.15 = (bf16[64,4096]{1,0:T(8,128)(2,1)S(1)}, bf16[64,4096]{1,0:T(8,128)(2,1)}, u32[]{:S(2)}) copy-start(bf16[64,4096]{1,0:T(8,128)(2,1)} %get-tuple-element.40) | copy-start | bytes 1572868
  147.9 16.0 %copy-start.11 = (bf16[64,4096]{1,0:T(8,128)(2,1)S(1)}, bf16[64,4096]{1,0:T(8,128)(2,1)}, u32[]{:S(2)}) copy-start(bf16[64,4096]{1,0:T(8,128)(2,1)} %get-tuple-element.39) | copy-start | bytes 1572868
  162.6 7.9 %copy-start = (bf16[256,4096]{1,0:T(8,128)(2,1)}, bf16[256,4096]{1,0:T(8,128)(2,1)S(1)}, u32[]{:S(2)}) copy-start(bf16[256,4096]{1,0:T(8,128)(2,1)S(1)} %broadcast_select_fusion.refs_0_) | copy-start | bytes 6291460
  162.6 7.8 %collective-permute-start.11 = (bf16[256,4096]{1,0:T(8,128)(2,1)S(1)}, bf16[256,4096]{1,0:T(8,128)(2,1)S(1)}, u32[]{:S(2)}, u32[]{:S(2)}) collective-permute-start(bf16[256,4096]{1,0:T(8,128)(2,1)S(1)} %broadcast_select_fusion.refs_0_), channel_id=1, source_target_pairs={{0,1},{1,0},{2,3},{3,2},{4,5},{5,4},{6,7},{7,6},{8,9},{9,8},{10,11... | collective-permute-start | bytes 6291464 | tf_op jit(solution)/shard_map/ppermute | solution.py:299
  162.7 4.9 %collective-permute-start.9 = (bf16[64,4096]{1,0:T(8,128)(2,1)S(1)}, bf16[64,4096]{1,0:T(8,128)(2,1)S(1)}, u32[]{:S(2)}, u32[]{:S(2)}) collective-permute-start(bf16[64,4096]{1,0:T(8,128)(2,1)S(1)} %copy-done.15), channel_id=1, source_target_pairs={{0,1},{1,0},{2,3},{3,2},{4,5},{5,4},{6,7},{7,6},{8,9},{9,8},{10,11... | collective-permute-start | bytes 1572872 | tf_op jit(solution)/shard_map/ppermute | solution.py:299
  163.1 42.1 %collective-permute-start.13 = (bf16[128,4096]{1,0:T(8,128)(2,1)}, bf16[128,4096]{1,0:T(8,128)(2,1)}, u32[]{:S(2)}, u32[]{:S(2)}) collective-permute-start(bf16[128,4096]{1,0:T(8,128)(2,1)} %constant_dynamic-update-slice_fusion.2), channel_id=1, source_target_pairs={{0,2},{1,3},{2,0},{3,1},{4,6},{5,7},{6,4},{7,5},{8,10},{9,11},{10,... | collective-permute-start | bytes 3145736 | tf_op jit(solution)/shard_map/ppermute | solution.py:299
  168.4 47.6 %collective-permute-start.14 = (bf16[128,4096]{1,0:T(8,128)(2,1)}, bf16[128,4096]{1,0:T(8,128)(2,1)}, u32[]{:S(2)}, u32[]{:S(2)}) collective-permute-start(bf16[128,4096]{1,0:T(8,128)(2,1)} %constant_dynamic-update-slice_fusion.4), channel_id=1, source_target_pairs={{0,4},{1,5},{2,6},{3,7},{4,0},{5,1},{6,2},{7,3},{8,12},{9,13},{10,... | collective-permute-start | bytes 3145736 | tf_op jit(solution)/shard_map/ppermute | solution.py:299
  189.2 2.2 collective-permute-start.12
  189.3 46.8 %collective-permute-start.16 = (bf16[1,528,1024]{2,1,0:T(8,128)(2,1)}, bf16[1,528,1024]{2,1,0:T(8,128)(2,1)S(1)}, u32[]{:S(2)}, u32[]{:S(2)}) collective-permute-start(bf16[1,528,1024]{2,1,0:T(8,128)(2,1)} %get-tuple-element.51), channel_id=1, source_target_pairs={{0,8},{8,0},{16,24},{24,16},{1,9},{9,1},{17,25},{25,17},{2,10},{10... | collective-permute-start | bytes 3244040 | tf_op jit(solution)/shard_map/ppermute | solution.py:347
  189.9 46.2 %collective-permute-start.17 = (bf16[1,528,1024]{2,1,0:T(8,128)(2,1)}, bf16[1,528,1024]{2,1,0:T(8,128)(2,1)S(1)}, u32[]{:S(2)}, u32[]{:S(2)}) collective-permute-start(bf16[1,528,1024]{2,1,0:T(8,128)(2,1)} %get-tuple-element.52), channel_id=1, source_target_pairs={{0,16},{8,24},{16,0},{24,8},{1,17},{9,25},{17,1},{25,9},{2,18},{10... | collective-permute-start | bytes 3244040 | tf_op jit(solution)/shard_map/ppermute | solution.py:347
  192.2 48.8 %collective-permute-start.18 = (bf16[1,528,1024]{2,1,0:T(8,128)(2,1)}, bf16[1,528,1024]{2,1,0:T(8,128)(2,1)S(1)}, u32[]{:S(2)}, u32[]{:S(2)}) collective-permute-start(bf16[1,528,1024]{2,1,0:T(8,128)(2,1)} %get-tuple-element.53), channel_id=1, source_target_pairs={{0,24},{8,16},{16,8},{24,0},{1,25},{9,17},{17,9},{25,1},{2,26},{10... | collective-permute-start | bytes 3244040 | tf_op jit(solution)/shard_map/ppermute | solution.py:347
  216.0 47.2 %collective-permute-start.15 = (bf16[128,4096]{1,0:T(8,128)(2,1)}, bf16[128,4096]{1,0:T(8,128)(2,1)}, u32[]{:S(2)}, u32[]{:S(2)}) collective-permute-start(bf16[128,4096]{1,0:T(8,128)(2,1)} %pad_maximum_fusion.1), channel_id=1, source_target_pairs={{0,6},{1,7},{2,4},{3,5},{4,2},{5,3},{6,0},{7,1},{8,14},{9,15},{10,... | collective-permute-start | bytes 3145736 | tf_op jit(solution)/shard_map/ppermute | solution.py:299
  (8 other events, 21.2 us)
